TPU v7x, 32 devices: a whole 2x2x4 slice. The times are simulated.
32 devices in a mesh: gx: 8 (over z, x), gy: 4 (over y, core).
Axes of the slice: x: 2, y: 2, z: 4, core: 2. Of those that a mesh axis runs over, the one named last changes fastest.
Arguments:
- field: bfloat16 [20, 64, 64, 256], P(None, 'gx', 'gy'), may hold values from -6 to 6
- cotangent: bfloat16 [20, 64, 64, 256], P(None, 'gx', 'gy'), may hold values from -6 to 6
- spectral_weight: bfloat16 [2, 20, 20, 24, 2304], P(None, None, None, 'gy', 'gx'), may hold values from -6 to 6
- pointwise_weight: bfloat16 [20, 20], replicated, may hold values from -1.25 to 1.25
- bias: float32 [20], replicated, may hold values from -1 to 1
Outputs:
- output: bfloat16 [20, 64, 64, 256], P(None, 'gx', 'gy')
- grad_field: bfloat16 [20, 64, 64, 256], P(None, 'gx', 'gy')
- grad_spectral: float32 [2, 20, 20, 24, 2304], P(None, None, None, 'gy', 'gx')
- grad_pointwise: float32 [20, 20], replicated
- grad_bias: float32 [20], replicated
All inputs are finite; a program needn't handle non-finite values.
Results may differ from a plain program's by a relative error of at most 0.0013.
Values sent between devices are 32-bit elements; how exact they have to be, the bound alone decides.
No kernel may reach another device: no remote copies, remote signals or barrier semaphores. Data moves between devices by JAX's collectives and lax.ppermute only.
A program may use at most 128 MiB of HBM per device.

v0:
```python
import math

import jax
import jax.numpy as jnp
from jax import lax
from jax.sharding import PartitionSpec as P

MX = 24
MY = 24
MZ = 24


PRECISE = lax.Precision.HIGHEST
TWO_PI = 2.0 * math.pi


def angles(frequencies, places, length):
    product = places[:, None] * frequencies[None, :] % length
    return product.astype(jnp.float32) * (TWO_PI / length)


def frequency(position, kept_modes, length):
    return jnp.where(position < kept_modes, position, position - 2 * kept_modes + length)


def forward_y(values, phases):
    cosine_table = jnp.cos(phases)
    sine_table = jnp.sin(phases)
    with_cos = jnp.einsum("brcxy,yj->brcxj", values, cosine_table, precision=PRECISE)
    with_sin = jnp.einsum("brcxy,yj->brcxj", values, sine_table, precision=PRECISE)
    real_part = with_cos[:, 0] + with_sin[:, 1]
    imag_part = with_cos[:, 1] - with_sin[:, 0]
    return jnp.stack([real_part, imag_part], axis=1)


def inverse_y(values, phases):
    cosine_table = jnp.cos(phases)
    sine_table = jnp.sin(phases)
    with_cos = jnp.einsum("brcxj,yj->brcxy", values, cosine_table, precision=PRECISE)
    with_sin = jnp.einsum("brcxj,yj->brcxy", values, sine_table, precision=PRECISE)
    real_part = with_cos[:, 0] - with_sin[:, 1]
    imag_part = with_sin[:, 0] + with_cos[:, 1]
    return jnp.stack([real_part, imag_part], axis=1)


def local(field, cotangent, spectral_weight, pointwise_weight, bias):
    channels, rows_x, rows_y, depth_cells = field.shape
    blocks_z = spectral_weight.shape[3]
    pair_rows = spectral_weight.shape[4]
    width_x = 2 * MX
    width_y = 2 * MY
    full_x = rows_x * lax.axis_size("gx")
    full_y = rows_y * lax.axis_size("gy")
    cell_count = float(full_x * full_y * depth_cells)
    place_x = lax.axis_index("gx")
    place_y = lax.axis_index("gy")
    own_x = place_x * rows_x + jnp.arange(rows_x, dtype=jnp.int32)
    freq_x = frequency(jnp.arange(width_x, dtype=jnp.int32), MX, full_x)
    freq_y = frequency(jnp.arange(width_y, dtype=jnp.int32), MY, full_y)
    phases_full_y = angles(freq_y, jnp.arange(full_y, dtype=jnp.int32), full_y)
    z_phases = angles(
        jnp.arange(MZ, dtype=jnp.int32), jnp.arange(depth_cells, dtype=jnp.int32), depth_cells
    )
    table_z = jnp.stack([jnp.cos(z_phases), -jnp.sin(z_phases)], axis=2).reshape(
        depth_cells, 2 * MZ
    )
    kz_own = place_y * blocks_z + jnp.arange(blocks_z, dtype=jnp.int32)
    weight_z = (jnp.where(kz_own == 0, 1.0, 2.0).astype(jnp.float32) / cell_count)[None, :, None]
    own_first = place_x * pair_rows
    flat_width = blocks_z * 2 * channels

    def kx_terms(values, places, first_pair, count):
        kx_count = min(count // width_y + 2, width_x)
        kx_first = jnp.minimum(first_pair // width_y, width_x - kx_count)
        kx_ids = kx_first + jnp.arange(kx_count, dtype=jnp.int32)
        phases = angles(frequency(kx_ids, MX, full_x), places, full_x)
        cosine_table = jnp.cos(phases)
        sine_table = jnp.sin(phases)
        real_part = jnp.einsum(
            "bcxj,xi->ijbc", values[:, 0], cosine_table, precision=PRECISE
        ) + jnp.einsum("bcxj,xi->ijbc", values[:, 1], sine_table, precision=PRECISE)
        imag_part = jnp.einsum(
            "bcxj,xi->ijbc", values[:, 1], cosine_table, precision=PRECISE
        ) - jnp.einsum("bcxj,xi->ijbc", values[:, 0], sine_table, precision=PRECISE)
        terms = jnp.stack([real_part, imag_part], axis=3).reshape(kx_count * width_y, flat_width)
        offset = first_pair - kx_first * width_y
        return lax.dynamic_slice_in_dim(terms, offset, count, 0)

    def analyze(values):
        flat = values.reshape(-1, depth_cells)
        spectra = jnp.einsum("zk,mz->km", table_z, flat, precision=PRECISE).reshape(
            2 * MZ, channels, rows_x, rows_y
        )
        columns = lax.all_to_all(spectra, "gy", split_axis=0, concat_axis=3, tiled=True)
        mode_data = forward_y(columns.reshape(blocks_z, 2, channels, rows_x, full_y), phases_full_y)
        portion = lax.all_gather(mode_data, "gx", axis=3, tiled=True)
        places = jnp.arange(portion.shape[3], dtype=jnp.int32)
        owned = kx_terms(portion, places, own_first, pair_rows)
        return jnp.transpose(owned.reshape(pair_rows, blocks_z, 2, channels), (2, 3, 1, 0))

    def synthesize(spectrum):
        portion = lax.all_gather(spectrum, "gx", axis=3, tiled=True)
        blocks = portion.reshape(2, channels, blocks_z, width_x, width_y)
        phases = angles(freq_x, own_x, full_x)
        cosine_table = jnp.cos(phases)
        sine_table = jnp.sin(phases)
        real_part = jnp.einsum(
            "cbij,xi->bcxj", blocks[0], cosine_table, precision=PRECISE
        ) - jnp.einsum("cbij,xi->bcxj", blocks[1], sine_table, precision=PRECISE)
        imag_part = jnp.einsum(
            "cbij,xi->bcxj", blocks[0], sine_table, precision=PRECISE
        ) + jnp.einsum("cbij,xi->bcxj", blocks[1], cosine_table, precision=PRECISE)
        mode_data = jnp.stack([real_part, imag_part], axis=1)
        fields = inverse_y(mode_data, phases_full_y)
        columns = lax.all_to_all(fields, "gy", split_axis=4, concat_axis=0, tiled=True)
        flat = columns.reshape(2 * MZ, -1)
        return jnp.einsum("km,zk->mz", flat, table_z, precision=PRECISE).reshape(
            channels, rows_x, rows_y, depth_cells
        )

    weights = spectral_weight.astype(jnp.float32)
    widened = field.astype(jnp.float32)
    spec_u = analyze(widened)
    mixed_re = jnp.einsum("cobp,cbp->obp", weights[0], spec_u[0], precision=PRECISE) - jnp.einsum(
        "cobp,cbp->obp", weights[1], spec_u[1], precision=PRECISE
    )
    mixed_im = jnp.einsum("cobp,cbp->obp", weights[0], spec_u[1], precision=PRECISE) + jnp.einsum(
        "cobp,cbp->obp", weights[1], spec_u[0], precision=PRECISE
    )
    mixed_modes = jnp.stack([mixed_re, mixed_im]) * weight_z
    conv = synthesize(mixed_modes)
    pointwise = jnp.dot(
        pointwise_weight.T, field.reshape(channels, -1), preferred_element_type=jnp.float32
    ).reshape(field.shape)
    preact = pointwise + bias[:, None, None, None] + conv
    activated, pullback = jax.vjp(jax.nn.gelu, preact)
    gradient = pullback(cotangent.astype(jnp.float32))[0]
    grad_mix = analyze(gradient) * weight_z
    spec_re = jnp.einsum("cobp,obp->cbp", weights[0], grad_mix[0], precision=PRECISE) + jnp.einsum(
        "cobp,obp->cbp", weights[1], grad_mix[1], precision=PRECISE
    )
    spec_im = jnp.einsum("cobp,obp->cbp", weights[0], grad_mix[1], precision=PRECISE) - jnp.einsum(
        "cobp,obp->cbp", weights[1], grad_mix[0], precision=PRECISE
    )
    grad_spec = jnp.stack([spec_re, spec_im])
    weight_re = jnp.einsum("cbp,obp->cobp", spec_u[0], grad_mix[0], precision=PRECISE) + jnp.einsum(
        "cbp,obp->cobp", spec_u[1], grad_mix[1], precision=PRECISE
    )
    weight_im = jnp.einsum("cbp,obp->cobp", spec_u[0], grad_mix[1], precision=PRECISE) - jnp.einsum(
        "cbp,obp->cobp", spec_u[1], grad_mix[0], precision=PRECISE
    )
    grad_spectral = jnp.stack([weight_re, weight_im])
    returned = synthesize(grad_spec)
    grad_flat = gradient.reshape(channels, -1)
    back_point = jnp.dot(
        pointwise_weight.astype(jnp.float32), grad_flat, precision=PRECISE
    ).reshape(field.shape)
    grad_field = (back_point + returned).astype(jnp.bfloat16)
    local_weight = jnp.dot(widened.reshape(channels, -1), grad_flat.T, precision=PRECISE)
    local_bias = jnp.sum(grad_flat, axis=1)
    summed_weight, summed_bias = lax.psum((local_weight, local_bias), ("gx", "gy"))
    shrink = cell_count ** (-0.5)
    return (
        activated.astype(jnp.bfloat16),
        grad_field,
        grad_spectral,
        summed_weight * shrink,
        summed_bias * shrink,
    )


def solution(mesh):
    placed = (
        P(None, "gx", "gy", None),
        P(None, "gx", "gy", None),
        P(None, None, None, "gy", "gx"),
        P(),
        P(),
    )
    return jax.shard_map(
        local,
        mesh=mesh,
        in_specs=placed,
        out_specs=(
            P(None, "gx", "gy", None),
            P(None, "gx", "gy", None),
            P(None, None, None, "gy", "gx"),
            P(),
            P(),
        ),
        check_vma=False,
    )
```

profile of v0, /device:TPU:0, one launch (start us, length us, event | category | flops | bytes accessed | tf_op | source)
XLA Modules:
  0.0 1144.5 jit_solution(5353411915811552613)
XLA Ops:
  10.4 3.7 copy.258
  14.1 5.3 reshape.217
  19.4 4.2 all-to-all-start
  23.8 8.3 all-to-all-done
  34.6 5.3 reshape.218
  39.9 5.7 copy.387
  45.6 3.6 reshape.211
  53.3 12.5 %fusion.240 = (bf16[1,20,20,6,288]{4,0,3,2,1:T(2,128)(2,1)}, bf16[1,20,20,6,288]{4,0,3,2,1:T(2,128)(2,1)}) fusion(bf16[2,20,20,6,288]{4,0,3,2,1:T(2,128)(2,1)} %param.7), kind=kLoop, calls=%fused_computation.294 | loop fusion | bytes 5529600 | tf_op jit(solution)/shard_map/slice | solution.py:125
  65.8 126.3 %all-gather.5.cloned.1.call-done = f32[6,2,20,64,48]{4,2,3,1,0:T(8,128)} async-done(((f32[6,2,20,8,48]{4,2,3,1,0:T(8,128)}), f32[6,2,20,64,48]{4,2,3,1,0:T(8,128)}) %all-gather.5.cloned.1.call-update) | async-done | bytes 2949136 | tf_op jit(solution)/shard_map/all_gather | solution.py:96
  192.1 8.2 slice_bitcast_fusion.3
  200.3 5.3 copy.262
  205.6 5.7 copy.263
  211.3 10.5 fusion.114
  221.8 8.5 fusion.112
  230.4 8.6 fusion.31
  238.9 8.7 fusion.30
  248.5 6.2 fusion
  257.0 193.9 %all-gather.7.cloned.1.call-done = f32[2,20,6,2304]{1,0,2,3:T(2,128)} async-done(((f32[2,20,6,288]{1,0,2,3:T(2,128)}), f32[2,20,6,2304]{1,0,2,3:T(2,128)}) %all-gather.7.cloned.1.call-update) | async-done | bytes 2211856 | tf_op jit(solution)/shard_map/all_gather | solution.py:102
  451.0 17.0 %fusion.239 = (f32[1,20,6,2304]{1,0,2,3:T(1,128)}, f32[1,20,6,2304]{1,0,2,3:T(1,128)}) fusion(f32[2,20,6,2304]{1,0,2,3:T(2,128)} %all-gather.7.cloned.1.call-done), kind=kLoop, calls=%fused_computation.293 | loop fusion | bytes 4423680 | tf_op jit(solution)/shard_map/slice | solution.py:109
  468.0 11.2 copy.389
  482.2 4.3 fusion.101
  488.8 11.2 copy.390
  503.4 3.6 fusion.29
  514.3 5.3 reshape.219
  519.6 3.5 all-to-all-start.1
  525.9 5.6 all-to-all-done.1
  533.5 5.3 reshape.220
  538.8 6.6 copy.385
  545.4 4.5 copy.280
  549.9 4.4 reshape.178
  555.7 9.6 fusion.236
  569.5 4.1 copy.285
  573.6 4.6 reshape.221
  578.2 10.9 all_to_all.60
  591.1 5.3 reshape.222
  596.4 5.7 copy.393
  602.1 3.6 reshape.214
  609.5 135.4 %all-gather.9.cloned.1.call-done = f32[6,2,20,64,48]{4,2,3,1,0:T(8,128)} async-done(((f32[6,2,20,8,48]{4,2,3,1,0:T(8,128)}), f32[6,2,20,64,48]{4,2,3,1,0:T(8,128)}) %all-gather.9.cloned.1.call-update) | async-done | bytes 2949136 | tf_op jit(solution)/shard_map/all_gather | solution.py:96
  745.0 8.2 slice_bitcast_fusion.1
  753.1 5.3 copy.289
  758.4 10.3 fusion.110
  768.8 5.5 copy.290
  774.3 10.5 fusion.108
  784.8 10.4 fusion.27
  795.1 8.5 fusion.26
  804.7 10.3 add_bitcast_fusion
  820.6 3.5 copy.409
  826.8 43.2 %all-reduce = (f32[20,20]{0,1:T(8,128)S(1)}, f32[20]{0:T(128)S(1)}) all-reduce(f32[20,20]{0,1:T(8,128)S(1)} %fusion.40, f32[20]{0:T(128)S(1)} %get-tuple-element.49), channel_id=1, replica_groups=mesh['gx'=8,'gy'=4] {'gx','gy'}, use_global_device_ids=true, to_apply=%region_0.1 | all-reduce | flops 420 | bytes 3360 | tf_op jit(solution)/shard_map/psum | solution.py:161
  870.0 5.1 fusion.241
  875.1 137.4 %all-gather.11.cloned.1.call-done = f32[2,20,6,2304]{1,0,2,3:T(2,128)} async-done(((f32[2,20,6,288]{1,0,2,3:T(2,128)}), f32[2,20,6,2304]{1,0,2,3:T(2,128)}) %all-gather.11.cloned.1.call-update) | async-done | bytes 2211856 | tf_op jit(solution)/shard_map/all_gather | solution.py:102
  1012.5 17.0 %fusion.238 = (f32[1,20,6,2304]{1,0,2,3:T(1,128)}, f32[1,20,6,2304]{1,0,2,3:T(1,128)}) fusion(f32[2,20,6,2304]{1,0,2,3:T(2,128)} %all-gather.11.cloned.1.call-done), kind=kLoop, calls=%fused_computation.292 | loop fusion | bytes 4423680 | tf_op jit(solution)/shard_map/slice | solution.py:109
  1029.5 11.2 copy.395
  1043.7 3.5 fusion.98
  1049.5 11.2 copy.396
  1063.9 3.6 fusion.25
  1074.7 5.3 reshape.223
  1080.0 3.7 all-to-all-start.3
  1092.7 4.5 pad_maximum_fusion
  1097.2 12.3 %copy.311 = f32[2,20,20,6,288]{4,0,3,2,1:T(2,128)} copy(f32[2,20,20,6,288]{4,2,3,1,0:T(8,128)} %pad_maximum_fusion) | data formatting | bytes 11059200
  1111.5 5.3 reshape.224
  1116.8 6.7 copy.386
  1123.5 4.5 copy.305
  1128.0 4.3 reshape.184
  1132.7 5.0 add_convert_fusion
  (123 shorter events, 81.5 us)
Async XLA Ops:
  7.2 1.3 copy-start
  19.4 12.7 %all-to-all-start = ((f32[4,1,30720]{2,1,0:T(1,128)}), f32[4,1,30720]{2,1,0:T(1,128)S(1)}, u32[]{:S(2)}, u32[]{:S(2)}) async-start(f32[4,1,30720]{2,1,0:T(1,128)} %reshape.217), calls=%async_computation | async-start | bytes 983040 | tf_op jit(solution)/shard_map/all_to_all | solution.py:94
  23.6 168.5 %all-gather.5.cloned.1.call-start = ((), (), s32[]{:S(2)}) async-start(), calls=%async_computation.4 | async-start | bytes 10616832 | tf_op jit(solution)/shard_map/all_gather | solution.py:96
  53.0 398.0 %all-gather.7.cloned.1.call-start = ((), (), s32[]{:S(2)}) async-start(), calls=%async_computation.5 | async-start | bytes 15925248 | tf_op jit(solution)/shard_map/all_gather | solution.py:102
  211.3 10.5 copy-start.7
  221.8 17.1 %copy-start.4 = (f32[6,20,64,48]{2,3,1,0:T(8,128)S(1)}, f32[6,20,64,48]{2,3,1,0:T(8,128)}, u32[]{:S(2)}) copy-start(f32[6,20,64,48]{2,3,1,0:T(8,128)} %copy.262) | copy-start | bytes 4423684
  482.2 4.3 copy-start.8
  503.4 3.6 copy-start.6
  503.4 3.6 copy-start.10
  514.3 8.8 copy-start.11
  519.6 11.9 %all-to-all-start.1 = ((f32[4,1,30720]{2,1,0:T(1,128)}), f32[4,1,30720]{2,1,0:T(1,128)S(1)}, u32[]{:S(2)}, u32[]{:S(2)}) async-start(f32[4,1,30720]{2,1,0:T(1,128)} %reshape.219), calls=%async_computation.1 | async-start | bytes 983040 | tf_op jit(solution)/shard_map/all_to_all | solution.py:115
  523.0 221.9 %all-gather.9.cloned.1.call-start = ((), (), s32[]{:S(2)}) async-start(), calls=%async_computation.6 | async-start | bytes 10616832 | tf_op jit(solution)/shard_map/all_gather | solution.py:96
  549.9 5.8 copy-start.12
  565.3 1.6 copy-start.1
  609.5 403.0 %all-gather.11.cloned.1.call-start = ((), (), s32[]{:S(2)}) async-start(), calls=%async_computation.7 | async-start | bytes 15925248 | tf_op jit(solution)/shard_map/all_gather | solution.py:102
  774.2 20.9 %copy-start.3 = (f32[6,20,64,48]{2,3,1,0:T(8,128)S(1)}, f32[6,20,64,48]{2,3,1,0:T(8,128)}, u32[]{:S(2)}) copy-start(f32[6,20,64,48]{2,3,1,0:T(8,128)} %copy.289) | copy-start | bytes 4423684
  820.6 3.5 copy-start.2
  1043.7 3.5 copy-start.9
  1063.9 3.6 copy-start.5
  1072.2 20.5 %slice-start.2 = ((s8[4423680]{0:T(1024)(128)(4,1)}), s8[229376]{0:T(1024)(128)(4,1)S(1)}, s32[]{:S(2)}) async-start(s8[4423680]{0:T(1024)(128)(4,1)} %bitcast.306), calls=%async_computation.10 | async-start | bytes 458752
  1080.0 29.5 %all-to-all-start.3 = ((f32[4,1,30720]{2,1,0:T(1,128)}), f32[4,1,30720]{2,1,0:T(1,128)S(1)}, u32[]{:S(2)}, u32[]{:S(2)}) async-start(f32[4,1,30720]{2,1,0:T(1,128)} %reshape.223), calls=%async_computation.3 | async-start | bytes 983040 | tf_op jit(solution)/shard_map/all_to_all | solution.py:115
  1084.9 7.8 slice-start.3
  1087.8 4.8 slice-start
  1087.8 4.8 slice-start.1
Sparse Core Ops, SparseCore 0:
  53.1 138.9 all-gather.4
  257.1 193.7 all-gather.6
  609.6 135.3 all-gather.8
  817.6 194.7 all-gather.10
where the time goes:
time: 1150 us; the launch traced here: 1140 us
  waiting for transfers between devices  607 us (53%)
  local copies, waits for them, and re-layouts  284 us (25%)
  matrix products  139 us (12%)
  blocking collectives  54.1 us (5%)
  other arithmetic  33.3 us (3%)
  between operations  14.7 us (1%)
  starting transfers between devices  11.9 us (1%)
    all_gather x2, waiting for transfers between devices, synthesize(): portion = lax.all_gather(spectrum, 'gx', axis=3, tiled=True)  331 us
    all_gather x2, waiting for transfers between devices, analyze(): portion = lax.all_gather(mode_data, 'gx', axis=3, tiled=True)  262 us
    unnamed x53, local copies, waits for them, and re-layouts  69.2 us
    psum x1, blocking collectives, local(): lax.psum((local_weight, local_bias), ('gx', 'gy'))  43.2 us
    slice x2, local copies, waits for them, and re-layouts, synthesize(): blocks[1]  34 us
    squeeze x4, local copies, waits for them, and re-layouts, synthesize(): blocks[1]  28.9 us
    squeeze x4, local copies, waits for them, and re-layouts, synthesize(): blocks[0]  28.4 us
    squeeze x4, local copies, waits for them, and re-layouts, kx_terms(): values[:, 0]  26.9 us
  transfers between devices with their start and end apart: 7, of which 6 were waited for; matrix products, arithmetic and copies ran while one was open for 5% of the time, Pallas kernels for 0%

commit v1 on v0

--- a/solution.py
+++ b/solution.py
@@ -1,8 +1,12 @@
+import functools
 import math
 
 import jax
 import jax.numpy as jnp
 from jax import lax
+import numpy as np
+from jax.experimental import pallas as pl
+from jax.experimental.pallas import tpu as pltpu
 from jax.sharding import PartitionSpec as P
 
 MX = 24
@@ -169,6 +173,742 @@
     )
 
 
+LANES = 128
+HALF = 64
+VMEM_BYTES = 48 * 1024 * 1024
+
+
+def split_table(table):
+    high = table.astype(jnp.bfloat16)
+    low = (table - high.astype(np.float64)).astype(jnp.bfloat16)
+    return high, low
+
+
+def frequency_table(kept_modes, length):
+    position = np.arange(2 * kept_modes)
+    return np.where(position < kept_modes, position, position - 2 * kept_modes + length)
+
+
+def phase_table(frequencies, places, length):
+    product = places[:, None] * frequencies[None, :] % length
+    return product.astype(np.float64) * (TWO_PI / length)
+
+
+def split(values):
+    high = values.astype(jnp.bfloat16)
+    low = (values - high.astype(jnp.float32)).astype(jnp.bfloat16)
+    return high, low
+
+
+def product(left, right, contract=((1,), (0,)), precision=None):
+    return lax.dot_general(
+        left, right, (contract, ((), ())), preferred_element_type=jnp.float32, precision=precision
+    )
+
+
+NT = ((1,), (1,))
+TN = ((0,), (0,))
+
+
+def lane_ids(rows):
+    return lax.broadcasted_iota(jnp.int32, (rows, LANES), 1)
+
+
+def roll_lanes(values, shift):
+    shift = shift % LANES
+    if shift == 0:
+        return values
+    return pltpu.roll(values, shift, 1)
+
+
+class Plan:
+    def __init__(self, field_shape, weight_shape, size_x, size_y):
+        self.channels, self.rows_x, self.rows_y, self.depth = field_shape
+        self.size_x, self.size_y = size_x, size_y
+        self.blocks_z = weight_shape[3]
+        self.pair_rows = weight_shape[4]
+        self.full_x = self.rows_x * size_x
+        self.full_y = self.rows_y * size_y
+        self.width_x, self.width_y = 2 * MX, 2 * MY
+        self.cells = self.rows_x * self.rows_y
+        self.part_c, self.part_z = 0, 0
+        for part_z in range(1, self.blocks_z + 1):
+            part_c = size_x // part_z
+            if size_x % part_z or self.blocks_z % part_z or self.channels % part_c:
+                continue
+            self.part_c, self.part_z = part_c, part_z
+        self.fits = False
+        if self.part_c == 0:
+            return
+        self.own_c = self.channels // self.part_c
+        self.own_z = self.blocks_z // self.part_z
+        self.planes = self.own_c * self.own_z
+        self.plane_rows = 16
+        self.own_kx = self.pair_rows // self.width_y
+        self.devices = size_x * size_y
+        self.fits = (
+            self.cells == LANES
+            and self.rows_y == 16
+            and self.depth % LANES == 0
+            and self.planes < self.plane_rows
+            and self.pair_rows % self.width_y == 0
+            and self.pair_rows == 2 * LANES + 32
+            and self.width_y <= HALF
+            and self.channels + 1 <= min(self.devices, 24)
+            and self.own_z * 2 * self.part_z * size_y == 2 * MZ
+        )
+
+    def z_table(self, scaled):
+        kz = np.arange(MZ)
+        phases = phase_table(kz, np.arange(self.depth), self.depth)
+        both = np.stack([np.cos(phases), -np.sin(phases)])
+        if scaled:
+            cells = float(self.full_x * self.full_y * self.depth)
+            both = both * (np.where(kz == 0, 1.0, 2.0) / cells)
+        both = both.reshape(2, self.depth, self.size_y, self.part_z, self.own_z)
+        return both.transpose(2, 3, 0, 4, 1).reshape(2 * MZ, self.depth)
+
+    def y_table(self):
+        freq = frequency_table(MY, self.full_y)
+        phases = phase_table(freq, np.arange(self.full_y), self.full_y)
+        cosine, sine = np.cos(phases), np.sin(phases)
+        one = np.zeros((self.size_y, 2, self.rows_y, 2, HALF))
+        by_block = (self.size_y, self.rows_y, self.width_y)
+        one[:, 0, :, 0, : self.width_y] = cosine.reshape(by_block)
+        one[:, 1, :, 0, : self.width_y] = sine.reshape(by_block)
+        one[:, 0, :, 1, : self.width_y] = -sine.reshape(by_block)
+        one[:, 1, :, 1, : self.width_y] = cosine.reshape(by_block)
+        full = np.zeros((self.size_y, 2, self.rows_x, self.rows_y, self.rows_x, LANES))
+        for row in range(self.rows_x):
+            full[:, :, row, :, row, :] = one.reshape(self.size_y, 2, self.rows_y, LANES)
+        return full.reshape(self.size_y * 2 * LANES, self.rows_x * LANES)
+
+    def x_tables(self):
+        freq = frequency_table(MX, self.full_x)
+        phases = phase_table(freq, np.arange(self.full_x), self.full_x)
+        cosine, sine = np.cos(phases), np.sin(phases)
+        forward = np.concatenate([cosine.T, sine.T], axis=0)
+        inverse = np.concatenate([cosine, sine], axis=0)
+        tables = []
+        for table in (forward, inverse):
+            high, low = split_table(table)
+            tables.append(np.concatenate([high, low, high], axis=1))
+        return tables
+
+
+def call(kernel, out_shape, scratch, *operands, smem=(), **more):
+    specs = [
+        pl.BlockSpec(memory_space=pltpu.SMEM if at in smem else pltpu.VMEM)
+        for at in range(len(operands))
+    ]
+    single = not isinstance(out_shape, (tuple, list))
+    outs = pl.BlockSpec(memory_space=pltpu.VMEM)
+    return pl.pallas_call(
+        kernel,
+        out_shape=out_shape,
+        in_specs=specs,
+        out_specs=outs if single else [outs] * len(out_shape),
+        scratch_shapes=scratch,
+        compiler_params=pltpu.CompilerParams(vmem_limit_bytes=VMEM_BYTES),
+        **more,
+    )(*operands)
+
+
+def put_spectrum(plan, out_ref, channel, rows):
+    block, inner = divmod(channel, plan.own_c)
+    size = plan.own_z
+    at = 0
+    for place_y in range(plan.size_y):
+        for part in range(plan.part_z):
+            place_x = block * plan.part_z + part
+            for which in range(2):
+                out_ref[place_x, place_y, which, inner * size : (inner + 1) * size, :] = rows[
+                    at : at + size
+                ]
+                at += size
+
+
+def take_spectrum(plan, in_ref, rows_ref, channel):
+    block, inner = divmod(channel, plan.own_c)
+    size = plan.own_z
+    at = 0
+    for place_y in range(plan.size_y):
+        for part in range(plan.part_z):
+            place_x = block * plan.part_z + part
+            for which in range(2):
+                rows_ref[at : at + size, :] = in_ref[
+                    place_x, place_y, which, inner * size : (inner + 1) * size, :
+                ]
+                at += size
+    return rows_ref[...]
+
+
+def clear_spare(plan, out_ref):
+    zeros = jnp.zeros((plan.plane_rows - plan.planes, LANES), jnp.float32)
+    for place_x in range(plan.size_x):
+        for place_y in range(plan.size_y):
+            for which in range(2):
+                out_ref[place_x, place_y, which, plan.planes :, :] = zeros
+
+
+def depth_analysis_kernel(plan, field_ref, table_ref, out_ref):
+    clear_spare(plan, out_ref)
+    table = table_ref[...]
+    for channel in range(plan.channels):
+        block = field_ref[channel].reshape(plan.cells, plan.depth)
+        both = product(table, block, NT)
+        put_spectrum(plan, out_ref, channel, both[: 2 * MZ] + both[2 * MZ :])
+
+
+def plane_analysis_kernel(
+    plan, in_ref, y_high_ref, y_low_ref, x_ref, out_ref, sums_ref, rows_ref, modes_ref, rest_ref
+):
+    pad = plan.plane_rows
+    spare = jnp.zeros((1, LANES), jnp.float32)
+    for place_x in range(plan.size_x):
+        for place_y in range(plan.size_y):
+            spare = spare + in_ref[place_x, place_y, 0, plan.planes : plan.planes + 1, :]
+    sums_ref[...] = jnp.broadcast_to(spare, (8, LANES))
+    left = jnp.concatenate(
+        [
+            in_ref[:, place_y, which].reshape(plan.size_x * pad, LANES)
+            for place_y in range(plan.size_y)
+            for which in range(2)
+        ],
+        axis=1,
+    )
+    high, low = split(left)
+    y_high = y_high_ref[...]
+    along_y = product(high, y_high) + product(low, y_high) + product(high, y_low_ref[...])
+    for place_x in range(plan.size_x):
+        for row in range(plan.rows_x):
+            at = (place_x * plan.rows_x + row) * pad
+            rows_ref[at : at + pad, :] = along_y[
+                place_x * pad : (place_x + 1) * pad, row * LANES : (row + 1) * LANES
+            ]
+    right = jnp.concatenate(
+        [rows_ref[pl.ds(plane, plan.full_x, stride=pad), :] for plane in range(plan.planes)], axis=1
+    )
+    high, low = split(right)
+    both = product(x_ref[...], jnp.concatenate([high, high, low], axis=0))
+    sign = jnp.where(lane_ids(plan.width_x) < HALF, 1.0, -1.0)
+    for plane in range(plan.planes):
+        mine = slice(plane * LANES, (plane + 1) * LANES)
+        turned = roll_lanes(both[plan.width_x :, mine], HALF)
+        modes_ref[pl.ds(plane, plan.width_x, stride=pad), :] = (
+            both[: plan.width_x, mine] + sign * turned
+        )
+    modes_ref[pl.ds(plan.planes, plan.width_x, stride=pad), :] = jnp.zeros(
+        (plan.width_x, LANES), jnp.float32
+    )
+    lanes = lane_ids(pad)
+    width = plan.width_y
+    for place_x in range(plan.size_x):
+        for which in range(2):
+            tiles = [None, None, None]
+            for inner in range(plan.own_kx):
+                kx = place_x * plan.own_kx + inner
+                first = inner * width
+                turned = roll_lanes(modes_ref[kx * pad : (kx + 1) * pad, :], first - which * HALF)
+                tile, offset = divmod(first, LANES)
+                for at in (tile, tile + 1):
+                    begin = first - at * LANES
+                    if begin >= LANES or begin + width <= 0:
+                        continue
+                    if tiles[at] is None:
+                        tiles[at] = turned
+                    else:
+                        tiles[at] = jnp.where(lanes < begin, tiles[at], turned)
+            for at in range(2):
+                row = at * 2 * pad + which * pad
+                out_ref[place_x, row : row + pad, :] = tiles[at]
+            rest_ref[which * pad : (which + 1) * pad, :] = tiles[2]
+        out_ref[place_x, 4 * pad : 4 * pad + 8, :] = pack_rest(rest_ref)
+
+
+def pack_rest(rest_ref):
+    lanes = lane_ids(8)
+    packed = rest_ref[0:8, :]
+    for group in range(1, 4):
+        turned = roll_lanes(rest_ref[group * 8 : (group + 1) * 8, :], group * 32)
+        packed = jnp.where(lanes < group * 32, packed, turned)
+    return packed
+
+
+def unpack_rest(packed, rest_ref):
+    for group in range(4):
+        rest_ref[group * 8 : (group + 1) * 8, :] = roll_lanes(packed, -group * 32)
+
+
+def take_modes(plan, in_ref, modes_ref, rest_ref):
+    pad, size = plan.plane_rows, plan.own_z
+    for place_x in range(plan.size_x):
+        block, part = divmod(place_x, plan.part_z)
+        unpack_rest(in_ref[place_x, 4 * pad : 4 * pad + 8, :], rest_ref)
+        for which in range(2):
+            for inner in range(plan.own_c):
+                channel = block * plan.own_c + inner
+                row = which * pad + inner * size
+                kz = slice(part * size, (part + 1) * size)
+                for at in range(2):
+                    begin = at * 2 * pad + row
+                    modes_ref[channel, which, kz, at * LANES : (at + 1) * LANES] = in_ref[
+                        place_x, begin : begin + size, :
+                    ]
+                modes_ref[channel, which, kz, 2 * LANES :] = rest_ref[row : row + size, 0:32]
+
+
+def put_modes(plan, modes_ref, out_ref, rest_ref):
+    pad, size = plan.plane_rows, plan.own_z
+    zeros = jnp.zeros((pad - plan.planes, LANES), jnp.float32)
+    rest_ref[...] = jnp.zeros((2 * pad, LANES), jnp.float32)
+    for place_x in range(plan.size_x):
+        block, part = divmod(place_x, plan.part_z)
+        for which in range(2):
+            for inner in range(plan.own_c):
+                channel = block * plan.own_c + inner
+                row = which * pad + inner * size
+                kz = slice(part * size, (part + 1) * size)
+                for at in range(2):
+                    begin = at * 2 * pad + row
+                    out_ref[place_x, begin : begin + size, :] = modes_ref[
+                        channel, which, kz, at * LANES : (at + 1) * LANES
+                    ]
+                rest_ref[row : row + size, 0:32] = modes_ref[channel, which, kz, 2 * LANES :]
+            for at in range(2):
+                begin = at * 2 * pad + which * pad + plan.planes
+                out_ref[place_x, begin : begin + pad - plan.planes, :] = zeros
+        out_ref[place_x, 4 * pad : 4 * pad + 8, :] = pack_rest(rest_ref)
+
+
+def mix_kernel(plan, in_ref, weight_ref, out_ref, spectrum_ref, mixed_ref, rest_ref):
+    take_modes(plan, in_ref, spectrum_ref, rest_ref)
+    shape = (plan.blocks_z, plan.pair_rows)
+
+    def one(out_channel, carry):
+        real_part = jnp.zeros(shape, jnp.float32)
+        imag_part = jnp.zeros(shape, jnp.float32)
+        for channel in range(plan.channels):
+            weight_re = weight_ref[0, channel, out_channel].astype(jnp.float32)
+            weight_im = weight_ref[1, channel, out_channel].astype(jnp.float32)
+            value_re = spectrum_ref[channel, 0]
+            value_im = spectrum_ref[channel, 1]
+            real_part += weight_re * value_re - weight_im * value_im
+            imag_part += weight_re * value_im + weight_im * value_re
+        mixed_ref[out_channel, 0] = real_part
+        mixed_ref[out_channel, 1] = imag_part
+        return carry
+
+    lax.fori_loop(0, plan.channels, one, 0)
+    put_modes(plan, mixed_ref, out_ref, rest_ref)
+
+
+def mix_back_kernel(plan, in_ref, weight_ref, out_ref, grad_ref, mixed_ref, rest_ref):
+    take_modes(plan, in_ref, grad_ref, rest_ref)
+    shape = (plan.blocks_z, plan.pair_rows)
+
+    def one(channel, carry):
+        real_part = jnp.zeros(shape, jnp.float32)
+        imag_part = jnp.zeros(shape, jnp.float32)
+        for out_channel in range(plan.channels):
+            weight_re = weight_ref[0, channel, out_channel].astype(jnp.float32)
+            weight_im = weight_ref[1, channel, out_channel].astype(jnp.float32)
+            value_re = grad_ref[out_channel, 0]
+            value_im = grad_ref[out_channel, 1]
+            real_part += weight_re * value_re + weight_im * value_im
+            imag_part += weight_re * value_im - weight_im * value_re
+        mixed_ref[channel, 0] = real_part
+        mixed_ref[channel, 1] = imag_part
+        return carry
+
+    lax.fori_loop(0, plan.channels, one, 0)
+    put_modes(plan, mixed_ref, out_ref, rest_ref)
+
+
+def weight_grad_kernel(plan, spectrum_ref, grad_ref, out_ref):
+    value_re = spectrum_ref[0, 0]
+    value_im = spectrum_ref[0, 1]
+    for out_channel in range(plan.channels):
+        grad_re = grad_ref[out_channel, 0]
+        grad_im = grad_ref[out_channel, 1]
+        out_ref[0, 0, out_channel] = value_re * grad_re + value_im * grad_im
+        out_ref[1, 0, out_channel] = value_re * grad_im - value_im * grad_re
+
+
+def weight_grad(plan, spectrum, grad):
+    modes = (plan.blocks_z, plan.pair_rows)
+    return pl.pallas_call(
+        functools.partial(weight_grad_kernel, plan),
+        grid=(plan.channels,),
+        out_shape=jax.ShapeDtypeStruct((2, plan.channels, plan.channels) + modes, jnp.float32),
+        in_specs=[
+            pl.BlockSpec((1, 2) + modes, lambda channel: (channel, 0, 0, 0)),
+            pl.BlockSpec((plan.channels, 2) + modes, lambda channel: (0, 0, 0, 0)),
+        ],
+        out_specs=pl.BlockSpec(
+            (2, 1, plan.channels) + modes, lambda channel: (0, channel, 0, 0, 0)
+        ),
+        compiler_params=pltpu.CompilerParams(vmem_limit_bytes=VMEM_BYTES),
+    )(spectrum, grad)
+
+
+def plane_synthesis_kernel(
+    plan, in_ref, sums_ref, y_high_ref, y_low_ref, x_ref, out_ref, rows_ref, modes_ref, rest_ref
+):
+    pad, width = plan.plane_rows, plan.width_y
+    lanes = lane_ids(pad)
+    for place_x in range(plan.size_x):
+        unpack_rest(in_ref[place_x, 4 * pad : 4 * pad + 8, :], rest_ref)
+        tiles = []
+        for which in range(2):
+            row = which * pad
+            tiles.append(
+                [
+                    in_ref[place_x, row : row + pad, :],
+                    in_ref[place_x, 2 * pad + row : 3 * pad + row, :],
+                    rest_ref[row : row + pad, :],
+                ]
+            )
+        for inner in range(plan.own_kx):
+            first = inner * width
+            tile, offset = divmod(first, LANES)
+            pieces = []
+            for which in range(2):
+                piece = roll_lanes(tiles[which][tile], which * HALF - offset)
+                if offset + width > LANES:
+                    later = roll_lanes(tiles[which][tile + 1], which * HALF - offset)
+                    piece = jnp.where(lanes < which * HALF + LANES - offset, piece, later)
+                pieces.append(piece)
+            merged = jnp.where(lanes < HALF, pieces[0], pieces[1])
+            used = jnp.bitwise_and(lanes, HALF - 1) < width
+            at = (place_x * plan.own_kx + inner) * pad
+            modes_ref[at : at + pad, :] = jnp.where(used, merged, 0.0)
+    right = jnp.concatenate(
+        [modes_ref[pl.ds(plane, plan.width_x, stride=pad), :] for plane in range(plan.planes)],
+        axis=1,
+    )
+    high, low = split(right)
+    both = product(x_ref[...], jnp.concatenate([high, high, low], axis=0))
+    sign = jnp.where(lane_ids(plan.full_x) < HALF, -1.0, 1.0)
+    for plane in range(plan.planes):
+        mine = slice(plane * LANES, (plane + 1) * LANES)
+        turned = roll_lanes(both[plan.full_x :, mine], HALF)
+        rows_ref[pl.ds(plane, plan.full_x, stride=pad), :] = (
+            both[: plan.full_x, mine] + sign * turned
+        )
+    rows_ref[pl.ds(plan.planes, plan.full_x, stride=pad), :] = jnp.zeros(
+        (plan.full_x, LANES), jnp.float32
+    )
+    columns = []
+    for row in range(plan.rows_x):
+        starts = [(place_x * plan.rows_x + row) * pad for place_x in range(plan.size_x)]
+        columns.append(jnp.concatenate([rows_ref[at : at + pad, :] for at in starts], axis=0))
+    high, low = split(jnp.concatenate(columns, axis=1))
+    y_high = y_high_ref[...]
+    along_y = (
+        product(high, y_high, NT) + product(low, y_high, NT) + product(high, y_low_ref[...], NT)
+    )
+    spare = sums_ref[0:1, :]
+    for place_y in range(plan.size_y):
+        for which in range(2):
+            at = (place_y * 2 + which) * LANES
+            out_ref[:, place_y, which] = along_y[:, at : at + LANES].reshape(
+                plan.size_x, pad, LANES
+            )
+    for place_x in range(plan.size_x):
+        for place_y in range(plan.size_y):
+            out_ref[place_x, place_y, 0, plan.planes : plan.planes + 1, :] = spare
+
+
+def widen_map(plan, small, transposed):
+    rows = plan.channels * plan.rows_y
+    row_ids = lax.broadcasted_iota(jnp.int32, (rows, plan.channels), 0)
+    column_ids = lax.broadcasted_iota(jnp.int32, (rows, plan.channels), 1)
+    spread = jnp.where(row_ids // plan.rows_y == column_ids, 1.0, 0.0).astype(jnp.bfloat16)
+    wide = product(spread, small, ((1,), (0,)) if transposed else ((1,), (1,)))
+    wide = product(wide.astype(jnp.bfloat16), spread, NT)
+    return jnp.where(same_cell(plan), wide, 0.0).astype(jnp.bfloat16)
+
+
+def same_cell(plan):
+    rows = plan.channels * plan.rows_y
+    row_ids = lax.broadcasted_iota(jnp.int32, (rows, rows), 0)
+    column_ids = lax.broadcasted_iota(jnp.int32, (rows, rows), 1)
+    return jnp.bitwise_and(row_ids, plan.rows_y - 1) == jnp.bitwise_and(
+        column_ids, plan.rows_y - 1
+    )
+
+
+def synthesize_depth(plan, in_ref, rows_ref, table, channel):
+    rows = take_spectrum(plan, in_ref, rows_ref, channel)
+    high, low = split(rows)
+    return product(jnp.concatenate([high, high, low], axis=0), table, TN)
+
+
+def middle_kernel(
+    plan,
+    in_ref,
+    field_ref,
+    cotangent_ref,
+    map_ref,
+    bias_ref,
+    inverse_ref,
+    forward_ref,
+    output_ref,
+    spectrum_ref,
+    high_ref,
+    low_ref,
+    conv_ref,
+    rows_ref,
+    cross_ref,
+    total_ref,
+):
+    clear_spare(plan, spectrum_ref)
+    block = (plan.rows_x, plan.rows_y, plan.depth)
+    rows = plan.channels * plan.rows_y
+    inverse = inverse_ref[...]
+    for channel in range(plan.channels):
+        conv = synthesize_depth(plan, in_ref, rows_ref, inverse, channel) + bias_ref[channel]
+        conv_ref[channel] = conv.reshape(block)
+    wide = widen_map(plan, map_ref[...], False)
+    cross_ref[...] = jnp.zeros((rows, rows), jnp.float32)
+    total_ref[...] = jnp.zeros((rows, plan.depth), jnp.float32)
+    scale = math.sqrt(2.0 / math.pi)
+    slab = (plan.channels, 1, plan.rows_y, plan.depth)
+
+    def one(row, carry):
+        here = pl.ds(row, 1)
+        values = field_ref[:, here].reshape(rows, plan.depth)
+        preact = conv_ref[:, here].reshape(rows, plan.depth) + product(wide, values)
+        square = preact * preact
+        bend = jnp.tanh(scale * preact * (1.0 + 0.044715 * square))
+        half = 0.5 * (1.0 + bend)
+        output_ref[:, here] = (preact * half).astype(jnp.bfloat16).reshape(slab)
+        slope = half + (0.5 * scale) * preact * (1.0 - bend * bend) * (
+            1.0 + (3.0 * 0.044715) * square
+        )
+        grad = cotangent_ref[:, here].reshape(rows, plan.depth).astype(jnp.float32) * slope
+        high, low = split(grad)
+        high_ref[:, here] = high.reshape(slab)
+        low_ref[:, here] = low.reshape(slab)
+        cross_ref[...] += product(values, high, NT) + product(values, low, NT)
+        total_ref[...] += grad
+        return carry
+
+    lax.fori_loop(0, plan.rows_x, one, 0)
+    forward = forward_ref[...]
+    for channel in range(plan.channels):
+        high = high_ref[channel].reshape(plan.cells, plan.depth)
+        low = low_ref[channel].reshape(plan.cells, plan.depth)
+        both = product(forward, high, NT)
+        more = product(forward[: 2 * MZ], low, NT)
+        put_spectrum(plan, spectrum_ref, channel, both[: 2 * MZ] + both[2 * MZ :] + more)
+    row_ids = lax.broadcasted_iota(jnp.int32, (rows, LANES), 0)
+    gather = jnp.where(row_ids // plan.rows_y == lane_ids(rows), 1.0, 0.0)
+    exact = lax.Precision.HIGHEST
+    cross = jnp.where(same_cell(plan), cross_ref[...], 0.0)
+    by_out = product(cross, gather, precision=exact)
+    sums = product(gather, by_out, TN, precision=exact)
+    ones = jnp.ones((8, plan.depth), jnp.float32)
+    bias_sums = product(
+        product(ones, total_ref[...], NT, precision=exact), gather, precision=exact
+    )
+    for row in range(plan.channels + 1):
+        place_x, place_y = divmod(row, plan.size_y)
+        spare = sums[row : row + 1] if row < plan.channels else bias_sums[0:1]
+        spectrum_ref[place_x, place_y, 0, plan.planes : plan.planes + 1, :] = spare
+
+
+def last_kernel(
+    plan,
+    in_ref,
+    high_ref,
+    low_ref,
+    map_ref,
+    inverse_ref,
+    grad_ref,
+    sums_ref,
+    conv_ref,
+    rows_ref,
+):
+    block = (plan.rows_x, plan.rows_y, plan.depth)
+    rows = plan.channels * plan.rows_y
+    inverse = inverse_ref[...]
+    for channel in range(plan.channels):
+        conv_ref[channel] = synthesize_depth(plan, in_ref, rows_ref, inverse, channel).reshape(
+            block
+        )
+    wide = widen_map(plan, map_ref[...], True)
+    slab = (plan.channels, 1, plan.rows_y, plan.depth)
+
+    def one(row, carry):
+        here = pl.ds(row, 1)
+        high = high_ref[:, here].reshape(rows, plan.depth)
+        low = low_ref[:, here].reshape(rows, plan.depth)
+        total = (
+            conv_ref[:, here].reshape(rows, plan.depth) + product(wide, high) + product(wide, low)
+        )
+        grad_ref[:, here] = total.astype(jnp.bfloat16).reshape(slab)
+        return carry
+
+    lax.fori_loop(0, plan.rows_x, one, 0)
+    sums_ref[...] = jnp.zeros((24, LANES), jnp.float32)
+    shrink = float(plan.full_x * plan.full_y * plan.depth) ** (-0.5)
+    for row in range(plan.channels + 1):
+        place_x, place_y = divmod(row, plan.size_y)
+        sums_ref[row : row + 1, :] = shrink * (
+            in_ref[place_x, place_y, 0, plan.planes : plan.planes + 1, :]
+        )
+
+
+def by_planes(plan, field, cotangent, spectral_weight, pointwise_weight, bias):
+    pad = plan.plane_rows
+    f32 = jnp.float32
+    cell_shape = (plan.size_x, plan.size_y, 2, pad, LANES)
+    mode_shape = (plan.size_x, 4 * pad + 8, LANES)
+    own_shape = (plan.channels, 2, plan.blocks_z, plan.pair_rows)
+    grid_shape = field.shape
+
+    def shape(dims, kind=f32):
+        return jax.ShapeDtypeStruct(dims, kind)
+
+    def cell_exchange(values):
+        flat = values.reshape(plan.devices, 2 * pad, LANES)
+        return lax.all_to_all(flat, ("gx", "gy"), 0, 0, tiled=True).reshape(cell_shape)
+
+    def mode_exchange(values):
+        return lax.all_to_all(values, "gx", 0, 0, tiled=True)
+
+    z_high, z_low = split_table(plan.z_table(False))
+    scaled_high, scaled_low = split_table(plan.z_table(True))
+    z_forward = jnp.asarray(np.concatenate([z_high, z_low]))
+    z_inverse = jnp.asarray(np.concatenate([z_high, z_low, z_high]))
+    scaled_forward = jnp.asarray(np.concatenate([scaled_high, scaled_low]))
+    scaled_inverse = jnp.asarray(np.concatenate([scaled_high, scaled_low, scaled_high]))
+    y_high, y_low = (jnp.asarray(table) for table in split_table(plan.y_table()))
+    x_forward, x_inverse = (jnp.asarray(table) for table in plan.x_tables())
+
+    lane_rows = pltpu.VMEM((plan.full_x * pad, LANES), f32)
+    lane_modes = pltpu.VMEM((plan.width_x * pad, LANES), f32)
+    rest = pltpu.VMEM((2 * pad, LANES), f32)
+    own = pltpu.VMEM(own_shape, f32)
+    grid = pltpu.VMEM(grid_shape, f32)
+    lines = pltpu.VMEM((2 * MZ, LANES), f32)
+    wide = plan.channels * plan.rows_y
+
+    def with_plan(kernel):
+        return functools.partial(kernel, plan)
+
+    def plane_analysis(cells):
+        return call(
+            with_plan(plane_analysis_kernel),
+            [shape(mode_shape), shape((8, LANES))],
+            [lane_rows, lane_modes, rest],
+            cells,
+            y_high,
+            y_low,
+            x_forward,
+        )
+
+    def plane_synthesis(modes, sums):
+        return call(
+            with_plan(plane_synthesis_kernel),
+            shape(cell_shape),
+            [lane_rows, lane_modes, rest],
+            modes,
+            sums,
+            y_high,
+            y_low,
+            x_inverse,
+        )
+
+    with jax.named_scope("depth_analysis"):
+        cells = call(with_plan(depth_analysis_kernel), shape(cell_shape), [], field, z_forward)
+    with jax.named_scope("cells_to_planes"):
+        cells = cell_exchange(cells)
+    with jax.named_scope("plane_analysis"):
+        modes, no_sums = plane_analysis(cells)
+    with jax.named_scope("planes_to_modes"):
+        modes = mode_exchange(modes)
+    with jax.named_scope("mix"):
+        modes, spectrum = call(
+            with_plan(mix_kernel),
+            [shape(mode_shape), shape(own_shape)],
+            [own, rest],
+            modes,
+            spectral_weight,
+        )
+    with jax.named_scope("modes_to_planes"):
+        modes = mode_exchange(modes)
+    with jax.named_scope("plane_synthesis"):
+        cells = plane_synthesis(modes, no_sums)
+    with jax.named_scope("planes_to_cells"):
+        cells = cell_exchange(cells)
+    with jax.named_scope("activation"):
+        output, cells, grad_high, grad_low = call(
+            with_plan(middle_kernel),
+            [
+                shape(grid_shape, jnp.bfloat16),
+                shape(cell_shape),
+                shape(grid_shape, jnp.bfloat16),
+                shape(grid_shape, jnp.bfloat16),
+            ],
+            [grid, lines, pltpu.VMEM((wide, wide), f32), pltpu.VMEM((wide, plan.depth), f32)],
+            cells,
+            field,
+            cotangent,
+            pointwise_weight,
+            bias,
+            scaled_inverse,
+            scaled_forward,
+            smem=(4,),
+        )
+    with jax.named_scope("grad_cells_to_planes"):
+        cells = cell_exchange(cells)
+    with jax.named_scope("grad_plane_analysis"):
+        modes, sums = plane_analysis(cells)
+    with jax.named_scope("grad_planes_to_modes"):
+        modes = mode_exchange(modes)
+    with jax.named_scope("grad_mix"):
+        modes, grad_mix = call(
+            with_plan(mix_back_kernel),
+            [shape(mode_shape), shape(own_shape)],
+            [own, rest],
+            modes,
+            spectral_weight,
+        )
+    with jax.named_scope("grad_modes_to_planes"):
+        modes = mode_exchange(modes)
+    with jax.named_scope("grad_spectral"):
+        grad_spectral = weight_grad(plan, spectrum, grad_mix)
+    with jax.named_scope("grad_plane_synthesis"):
+        cells = plane_synthesis(modes, sums)
+    with jax.named_scope("grad_planes_to_cells"):
+        cells = cell_exchange(cells)
+    with jax.named_scope("grad_field"):
+        grad_field, sums = call(
+            with_plan(last_kernel),
+            [shape(grid_shape, jnp.bfloat16), shape((24, LANES))],
+            [grid, lines],
+            cells,
+            grad_high,
+            grad_low,
+            pointwise_weight,
+            z_inverse,
+        )
+    channels = plan.channels
+    return output, grad_field, grad_spectral, sums[:channels, :channels], sums[channels, :channels]
+
+
+def layer(field, cotangent, spectral_weight, pointwise_weight, bias):
+    plan = Plan(
+        field.shape, spectral_weight.shape, lax.axis_size("gx"), lax.axis_size("gy")
+    )
+    if plan.fits:
+        return by_planes(plan, field, cotangent, spectral_weight, pointwise_weight, bias)
+    return local(field, cotangent, spectral_weight, pointwise_weight, bias)
+
+
 def solution(mesh):
     placed = (
         P(None, "gx", "gy", None),
@@ -178,7 +918,7 @@
         P(),
     )
     return jax.shard_map(
-        local,
+        layer,
         mesh=mesh,
         in_specs=placed,
         out_specs=(

time: 1150 us -> 180 us (0.16)
  waiting for transfers between devices: 607 us -> 4.7 us
  local copies, waits for them, and re-layouts: 284 us -> 26.8 us
  matrix products: 139 us -> 0 us
  blocking collectives: 54.1 us -> 99.3 us
  Pallas kernels: 0 us -> 41.2 us
  other arithmetic: 33.3 us -> 0.01 us
  between operations: 14.7 us -> 0.81 us
    all_gather x4 -> x0, waiting for transfers between devices: 593 us -> none  [the longest x2 331 us: synthesize(): portion = lax.all_gather(spectrum, 'gx', axis=3, tiled=True)]
    dot_general x31 -> x0, matrix products: 139 us -> none  [the longest x2 20.8 us: kx_terms(): jnp.einsum('bcxj,xi->ijbc', values[:, 0], cosine_table, precision=PRECISE)]
    squeeze x14 -> x1, local copies, waits for them, and re-layouts: 95.4 us -> 1.2 us  [by_planes(): sums[channels, :channels]]
    all_to_all x1 -> x6, blocking collectives: 10.9 us -> 99.3 us  [the longest x3 59.5 us: cell_exchange(): lax.all_to_all(flat, ('gx', 'gy'), 0, 0, tiled=True).reshape(cell_shape)]
    slice x3 -> x0, local copies, waits for them, and re-layouts: 46.5 us -> none  [the longest x2 34 us: synthesize(): blocks[1]]
    unnamed x53 -> x46, local copies, waits for them, and re-layouts: 69.2 us -> 25.6 us
    psum x1 -> x0, blocking collectives: 43.2 us -> none  [local(): lax.psum((local_weight, local_bias), ('gx', 'gy'))]
    pallas_call x0 -> x10, Pallas kernels: none -> 41.2 us  [the longest x9 32.4 us: call(): pl.pallas_call(kernel, out_shape=out_shape, in_specs=specs, out_specs=out...]
  transfers between devices with their start and end apart: 7 -> 2, of which waited for: 6 -> 1; matrix products, arithmetic and copies ran while one was open for 5% -> 10% of each run, Pallas kernels for 0% -> 5%
where the time goes in v1:
time: 180 us; the launch traced here: 179 us
  blocking collectives  99.3 us (55%)
  Pallas kernels  41.2 us (23%)
  local copies, waits for them, and re-layouts  26.8 us (15%)
  starting transfers between devices  6.03 us (3%)
  waiting for transfers between devices  4.7 us (3%)
    all_to_all x3, blocking collectives, cell_exchange(): lax.all_to_all(flat, ('gx', 'gy'), 0, 0, tiled=True).reshape(cell_shape)  59.5 us
    all_to_all x3, blocking collectives, mode_exchange(): return lax.all_to_all(values, 'gx', 0, 0, tiled=True)  39.9 us
    pallas_call x9, Pallas kernels, call(): pl.pallas_call(kernel, out_shape=out_shape, in_specs=specs, out_specs=out...  32.4 us
    unnamed x46, local copies, waits for them, and re-layouts  25.6 us
    pallas_call x1, Pallas kernels, weight_grad(): pl.pallas_call(functools.partial(weight_grad_kernel, plan), grid=(plan.ch...  8.79 us
    all_to_all x1, waiting for transfers between devices, mode_exchange(): return lax.all_to_all(values, 'gx', 0, 0, tiled=True)  4.69 us
  transfers between devices with their start and end apart: 2, of which 1 were waited for; matrix products, arithmetic and copies ran while one was open for 10% of the time, Pallas kernels for 5%

profile of v1, /device:TPU:0, one launch (start us, length us, event | category | flops | bytes accessed | tf_op | source)
XLA Modules:
  0.0 178.9 jit_solution(1354340864079247883)
XLA Ops:
  0.6 0.0 copy-start.1
  0.6 0.0 copy-start.4
  0.7 1.5 copy-done.4
  2.1 0.0 copy-start.17
  2.1 0.8 copy-done.17
  2.9 0.0 copy-start.13
  2.9 0.6 depth_analysis.1
  3.5 22.6 %all_to_all.40 = f32[32,32,128]{2,1,0:T(8,128)S(1)} all-to-all(f32[32,32,128]{2,1,0:T(8,128)S(1)} %bitcast.17), channel_id=1, replica_groups=mesh['gx'=8,'gy'=4] {'gx','gy'}, dimensions={0} | all-to-all | bytes 1048576 | tf_op jit(solution)/shard_map/cells_to_planes/all_to_all | solution.py:777
  26.1 0.0 copy-done.1
  26.1 0.0 copy-done.13
  26.1 0.0 copy-start.2
  26.1 1.6 copy-done.2
  27.7 2.4 %plane_analysis.1 = (f32[8,72,128]{2,1,0:T(8,128)}, f32[8,128]{1,0:T(8,128)S(1)}) custom-call(f32[8,4,2,16,128]{4,3,2,1,0:T(8,128)S(1)} %bitcast.15, bf16[1024,1024]{1,0:T(8,128)(2,1)S(1)} %copy-done.1, bf16[1024,1024]{1,0:T(8,128)(2,1)S(1)} %copy-done.2, bf16[96,192]{1,0:T(8,128)(2,1)S(1)} %copy-done.13), custom_call_target="tpu_custom_call" | custom-call | tf_op jit(solution)/shard_map/plane_analysis/pallas_call | solution.py:306
  30.1 3.4 %all-to-all-start.1 = ((f32[8,72,128]{2,1,0:T(8,128)}), f32[8,72,128]{2,1,0:T(8,128)S(1)}, u32[]{:S(2)}, u32[]{:S(2)}) async-start(f32[8,72,128]{2,1,0:T(8,128)} %get-tuple-element.19), calls=%async_computation.1 | async-start | bytes 589824 | tf_op jit(solution)/shard_map/planes_to_modes/all_to_all | solution.py:780
  33.6 5.1 %copy.18.weight_ref = bf16[2,20,20,6,288]{4,3,2,1,0:T(8,128)(2,1)} copy(bf16[2,20,20,6,288]{4,0,3,2,1:T(2,128)(2,1)} %param.15) | data formatting | bytes 5529600 | tf_op args[2]
  38.7 4.7 %all-to-all-done.1.in_ref = f32[8,72,128]{2,1,0:T(8,128)S(1)} async-done(((f32[8,72,128]{2,1,0:T(8,128)}), f32[8,72,128]{2,1,0:T(8,128)S(1)}, u32[]{:S(2)}, u32[]{:S(2)}) %all-to-all-start.1) | async-done | bytes 294944 | tf_op jit(solution)/shard_map/planes_to_modes/all_to_all | solution.py:780
  43.4 0.0 copy-start
  43.4 2.4 %copy-done = bf16[2,20,20,6,288]{4,3,2,1,0:T(8,128)(2,1)S(1)} copy-done((bf16[2,20,20,6,288]{4,3,2,1,0:T(8,128)(2,1)S(1)}, bf16[2,20,20,6,288]{4,3,2,1,0:T(8,128)(2,1)}, u32[]{:S(2)}) %copy-start) | copy-done | bytes 2764824
  45.8 0.0 copy-start.3
  45.8 0.0 copy-start.12
  45.8 2.7 %mix.1 = (f32[8,72,128]{2,1,0:T(8,128)S(1)}, f32[20,2,6,288]{3,2,1,0:T(8,128)S(1)}) custom-call(f32[8,72,128]{2,1,0:T(8,128)S(1)} %all-to-all-done.1.in_ref, bf16[2,20,20,6,288]{4,3,2,1,0:T(8,128)(2,1)S(1)} %copy-done), custom_call_target="tpu_custom_call" | custom-call | tf_op jit(solution)/shard_map/mix/pallas_call | solution.py:306
  48.5 0.0 copy-start.8
  48.5 13.7 %all_to_all.41.in_ref = f32[8,72,128]{2,1,0:T(8,128)S(1)} all-to-all(f32[8,72,128]{2,1,0:T(8,128)S(1)} %get-tuple-element.20), channel_id=1, replica_groups=mesh['gx'=8,'gy'=4] {'gx'}, dimensions={0} | all-to-all | bytes 589824 | tf_op jit(solution)/shard_map/modes_to_planes/all_to_all | solution.py:780
  62.3 0.0 copy-done.3
  62.3 0.0 copy-done.12
  62.3 0.0 copy-start.5
  62.3 0.0 copy-start.15
  62.3 0.0 copy-start.16
  62.3 0.0 copy-start.18
  62.3 0.0 copy-start.19
  62.3 0.0 slice-start
  62.3 2.9 %plane_synthesis.1 = f32[8,4,2,16,128]{4,3,2,1,0:T(8,128)S(1)} custom-call(f32[8,72,128]{2,1,0:T(8,128)S(1)} %all_to_all.41.in_ref, f32[8,128]{1,0:T(8,128)S(1)} %get-tuple-element.21.sums_ref, bf16[1024,1024]{1,0:T(8,128)(2,1)S(1)} %copy-done.1, bf16[1024,1024]{1,0:T(8,128)(2,1)S(1)} %copy-done.3, bf16[128,144]{1,0:T(8,128)(2,1)S(1)} %copy-done.12), custom_call_target="tpu_custom_call" | custom-call | tf_op jit(solution)/shard_map/plane_synthesis/pallas_call | solution.py:306
  65.2 0.0 copy-done.8
  65.2 18.4 %all_to_all.42 = f32[32,32,128]{2,1,0:T(8,128)S(1)} all-to-all(f32[32,32,128]{2,1,0:T(8,128)S(1)} %bitcast.16), channel_id=1, replica_groups=mesh['gx'=8,'gy'=4] {'gx','gy'}, dimensions={0} | all-to-all | bytes 1048576 | tf_op jit(solution)/shard_map/planes_to_cells/all_to_all | solution.py:777
  83.6 0.0 copy-done.5
  83.6 0.0 copy-done.15
  83.6 0.0 copy-done.16
  83.6 0.0 copy-done.18
  83.6 0.0 copy-done.19
  83.6 0.0 slice-start.1
  83.6 11.3 %activation.1 = (bf16[20,8,16,256]{3,2,1,0:T(8,128)(2,1)}, f32[8,4,2,16,128]{4,3,2,1,0:T(8,128)S(1)}, bf16[20,8,16,256]{3,2,1,0:T(8,128)(2,1)S(1)}, bf16[20,8,16,256]{3,2,1,0:T(8,128)(2,1)S(1)}) custom-call(f32[8,4,2,16,128]{4,3,2,1,0:T(8,128)S(1)} %bitcast.13, bf16[20,8,16,256]{3,2,1,0:T(8,128)(2,1)S(1)} %copy-done.5, ...), custom_call_target="tpu_custom_call" | custom-call | tf_op jit(solution)/shard_map/activation/pallas_call | solution.py:306
  94.9 0.0 copy-start.6
  94.9 18.4 %all_to_all.43 = f32[32,32,128]{2,1,0:T(8,128)S(1)} all-to-all(f32[32,32,128]{2,1,0:T(8,128)S(1)} %bitcast.19), channel_id=1, replica_groups=mesh['gx'=8,'gy'=4] {'gx','gy'}, dimensions={0} | all-to-all | bytes 1048576 | tf_op jit(solution)/shard_map/grad_cells_to_planes/all_to_all | solution.py:777
  113.4 1.7 grad_plane_analysis.1
  115.1 0.0 copy-done.6
  115.1 13.3 %all_to_all.44.in_ref = f32[8,72,128]{2,1,0:T(8,128)S(1)} all-to-all(f32[8,72,128]{2,1,0:T(8,128)S(1)} %get-tuple-element.24), channel_id=1, replica_groups=mesh['gx'=8,'gy'=4] {'gx'}, dimensions={0} | all-to-all | bytes 589824 | tf_op jit(solution)/shard_map/grad_planes_to_modes/all_to_all | solution.py:780
  128.4 0.0 slice-done
  128.4 0.0 slice-done.1
  128.4 2.7 %grad_mix.1 = (f32[8,72,128]{2,1,0:T(8,128)S(1)}, f32[20,2,6,288]{3,2,1,0:T(8,128)S(1)}) custom-call(f32[8,72,128]{2,1,0:T(8,128)S(1)} %all_to_all.44.in_ref, bf16[2,20,20,6,288]{4,3,2,1,0:T(8,128)(2,1)S(1)} %bitcast.12), custom_call_target="tpu_custom_call" | custom-call | tf_op jit(solution)/shard_map/grad_mix/pallas_call | solution.py:306
  131.1 0.0 copy-start.10
  131.1 12.9 %all_to_all.45.in_ref = f32[8,72,128]{2,1,0:T(8,128)S(1)} all-to-all(f32[8,72,128]{2,1,0:T(8,128)S(1)} %get-tuple-element.25), channel_id=1, replica_groups=mesh['gx'=8,'gy'=4] {'gx'}, dimensions={0} | all-to-all | bytes 589824 | tf_op jit(solution)/shard_map/grad_modes_to_planes/all_to_all | solution.py:780
  143.9 3.7 %grad_plane_synthesis.1 = f32[8,4,2,16,128]{4,3,2,1,0:T(8,128)} custom-call(f32[8,72,128]{2,1,0:T(8,128)S(1)} %all_to_all.45.in_ref, f32[8,128]{1,0:T(8,128)S(1)} %get-tuple-element.26.sums_ref, bf16[1024,1024]{1,0:T(8,128)(2,1)S(1)} %copy-done.1, bf16[1024,1024]{1,0:T(8,128)(2,1)S(1)} %copy-done.3, bf16[128,144]{1,0:T(8,128)(2,1)S(1)} %copy-done.12), custom_call_target="tpu_custom_call" | custom-call | tf_op jit(solution)/shard_map/grad_plane_synthesis/pallas_call | solution.py:306
  147.6 0.0 copy-done.10
  147.6 2.6 %all-to-all-start.7 = ((f32[32,32,128]{2,1,0:T(8,128)}), f32[32,32,128]{2,1,0:T(8,128)S(1)}, u32[]{:S(2)}, u32[]{:S(2)}) async-start(f32[32,32,128]{2,1,0:T(8,128)} %bitcast.6), calls=%async_computation.7 | async-start | bytes 1048576 | tf_op jit(solution)/shard_map/grad_planes_to_cells/all_to_all | solution.py:777
  150.2 0.0 copy-start.9
  150.2 1.0 copy-done.9
  151.3 1.0 copy-done.11
  152.3 8.8 %grad_spectral.1 = f32[2,20,20,6,288]{4,3,2,1,0:T(8,128)} custom-call(f32[20,2,6,288]{3,2,1,0:T(8,128)S(1)} %copy-done.9, f32[20,2,6,288]{3,2,1,0:T(8,128)S(1)} %copy-done.11), custom_call_target="tpu_custom_call" | custom-call | tf_op jit(solution)/shard_map/grad_spectral/pallas_call | solution.py:540
  161.1 12.1 %copy.20 = f32[2,20,20,6,288]{4,0,3,2,1:T(2,128)} copy(f32[2,20,20,6,288]{4,3,2,1,0:T(8,128)} %grad_spectral.1) | data formatting | bytes 11059200
  173.2 0.0 all-to-all-done.7
  173.2 0.0 copy-done.7
  173.2 0.0 copy-done.14
  173.2 4.5 %grad_field.1 = (bf16[20,8,16,256]{3,2,1,0:T(8,128)(2,1)}, f32[24,128]{1,0:T(8,128)}) custom-call(f32[8,4,2,16,128]{4,3,2,1,0:T(8,128)S(1)} %bitcast.18, bf16[20,8,16,256]{3,2,1,0:T(8,128)(2,1)S(1)} %get-tuple-element.27.high_ref, bf16[20,8,16,256]{3,2,1,0:T(8,128)(2,1)S(1)} %copy-done.7, bf16[20,20]{1,0:T(8,128)(2,1)S(1)} %copy-done.18, ...), custom_call_target="tpu_custom_call" | custom-call | tf_op jit(solution)/shard_map/grad_field/pallas_call | solution.py:306
  177.7 1.2 slice_bitcast_fusion
  (4 shorter events, 0.0 us)
Async XLA Ops:
  0.6 25.5 %copy-start.1 = (bf16[1024,1024]{1,0:T(8,128)(2,1)S(1)}, bf16[1024,1024]{1,0:T(8,128)(2,1)}, u32[]{:S(2)}) copy-start(bf16[1024,1024]{1,0:T(8,128)(2,1)} %constant.20.clone.y_high_ref) | copy-start | bytes 6291460
  0.6 1.5 copy-start.4
  2.1 0.8 copy-start.17
  2.9 23.2 %copy-start.13 = (bf16[96,192]{1,0:T(8,128)(2,1)S(1)}, bf16[96,192]{1,0:T(8,128)(2,1)}, u32[]{:S(2)}) copy-start(bf16[96,192]{1,0:T(8,128)(2,1)} %constant.22.clone.x_ref) | copy-start | bytes 110596
  26.1 1.6 copy-start.2
  30.1 13.3 %all-to-all-start.1 = ((f32[8,72,128]{2,1,0:T(8,128)}), f32[8,72,128]{2,1,0:T(8,128)S(1)}, u32[]{:S(2)}, u32[]{:S(2)}) async-start(f32[8,72,128]{2,1,0:T(8,128)} %get-tuple-element.19), calls=%async_computation.1 | async-start | bytes 589824 | tf_op jit(solution)/shard_map/planes_to_modes/all_to_all | solution.py:780
  43.4 2.4 %copy-start = (bf16[2,20,20,6,288]{4,3,2,1,0:T(8,128)(2,1)S(1)}, bf16[2,20,20,6,288]{4,3,2,1,0:T(8,128)(2,1)}, u32[]{:S(2)}) copy-start(bf16[2,20,20,6,288]{4,3,2,1,0:T(8,128)(2,1)} %copy.18.weight_ref) | copy-start | bytes 8294404
  45.8 16.5 %copy-start.3 = (bf16[1024,1024]{1,0:T(8,128)(2,1)S(1)}, bf16[1024,1024]{1,0:T(8,128)(2,1)}, u32[]{:S(2)}) copy-start(bf16[1024,1024]{1,0:T(8,128)(2,1)} %constant.21.clone.y_low_ref) | copy-start | bytes 6291460
  45.8 16.5 %copy-start.12 = (bf16[128,144]{1,0:T(8,128)(2,1)S(1)}, bf16[128,144]{1,0:T(8,128)(2,1)}, u32[]{:S(2)}) copy-start(bf16[128,144]{1,0:T(8,128)(2,1)} %constant.23.clone.x_ref) | copy-start | bytes 110596
  48.5 16.7 %copy-start.8 = (f32[20,2,6,288]{3,2,1,0:T(8,128)}, f32[20,2,6,288]{3,2,1,0:T(8,128)S(1)}, u32[]{:S(2)}) copy-start(f32[20,2,6,288]{3,2,1,0:T(8,128)S(1)} %get-tuple-element.30.spectrum_ref) | copy-start | bytes 829444
  62.3 21.3 %copy-start.5 = (bf16[20,8,16,256]{3,2,1,0:T(8,128)(2,1)S(1)}, bf16[20,8,16,256]{3,2,1,0:T(8,128)(2,1)}, u32[]{:S(2)}) copy-start(bf16[20,8,16,256]{3,2,1,0:T(8,128)(2,1)} %field_ref.3) | copy-start | bytes 3932164
  62.3 21.3 %copy-start.15 = (bf16[144,256]{1,0:T(8,128)(2,1)S(1)}, bf16[144,256]{1,0:T(8,128)(2,1)}, u32[]{:S(2)}) copy-start(bf16[144,256]{1,0:T(8,128)(2,1)} %constant.19.clone.inverse_ref) | copy-start | bytes 221188
  62.3 21.3 %copy-start.16 = (bf16[96,256]{1,0:T(8,128)(2,1)S(1)}, bf16[96,256]{1,0:T(8,128)(2,1)}, u32[]{:S(2)}) copy-start(bf16[96,256]{1,0:T(8,128)(2,1)} %constant.18.clone.forward_ref) | copy-start | bytes 147460
  62.3 21.3 %copy-start.18 = (bf16[20,20]{1,0:T(8,128)(2,1)S(1)}, bf16[20,20]{1,0:T(8,128)(2,1)}, u32[]{:S(2)}) copy-start(bf16[20,20]{1,0:T(8,128)(2,1)} %map_ref.3) | copy-start | bytes 2404
  62.3 21.3 %copy-start.19 = (f32[20]{0:T(128)S(1)}, f32[20]{0:T(128)}, u32[]{:S(2)}) copy-start(f32[20]{0:T(128)} %bias_ref.1) | copy-start | bytes 244
  62.3 66.1 %slice-start = ((s8[4915200]{0:T(1024)(128)(4,1)}), s8[4194304]{0:T(1024)(128)(4,1)S(1)}, s32[]{:S(2)}) async-start(s8[4915200]{0:T(1024)(128)(4,1)} %bitcast.11), calls=%async_computation.8 | async-start | bytes 8388608
  83.6 44.8 %slice-start.1 = ((s8[4915200]{0:T(1024)(128)(4,1)}), s8[720896]{0:T(1024)(128)(4,1)S(1)}, s32[]{:S(2)}) async-start(s8[4915200]{0:T(1024)(128)(4,1)} %bitcast.11), calls=%async_computation.9 | async-start | bytes 1441792
  94.9 20.1 %copy-start.6 = (bf16[20,8,16,256]{3,2,1,0:T(8,128)(2,1)}, bf16[20,8,16,256]{3,2,1,0:T(8,128)(2,1)S(1)}, u32[]{:S(2)}) copy-start(bf16[20,8,16,256]{3,2,1,0:T(8,128)(2,1)S(1)} %get-tuple-element.28.low_ref) | copy-start | bytes 3932164
  131.1 16.5 %copy-start.10 = (f32[20,2,6,288]{3,2,1,0:T(8,128)}, f32[20,2,6,288]{3,2,1,0:T(8,128)S(1)}, u32[]{:S(2)}) copy-start(f32[20,2,6,288]{3,2,1,0:T(8,128)S(1)} %get-tuple-element.31.grad_ref) | copy-start | bytes 829444
  147.6 25.6 %all-to-all-start.7 = ((f32[32,32,128]{2,1,0:T(8,128)}), f32[32,32,128]{2,1,0:T(8,128)S(1)}, u32[]{:S(2)}, u32[]{:S(2)}) async-start(f32[32,32,128]{2,1,0:T(8,128)} %bitcast.6), calls=%async_computation.7 | async-start | bytes 1048576 | tf_op jit(solution)/shard_map/grad_planes_to_cells/all_to_all | solution.py:777
  150.2 1.0 copy-start.9
  151.3 1.0 copy-start.11
  161.1 12.1 %copy-start.7 = (bf16[20,8,16,256]{3,2,1,0:T(8,128)(2,1)S(1)}, bf16[20,8,16,256]{3,2,1,0:T(8,128)(2,1)}, u32[]{:S(2)}) copy-start(bf16[20,8,16,256]{3,2,1,0:T(8,128)(2,1)} %copy-done.6) | copy-start | bytes 3932164
  161.1 12.1 %copy-start.14 = (bf16[144,256]{1,0:T(8,128)(2,1)S(1)}, bf16[144,256]{1,0:T(8,128)(2,1)}, u32[]{:S(2)}) copy-start(bf16[144,256]{1,0:T(8,128)(2,1)} %constant.17.clone.inverse_ref) | copy-start | bytes 221188

commit v2 on v1

--- a/solution.py
+++ b/solution.py
@@ -6,6 +6,7 @@
 from jax import lax
 import numpy as np
 from jax.experimental import pallas as pl
+from jax.experimental.layout import Layout, with_layout_constraint
 from jax.experimental.pallas import tpu as pltpu
 from jax.sharding import PartitionSpec as P
 
@@ -175,7 +176,8 @@
 
 LANES = 128
 HALF = 64
-VMEM_BYTES = 48 * 1024 * 1024
+SLOT = 32
+VMEM_BYTES = 40 * 1024 * 1024
 
 
 def split_table(table):
@@ -249,12 +251,15 @@
         self.fits = (
             self.cells == LANES
             and self.rows_y == 16
+            and self.size_y * 2 == self.rows_x
             and self.depth % LANES == 0
             and self.planes < self.plane_rows
             and self.pair_rows % self.width_y == 0
             and self.pair_rows == 2 * LANES + 32
             and self.width_y <= HALF
-            and self.channels + 1 <= min(self.devices, 24)
+            and size_x == 8
+            and self.channels <= SLOT
+            and self.channels < size_x * (LANES // SLOT)
             and self.own_z * 2 * self.part_z * size_y == 2 * MZ
         )
 
@@ -268,7 +273,7 @@
         both = both.reshape(2, self.depth, self.size_y, self.part_z, self.own_z)
         return both.transpose(2, 3, 0, 4, 1).reshape(2 * MZ, self.depth)
 
-    def y_table(self):
+    def y_tables(self):
         freq = frequency_table(MY, self.full_y)
         phases = phase_table(freq, np.arange(self.full_y), self.full_y)
         cosine, sine = np.cos(phases), np.sin(phases)
@@ -278,14 +283,20 @@
         one[:, 1, :, 0, : self.width_y] = sine.reshape(by_block)
         one[:, 0, :, 1, : self.width_y] = -sine.reshape(by_block)
         one[:, 1, :, 1, : self.width_y] = cosine.reshape(by_block)
-        full = np.zeros((self.size_y, 2, self.rows_x, self.rows_y, self.rows_x, LANES))
-        for row in range(self.rows_x):
-            full[:, :, row, :, row, :] = one.reshape(self.size_y, 2, self.rows_y, LANES)
-        return full.reshape(self.size_y * 2 * LANES, self.rows_x * LANES)
+        one = one.reshape(LANES, LANES)
+        tables = []
+        for table in (one, one.T):
+            high, low = split_table(table)
+            top = np.concatenate([high, low], axis=1)
+            bottom = np.concatenate([high, np.zeros_like(low)], axis=1)
+            tables.append(np.concatenate([top, bottom], axis=0))
+        return tables
 
     def x_tables(self):
         freq = frequency_table(MX, self.full_x)
         phases = phase_table(freq, np.arange(self.full_x), self.full_x)
+        phases = phases.reshape(self.size_x, self.rows_x, self.width_x).transpose(1, 0, 2)
+        phases = phases.reshape(self.full_x, self.width_x)
         cosine, sine = np.cos(phases), np.sin(phases)
         forward = np.concatenate([cosine.T, sine.T], axis=0)
         inverse = np.concatenate([cosine, sine], axis=0)
@@ -360,32 +371,40 @@
         put_spectrum(plan, out_ref, channel, both[: 2 * MZ] + both[2 * MZ :])
 
 
+def swap_blocks(values, block):
+    values = list(values)
+    lanes = lane_ids(values[0].shape[0])
+    step = 1
+    while step < len(values):
+        low = jnp.bitwise_and(lanes, step * block) == 0
+        for at in range(len(values)):
+            if at & step:
+                continue
+            first, second = values[at], values[at + step]
+            values[at] = jnp.where(low, first, roll_lanes(second, step * block))
+            values[at + step] = jnp.where(low, roll_lanes(first, -step * block), second)
+        step *= 2
+    return values
+
+
+def along_y(values, table):
+    high, low = split(values)
+    both = product(jnp.concatenate([high, low], axis=1), table)
+    return both[:, :LANES] + both[:, LANES:]
+
+
 def plane_analysis_kernel(
-    plan, in_ref, y_high_ref, y_low_ref, x_ref, out_ref, sums_ref, rows_ref, modes_ref, rest_ref
+    plan, in_ref, extra_ref, y_ref, x_ref, out_ref, rows_ref, modes_ref, rest_ref
 ):
     pad = plan.plane_rows
-    spare = jnp.zeros((1, LANES), jnp.float32)
-    for place_x in range(plan.size_x):
-        for place_y in range(plan.size_y):
-            spare = spare + in_ref[place_x, place_y, 0, plan.planes : plan.planes + 1, :]
-    sums_ref[...] = jnp.broadcast_to(spare, (8, LANES))
-    left = jnp.concatenate(
-        [
-            in_ref[:, place_y, which].reshape(plan.size_x * pad, LANES)
-            for place_y in range(plan.size_y)
-            for which in range(2)
-        ],
-        axis=1,
-    )
-    high, low = split(left)
-    y_high = y_high_ref[...]
-    along_y = product(high, y_high) + product(low, y_high) + product(high, y_low_ref[...])
-    for place_x in range(plan.size_x):
-        for row in range(plan.rows_x):
-            at = (place_x * plan.rows_x + row) * pad
-            rows_ref[at : at + pad, :] = along_y[
-                place_x * pad : (place_x + 1) * pad, row * LANES : (row + 1) * LANES
-            ]
+    left = [
+        in_ref[:, place_y, which].reshape(plan.size_x * pad, LANES)
+        for place_y in range(plan.size_y)
+        for which in range(2)
+    ]
+    rows_ref[...] = along_y(
+        jnp.concatenate(swap_blocks(left, plan.rows_y), axis=0), y_ref[...]
+    )
     right = jnp.concatenate(
         [rows_ref[pl.ds(plane, plan.full_x, stride=pad), :] for plane in range(plan.planes)], axis=1
     )
@@ -424,6 +443,7 @@
                 out_ref[place_x, row : row + pad, :] = tiles[at]
             rest_ref[which * pad : (which + 1) * pad, :] = tiles[2]
         out_ref[place_x, 4 * pad : 4 * pad + 8, :] = pack_rest(rest_ref)
+        out_ref[place_x, plan.planes : plan.planes + 1, :] = extra_ref[place_x : place_x + 1, :]
 
 
 def pack_rest(rest_ref):
@@ -503,7 +523,11 @@
     put_modes(plan, mixed_ref, out_ref, rest_ref)
 
 
-def mix_back_kernel(plan, in_ref, weight_ref, out_ref, grad_ref, mixed_ref, rest_ref):
+def mix_back_kernel(plan, in_ref, weight_ref, out_ref, grad_ref, sums_ref, mixed_ref, rest_ref):
+    spare = jnp.zeros((1, LANES), jnp.float32)
+    for place_x in range(plan.size_x):
+        spare = spare + in_ref[place_x, plan.planes : plan.planes + 1, :]
+    sums_ref[...] = jnp.broadcast_to(spare, (8, LANES))
     take_modes(plan, in_ref, grad_ref, rest_ref)
     shape = (plan.blocks_z, plan.pair_rows)
 
@@ -553,7 +577,7 @@
 
 
 def plane_synthesis_kernel(
-    plan, in_ref, sums_ref, y_high_ref, y_low_ref, x_ref, out_ref, rows_ref, modes_ref, rest_ref
+    plan, in_ref, extra_ref, y_ref, x_ref, out_ref, rows_ref, modes_ref, rest_ref
 ):
     pad, width = plan.plane_rows, plan.width_y
     lanes = lane_ids(pad)
@@ -599,22 +623,17 @@
     rows_ref[pl.ds(plan.planes, plan.full_x, stride=pad), :] = jnp.zeros(
         (plan.full_x, LANES), jnp.float32
     )
-    columns = []
-    for row in range(plan.rows_x):
-        starts = [(place_x * plan.rows_x + row) * pad for place_x in range(plan.size_x)]
-        columns.append(jnp.concatenate([rows_ref[at : at + pad, :] for at in starts], axis=0))
-    high, low = split(jnp.concatenate(columns, axis=1))
-    y_high = y_high_ref[...]
-    along_y = (
-        product(high, y_high, NT) + product(low, y_high, NT) + product(high, y_low_ref[...], NT)
-    )
-    spare = sums_ref[0:1, :]
+    cells = along_y(rows_ref[...], y_ref[...])
+    size = plan.size_x * pad
+    cells = swap_blocks(
+        [cells[row * size : (row + 1) * size] for row in range(plan.rows_x)], plan.rows_y
+    )
     for place_y in range(plan.size_y):
         for which in range(2):
-            at = (place_y * 2 + which) * LANES
-            out_ref[:, place_y, which] = along_y[:, at : at + LANES].reshape(
+            out_ref[:, place_y, which] = cells[place_y * 2 + which].reshape(
                 plan.size_x, pad, LANES
             )
+    spare = extra_ref[0:1, :]
     for place_x in range(plan.size_x):
         for place_y in range(plan.size_y):
             out_ref[place_x, place_y, 0, plan.planes : plan.planes + 1, :] = spare
@@ -645,120 +664,122 @@
     return product(jnp.concatenate([high, high, low], axis=0), table, TN)
 
 
-def middle_kernel(
+def pointwise_kernel(plan, field_ref, map_ref, bias_ref, out_ref):
+    rows, size = plan.channels * plan.rows_y, plan.rows_y
+    wide = widen_map(plan, map_ref[...], False)
+
+    def one(row, carry):
+        here = pl.ds(row, 1)
+        mapped = product(wide, field_ref[:, here].reshape(rows, plan.depth))
+        for channel in range(plan.channels):
+            part = mapped[channel * size : (channel + 1) * size] + bias_ref[channel]
+            out_ref[channel, here] = part.reshape(1, size, plan.depth)
+        return carry
+
+    lax.fori_loop(0, plan.rows_x, one, 0)
+
+
+def activation_kernel(
     plan,
     in_ref,
-    field_ref,
+    pointwise_ref,
     cotangent_ref,
-    map_ref,
-    bias_ref,
     inverse_ref,
     forward_ref,
     output_ref,
     spectrum_ref,
     high_ref,
     low_ref,
-    conv_ref,
     rows_ref,
-    cross_ref,
-    total_ref,
 ):
     clear_spare(plan, spectrum_ref)
+    flat = (plan.cells, plan.depth)
     block = (plan.rows_x, plan.rows_y, plan.depth)
+    inverse = inverse_ref[...]
+    forward = forward_ref[...]
+    scale = math.sqrt(2.0 / math.pi)
+    for channel in range(plan.channels):
+        preact = synthesize_depth(plan, in_ref, rows_ref, inverse, channel)
+        preact = preact + pointwise_ref[channel].reshape(flat)
+        square = preact * preact
+        bend = jnp.tanh(scale * preact * (1.0 + 0.044715 * square))
+        half = 0.5 * (1.0 + bend)
+        output_ref[channel] = (preact * half).astype(jnp.bfloat16).reshape(block)
+        slope = half + (0.5 * scale) * preact * (1.0 - bend * bend) * (
+            1.0 + (3.0 * 0.044715) * square
+        )
+        grad = cotangent_ref[channel].reshape(flat).astype(jnp.float32) * slope
+        high, low = split(grad)
+        high_ref[channel] = high.reshape(block)
+        low_ref[channel] = low.reshape(block)
+        both = product(forward, high, NT)
+        more = product(forward[: 2 * MZ], low, NT)
+        put_spectrum(plan, spectrum_ref, channel, both[: 2 * MZ] + both[2 * MZ :] + more)
+
+
+def pointwise_grad_kernel(
+    plan, field_ref, high_ref, low_ref, map_ref, back_ref, sums_ref, cross_ref
+):
     rows = plan.channels * plan.rows_y
-    inverse = inverse_ref[...]
-    for channel in range(plan.channels):
-        conv = synthesize_depth(plan, in_ref, rows_ref, inverse, channel) + bias_ref[channel]
-        conv_ref[channel] = conv.reshape(block)
-    wide = widen_map(plan, map_ref[...], False)
-    cross_ref[...] = jnp.zeros((rows, rows), jnp.float32)
-    total_ref[...] = jnp.zeros((rows, plan.depth), jnp.float32)
-    scale = math.sqrt(2.0 / math.pi)
+    wide = widen_map(plan, map_ref[...], True)
+    cross_ref[...] = jnp.zeros((rows + 16, rows), jnp.float32)
+    ones = jnp.ones((16, plan.depth), jnp.bfloat16)
     slab = (plan.channels, 1, plan.rows_y, plan.depth)
 
     def one(row, carry):
         here = pl.ds(row, 1)
         values = field_ref[:, here].reshape(rows, plan.depth)
-        preact = conv_ref[:, here].reshape(rows, plan.depth) + product(wide, values)
-        square = preact * preact
-        bend = jnp.tanh(scale * preact * (1.0 + 0.044715 * square))
-        half = 0.5 * (1.0 + bend)
-        output_ref[:, here] = (preact * half).astype(jnp.bfloat16).reshape(slab)
-        slope = half + (0.5 * scale) * preact * (1.0 - bend * bend) * (
-            1.0 + (3.0 * 0.044715) * square
-        )
-        grad = cotangent_ref[:, here].reshape(rows, plan.depth).astype(jnp.float32) * slope
-        high, low = split(grad)
-        high_ref[:, here] = high.reshape(slab)
-        low_ref[:, here] = low.reshape(slab)
+        values = jnp.concatenate([values, ones], axis=0)
+        high = high_ref[:, here].reshape(rows, plan.depth)
+        low = low_ref[:, here].reshape(rows, plan.depth)
+        back_ref[:, here] = (product(wide, high) + product(wide, low)).reshape(slab)
         cross_ref[...] += product(values, high, NT) + product(values, low, NT)
-        total_ref[...] += grad
         return carry
 
     lax.fori_loop(0, plan.rows_x, one, 0)
-    forward = forward_ref[...]
-    for channel in range(plan.channels):
-        high = high_ref[channel].reshape(plan.cells, plan.depth)
-        low = low_ref[channel].reshape(plan.cells, plan.depth)
-        both = product(forward, high, NT)
-        more = product(forward[: 2 * MZ], low, NT)
-        put_spectrum(plan, spectrum_ref, channel, both[: 2 * MZ] + both[2 * MZ :] + more)
     row_ids = lax.broadcasted_iota(jnp.int32, (rows, LANES), 0)
     gather = jnp.where(row_ids // plan.rows_y == lane_ids(rows), 1.0, 0.0)
     exact = lax.Precision.HIGHEST
-    cross = jnp.where(same_cell(plan), cross_ref[...], 0.0)
+    cross = jnp.where(same_cell(plan), cross_ref[:rows], 0.0)
     by_out = product(cross, gather, precision=exact)
     sums = product(gather, by_out, TN, precision=exact)
-    ones = jnp.ones((8, plan.depth), jnp.float32)
-    bias_sums = product(
-        product(ones, total_ref[...], NT, precision=exact), gather, precision=exact
-    )
-    for row in range(plan.channels + 1):
-        place_x, place_y = divmod(row, plan.size_y)
-        spare = sums[row : row + 1] if row < plan.channels else bias_sums[0:1]
-        spectrum_ref[place_x, place_y, 0, plan.planes : plan.planes + 1, :] = spare
+    bias_sums = product(cross_ref[rows : rows + 8], gather, precision=exact)
+    lanes = lane_ids(1)
+    per_row = LANES // SLOT
+    for at in range(8):
+        packed = jnp.zeros((1, LANES), jnp.float32)
+        for slot in range(per_row):
+            row = at * per_row + slot
+            if row > plan.channels:
+                continue
+            line = sums[row : row + 1] if row < plan.channels else bias_sums[0:1]
+            packed = jnp.where(lanes // SLOT == slot, roll_lanes(line, slot * SLOT), packed)
+        sums_ref[at : at + 1, :] = packed
 
 
 def last_kernel(
-    plan,
-    in_ref,
-    high_ref,
-    low_ref,
-    map_ref,
-    inverse_ref,
-    grad_ref,
-    sums_ref,
-    conv_ref,
-    rows_ref,
+    plan, in_ref, back_ref, inverse_ref, grad_ref, map_grad_ref, bias_grad_ref, rows_ref
 ):
     block = (plan.rows_x, plan.rows_y, plan.depth)
-    rows = plan.channels * plan.rows_y
+    flat = (plan.cells, plan.depth)
     inverse = inverse_ref[...]
     for channel in range(plan.channels):
-        conv_ref[channel] = synthesize_depth(plan, in_ref, rows_ref, inverse, channel).reshape(
-            block
-        )
-    wide = widen_map(plan, map_ref[...], True)
-    slab = (plan.channels, 1, plan.rows_y, plan.depth)
-
-    def one(row, carry):
-        here = pl.ds(row, 1)
-        high = high_ref[:, here].reshape(rows, plan.depth)
-        low = low_ref[:, here].reshape(rows, plan.depth)
-        total = (
-            conv_ref[:, here].reshape(rows, plan.depth) + product(wide, high) + product(wide, low)
-        )
-        grad_ref[:, here] = total.astype(jnp.bfloat16).reshape(slab)
-        return carry
-
-    lax.fori_loop(0, plan.rows_x, one, 0)
-    sums_ref[...] = jnp.zeros((24, LANES), jnp.float32)
+        total = synthesize_depth(plan, in_ref, rows_ref, inverse, channel)
+        total = total + back_ref[channel].reshape(flat)
+        grad_ref[channel] = total.astype(jnp.bfloat16).reshape(block)
     shrink = float(plan.full_x * plan.full_y * plan.depth) ** (-0.5)
-    for row in range(plan.channels + 1):
-        place_x, place_y = divmod(row, plan.size_y)
-        sums_ref[row : row + 1, :] = shrink * (
-            in_ref[place_x, place_y, 0, plan.planes : plan.planes + 1, :]
-        )
+    per_row = LANES // SLOT
+    for at in range(plan.size_x):
+        line = jnp.zeros((1, LANES), jnp.float32)
+        for place_y in range(plan.size_y):
+            line = line + in_ref[at, place_y, 0, plan.planes : plan.planes + 1, :]
+        for slot in range(per_row):
+            row = at * per_row + slot
+            mine = shrink * roll_lanes(line, -slot * SLOT)[:, : plan.channels]
+            if row < plan.channels:
+                map_grad_ref[row : row + 1, :] = mine
+            elif row == plan.channels:
+                bias_grad_ref[...] = mine
 
 
 def by_planes(plan, field, cotangent, spectral_weight, pointwise_weight, bias):
@@ -785,49 +806,61 @@
     z_inverse = jnp.asarray(np.concatenate([z_high, z_low, z_high]))
     scaled_forward = jnp.asarray(np.concatenate([scaled_high, scaled_low]))
     scaled_inverse = jnp.asarray(np.concatenate([scaled_high, scaled_low, scaled_high]))
-    y_high, y_low = (jnp.asarray(table) for table in split_table(plan.y_table()))
+    y_forward, y_inverse = (jnp.asarray(table) for table in plan.y_tables())
     x_forward, x_inverse = (jnp.asarray(table) for table in plan.x_tables())
 
     lane_rows = pltpu.VMEM((plan.full_x * pad, LANES), f32)
     lane_modes = pltpu.VMEM((plan.width_x * pad, LANES), f32)
     rest = pltpu.VMEM((2 * pad, LANES), f32)
     own = pltpu.VMEM(own_shape, f32)
-    grid = pltpu.VMEM(grid_shape, f32)
     lines = pltpu.VMEM((2 * MZ, LANES), f32)
     wide = plan.channels * plan.rows_y
+    row_shape = shape((8, LANES))
 
     def with_plan(kernel):
         return functools.partial(kernel, plan)
 
-    def plane_analysis(cells):
+    def plane_analysis(cells, extra):
         return call(
             with_plan(plane_analysis_kernel),
-            [shape(mode_shape), shape((8, LANES))],
+            shape(mode_shape),
             [lane_rows, lane_modes, rest],
             cells,
-            y_high,
-            y_low,
+            extra,
+            y_forward,
             x_forward,
         )
 
-    def plane_synthesis(modes, sums):
+    def plane_synthesis(modes, extra):
         return call(
             with_plan(plane_synthesis_kernel),
             shape(cell_shape),
             [lane_rows, lane_modes, rest],
             modes,
-            sums,
-            y_high,
-            y_low,
+            extra,
+            y_inverse,
             x_inverse,
         )
 
+    nothing = jnp.zeros((8, LANES), f32)
     with jax.named_scope("depth_analysis"):
         cells = call(with_plan(depth_analysis_kernel), shape(cell_shape), [], field, z_forward)
     with jax.named_scope("cells_to_planes"):
         cells = cell_exchange(cells)
+    with jax.named_scope("pointwise"):
+        pointwise = call(
+            with_plan(pointwise_kernel),
+            shape(grid_shape),
+            [],
+            field,
+            pointwise_weight,
+            bias,
+            smem=(2,),
+        )
+        weights = with_layout_constraint(spectral_weight, Layout((0, 1, 2, 3, 4)))
+        cells, pointwise, weights = lax.optimization_barrier((cells, pointwise, weights))
     with jax.named_scope("plane_analysis"):
-        modes, no_sums = plane_analysis(cells)
+        modes = plane_analysis(cells, nothing)
     with jax.named_scope("planes_to_modes"):
         modes = mode_exchange(modes)
     with jax.named_scope("mix"):
@@ -836,68 +869,71 @@
             [shape(mode_shape), shape(own_shape)],
             [own, rest],
             modes,
-            spectral_weight,
+            weights,
         )
     with jax.named_scope("modes_to_planes"):
         modes = mode_exchange(modes)
     with jax.named_scope("plane_synthesis"):
-        cells = plane_synthesis(modes, no_sums)
+        cells = plane_synthesis(modes, nothing)
     with jax.named_scope("planes_to_cells"):
         cells = cell_exchange(cells)
     with jax.named_scope("activation"):
+        half_grid = shape(grid_shape, jnp.bfloat16)
         output, cells, grad_high, grad_low = call(
-            with_plan(middle_kernel),
-            [
-                shape(grid_shape, jnp.bfloat16),
-                shape(cell_shape),
-                shape(grid_shape, jnp.bfloat16),
-                shape(grid_shape, jnp.bfloat16),
-            ],
-            [grid, lines, pltpu.VMEM((wide, wide), f32), pltpu.VMEM((wide, plan.depth), f32)],
+            with_plan(activation_kernel),
+            [half_grid, shape(cell_shape), half_grid, half_grid],
+            [lines],
             cells,
-            field,
+            pointwise,
             cotangent,
-            pointwise_weight,
-            bias,
             scaled_inverse,
             scaled_forward,
-            smem=(4,),
         )
     with jax.named_scope("grad_cells_to_planes"):
         cells = cell_exchange(cells)
+    with jax.named_scope("pointwise_grad"):
+        back, sums = call(
+            with_plan(pointwise_grad_kernel),
+            [shape(grid_shape), row_shape],
+            [pltpu.VMEM((wide + 16, wide), f32)],
+            field,
+            grad_high,
+            grad_low,
+            pointwise_weight,
+        )
+        cells, back, sums = lax.optimization_barrier((cells, back, sums))
     with jax.named_scope("grad_plane_analysis"):
-        modes, sums = plane_analysis(cells)
+        modes = plane_analysis(cells, sums)
     with jax.named_scope("grad_planes_to_modes"):
         modes = mode_exchange(modes)
     with jax.named_scope("grad_mix"):
-        modes, grad_mix = call(
+        modes, grad_mix, sums = call(
             with_plan(mix_back_kernel),
-            [shape(mode_shape), shape(own_shape)],
+            [shape(mode_shape), shape(own_shape), row_shape],
             [own, rest],
             modes,
-            spectral_weight,
+            weights,
         )
     with jax.named_scope("grad_modes_to_planes"):
         modes = mode_exchange(modes)
     with jax.named_scope("grad_spectral"):
         grad_spectral = weight_grad(plan, spectrum, grad_mix)
+        modes, grad_spectral = lax.optimization_barrier((modes, grad_spectral))
     with jax.named_scope("grad_plane_synthesis"):
         cells = plane_synthesis(modes, sums)
     with jax.named_scope("grad_planes_to_cells"):
         cells = cell_exchange(cells)
     with jax.named_scope("grad_field"):
-        grad_field, sums = call(
+        channels = plan.channels
+        grad_field, map_grad, bias_grad = call(
             with_plan(last_kernel),
-            [shape(grid_shape, jnp.bfloat16), shape((24, LANES))],
-            [grid, lines],
+            [half_grid, shape((channels, channels)), shape((1, channels))],
+            [lines],
             cells,
-            grad_high,
-            grad_low,
-            pointwise_weight,
+            back,
             z_inverse,
         )
-    channels = plan.channels
-    return output, grad_field, grad_spectral, sums[:channels, :channels], sums[channels, :channels]
+    return output, grad_field, grad_spectral, map_grad, bias_grad.reshape(channels)
 
 
 def layer(field, cotangent, spectral_weight, pointwise_weight, bias):

time: 180 us -> 160 us (0.89)
  blocking collectives: 99.3 us -> 57.4 us
  waiting for transfers between devices: 4.7 us -> 19.2 us
  starting transfers between devices: 6.03 us -> 17.1 us
  Pallas kernels: 41.2 us -> 30.8 us
  local copies, waits for them, and re-layouts: 26.8 us -> 34.3 us
    all_to_all x3 -> x1, blocking collectives: 59.5 us -> 17.8 us  [cell_exchange(): lax.all_to_all(flat, ('gx', 'gy'), 0, 0, tiled=True).reshape(cell_shape)]
    all_to_all x1 -> x3, waiting for transfers between devices: 0.01 us -> 16.2 us  [cell_exchange(): lax.all_to_all(flat, ('gx', 'gy'), 0, 0, tiled=True).reshape(cell_shape)]
    all_to_all x1 -> x3, starting transfers between devices: 2.6 us -> 13.5 us  [cell_exchange(): lax.all_to_all(flat, ('gx', 'gy'), 0, 0, tiled=True).reshape(cell_shape)]
    unnamed x46 -> x52, local copies, waits for them, and re-layouts: 25.6 us -> 34.3 us
    pallas_call x1, Pallas kernels: 8.79 us -> 2.02 us  [weight_grad(): pl.pallas_call(functools.partial(weight_grad_kernel, plan), grid=(plan.ch...]
    pallas_call x9 -> x11, Pallas kernels: 32.4 us -> 28.8 us  [call(): pl.pallas_call(kernel, out_shape=out_shape, in_specs=specs, out_specs=out...]
  transfers between devices with their start and end apart: 2 -> 4, of which waited for: 1 -> 4; matrix products, arithmetic and copies ran while one was open for 10% -> 11% of each run, Pallas kernels for 5% -> 7%
where the time goes in v2:
time: 160 us
  blocking collectives  57.4 us (36%)
  local copies, waits for them, and re-layouts  34.3 us (21%)
  Pallas kernels  30.8 us (19%)
  waiting for transfers between devices  19.2 us (12%)
  starting transfers between devices  17.1 us (11%)
    all_to_all x3, blocking collectives, mode_exchange(): return lax.all_to_all(values, 'gx', 0, 0, tiled=True)  39.7 us
    unnamed x52, local copies, waits for them, and re-layouts  34.3 us
    pallas_call x11, Pallas kernels, call(): pl.pallas_call(kernel, out_shape=out_shape, in_specs=specs, out_specs=out...  28.8 us
    all_to_all x1, blocking collectives, cell_exchange(): lax.all_to_all(flat, ('gx', 'gy'), 0, 0, tiled=True).reshape(cell_shape)  17.8 us
    all_to_all x3, waiting for transfers between devices, cell_exchange(): lax.all_to_all(flat, ('gx', 'gy'), 0, 0, tiled=True).reshape(cell_shape)  16.2 us
    all_to_all x3, starting transfers between devices, cell_exchange(): lax.all_to_all(flat, ('gx', 'gy'), 0, 0, tiled=True).reshape(cell_shape)  13.5 us
    all_to_all x1, starting transfers between devices, mode_exchange(): return lax.all_to_all(values, 'gx', 0, 0, tiled=True)  3.6 us
  transfers between devices with their start and end apart: 4, of which 4 were waited for; matrix products, arithmetic and copies ran while one was open for 11% of the time, Pallas kernels for 7%

profile of v2, /device:TPU:0, one launch (start us, length us, event | category | flops | bytes accessed | tf_op | source)
XLA Modules:
  0.0 159.7 jit_solution(874888006749217076)
XLA Ops:
  0.6 0.0 copy-start.3
  0.6 1.3 copy-done.3
  2.0 0.8 copy-done.22
  2.7 1.3 depth_analysis.1
  4.1 7.3 %all-to-all-start = ((f32[32,32,128]{2,1,0:T(8,128)}), f32[32,32,128]{2,1,0:T(8,128)S(1)}, u32[]{:S(2)}, u32[]{:S(2)}) async-start(f32[32,32,128]{2,1,0:T(8,128)} %bitcast), calls=%async_computation | async-start | bytes 1048576 | tf_op jit(solution)/shard_map/cells_to_planes/all_to_all | solution.py:798
  11.4 0.0 copy-start.4
  11.4 0.0 copy-start.23
  11.4 0.0 copy-start.24
  11.4 5.2 %copy.18.weight_ref = bf16[2,20,20,6,288]{4,3,2,1,0:T(8,128)(2,1)} copy(bf16[2,20,20,6,288]{4,0,3,2,1:T(2,128)(2,1)} %param.15) | data formatting | bytes 5529600 | tf_op args[2]
  16.7 0.0 copy-done.4
  16.7 0.0 copy-done.23
  16.7 0.0 copy-done.24
  16.7 0.0 copy-start.12
  16.7 0.0 copy-start.18
  16.7 2.8 %pointwise.1.pointwise_ref = f32[20,8,16,256]{3,2,1,0:T(8,128)S(1)} custom-call(bf16[20,8,16,256]{3,2,1,0:T(8,128)(2,1)S(1)} %copy-done.4, bf16[20,20]{1,0:T(8,128)(2,1)S(1)} %copy-done.23, f32[20]{0:T(128)S(1)} %copy-done.24), custom_call_target="tpu_custom_call" | custom-call | tf_op jit(solution)/shard_map/pointwise/pallas_call | solution.py:317
  19.5 0.0 copy-start.5
  19.5 1.5 copy-done.5
  21.0 5.9 %all-to-all-done = f32[32,32,128]{2,1,0:T(8,128)S(1)} async-done(((f32[32,32,128]{2,1,0:T(8,128)}), f32[32,32,128]{2,1,0:T(8,128)S(1)}, u32[]{:S(2)}, u32[]{:S(2)}) %all-to-all-start) | async-done | bytes 524320 | tf_op jit(solution)/shard_map/cells_to_planes/all_to_all | solution.py:798
  26.9 0.0 copy-done.12
  26.9 0.0 copy-done.18
  26.9 1.4 plane_analysis.1
  28.4 13.3 %all_to_all.40.in_ref = f32[8,72,128]{2,1,0:T(8,128)S(1)} all-to-all(f32[8,72,128]{2,1,0:T(8,128)S(1)} %plane_analysis.1), channel_id=1, replica_groups=mesh['gx'=8,'gy'=4] {'gx'}, dimensions={0} | all-to-all | bytes 589824 | tf_op jit(solution)/shard_map/planes_to_modes/all_to_all | solution.py:801
  41.6 2.4 %copy-done = bf16[2,20,20,6,288]{4,3,2,1,0:T(8,128)(2,1)S(1)} copy-done((bf16[2,20,20,6,288]{4,3,2,1,0:T(8,128)(2,1)S(1)}, bf16[2,20,20,6,288]{4,3,2,1,0:T(8,128)(2,1)}, u32[]{:S(2)}) %copy-start) | copy-done | bytes 2764824
  44.0 0.0 copy-start.21
  44.1 2.7 %mix.1 = (f32[8,72,128]{2,1,0:T(8,128)S(1)}, f32[20,2,6,288]{3,2,1,0:T(8,128)S(1)}) custom-call(f32[8,72,128]{2,1,0:T(8,128)S(1)} %all_to_all.40.in_ref, bf16[2,20,20,6,288]{4,3,2,1,0:T(8,128)(2,1)S(1)} %copy-done), custom_call_target="tpu_custom_call" | custom-call | tf_op jit(solution)/shard_map/mix/pallas_call | solution.py:317
  46.8 0.0 copy-start.15
  46.8 0.0 copy-start.6
  46.8 13.1 %all_to_all.41.in_ref = f32[8,72,128]{2,1,0:T(8,128)S(1)} all-to-all(f32[8,72,128]{2,1,0:T(8,128)S(1)} %get-tuple-element.29), channel_id=1, replica_groups=mesh['gx'=8,'gy'=4] {'gx'}, dimensions={0} | all-to-all | bytes 589824 | tf_op jit(solution)/shard_map/modes_to_planes/all_to_all | solution.py:801
  59.9 0.0 copy-done.14
  59.9 0.0 copy-done.17
  59.9 1.4 plane_synthesis.1
  61.3 17.8 %all_to_all.42 = f32[32,32,128]{2,1,0:T(8,128)S(1)} all-to-all(f32[32,32,128]{2,1,0:T(8,128)S(1)} %bitcast.13), channel_id=1, replica_groups=mesh['gx'=8,'gy'=4] {'gx','gy'}, dimensions={0} | all-to-all | bytes 1048576 | tf_op jit(solution)/shard_map/planes_to_cells/all_to_all | solution.py:798
  79.1 0.0 copy-done.11
  79.1 0.0 copy-done.20
  79.1 0.0 copy-done.21
  79.1 0.0 copy-done.6
  79.1 4.8 %activation.1 = (bf16[20,8,16,256]{3,2,1,0:T(8,128)(2,1)}, f32[8,4,2,16,128]{4,3,2,1,0:T(8,128)S(1)}, bf16[20,8,16,256]{3,2,1,0:T(8,128)(2,1)S(1)}, bf16[20,8,16,256]{3,2,1,0:T(8,128)(2,1)S(1)}) custom-call(f32[8,4,2,16,128]{4,3,2,1,0:T(8,128)S(1)} %bitcast.10, f32[20,8,16,256]{3,2,1,0:T(8,128)S(1)} %copy-done.6, bf16[20,8,16,256]{3,2,1,0:T(8,128)(2,1)S(1)} %copy-done.11, ...), custom_call_target="tpu_custom_call" | custom-call | tf_op jit(solution)/shard_map/activation/pallas_call | solution.py:317
  83.8 0.0 copy-done.15
  83.8 1.1 copy-done.9
  84.9 0.8 copy-done.13
  85.7 3.1 %all-to-all-start.4 = ((f32[32,32,128]{2,1,0:T(8,128)}), f32[32,32,128]{2,1,0:T(8,128)S(1)}, u32[]{:S(2)}, u32[]{:S(2)}) async-start(f32[32,32,128]{2,1,0:T(8,128)} %bitcast.14), calls=%async_computation.4 | async-start | bytes 1048576 | tf_op jit(solution)/shard_map/grad_cells_to_planes/all_to_all | solution.py:798
  88.8 0.0 copy-start.10
  88.8 1.3 copy-done.10
  90.1 5.8 %pointwise_grad.1 = (f32[20,8,16,256]{3,2,1,0:T(8,128)S(1)}, f32[8,128]{1,0:T(8,128)S(1)}) custom-call(bf16[20,8,16,256]{3,2,1,0:T(8,128)(2,1)S(1)} %copy-done.4, bf16[20,8,16,256]{3,2,1,0:T(8,128)(2,1)S(1)} %get-tuple-element.33.high_ref, bf16[20,8,16,256]{3,2,1,0:T(8,128)(2,1)S(1)} %copy-done.10, bf16[20,20]{1,0:T(8,128)(2,1)S(1)} %copy-done.23), custom_call_target="tpu_custom_call" | custom-call | tf_op jit(solution)/shard_map/pointwise_grad/pallas_call | solution.py:317
  95.9 0.0 copy-start.7
  95.9 1.5 copy-done.7
  97.4 6.9 %all-to-all-done.4 = f32[32,32,128]{2,1,0:T(8,128)S(1)} async-done(((f32[32,32,128]{2,1,0:T(8,128)}), f32[32,32,128]{2,1,0:T(8,128)S(1)}, u32[]{:S(2)}, u32[]{:S(2)}) %all-to-all-start.4) | async-done | bytes 524320 | tf_op jit(solution)/shard_map/grad_cells_to_planes/all_to_all | solution.py:798
  104.3 1.4 grad_plane_analysis.1
  105.7 13.3 %all_to_all.43.in_ref = f32[8,72,128]{2,1,0:T(8,128)S(1)} all-to-all(f32[8,72,128]{2,1,0:T(8,128)S(1)} %grad_plane_analysis.1), channel_id=1, replica_groups=mesh['gx'=8,'gy'=4] {'gx'}, dimensions={0} | all-to-all | bytes 589824 | tf_op jit(solution)/shard_map/grad_planes_to_modes/all_to_all | solution.py:801
  119.0 2.4 %copy-done.1 = bf16[2,20,20,6,288]{4,3,2,1,0:T(8,128)(2,1)S(1)} copy-done((bf16[2,20,20,6,288]{4,3,2,1,0:T(8,128)(2,1)S(1)}, bf16[2,20,20,6,288]{4,3,2,1,0:T(8,128)(2,1)}, u32[]{:S(2)}) %copy-start.1) | copy-done | bytes 2764824
  121.4 3.4 %grad_mix.1 = (f32[8,72,128]{2,1,0:T(8,128)}, f32[20,2,6,288]{3,2,1,0:T(8,128)S(1)}, f32[8,128]{1,0:T(8,128)S(1)}) custom-call(f32[8,72,128]{2,1,0:T(8,128)S(1)} %all_to_all.43.in_ref, bf16[2,20,20,6,288]{4,3,2,1,0:T(8,128)(2,1)S(1)} %copy-done.1), custom_call_target="tpu_custom_call" | custom-call | tf_op jit(solution)/shard_map/grad_mix/pallas_call | solution.py:317
  124.8 3.6 %all-to-all-start.6 = ((f32[8,72,128]{2,1,0:T(8,128)}), f32[8,72,128]{2,1,0:T(8,128)S(1)}, u32[]{:S(2)}, u32[]{:S(2)}) async-start(f32[8,72,128]{2,1,0:T(8,128)} %get-tuple-element.39), calls=%async_computation.6 | async-start | bytes 589824 | tf_op jit(solution)/shard_map/grad_modes_to_planes/all_to_all | solution.py:801
  128.4 0.0 copy-done.16
  128.4 2.0 %grad_spectral.1 = f32[2,20,20,6,288]{4,3,2,1,0:T(8,128)S(1)} custom-call(f32[20,2,6,288]{3,2,1,0:T(8,128)S(1)} %copy-done.16, f32[20,2,6,288]{3,2,1,0:T(8,128)S(1)} %get-tuple-element.41.grad_ref), custom_call_target="tpu_custom_call" | custom-call | tf_op jit(solution)/shard_map/grad_spectral/pallas_call | solution.py:564
  130.5 0.0 copy-start.2
  130.5 3.8 %copy-done.2 = f32[2,20,20,6,288]{4,3,2,1,0:T(8,128)} copy-done((f32[2,20,20,6,288]{4,3,2,1,0:T(8,128)}, f32[2,20,20,6,288]{4,3,2,1,0:T(8,128)S(1)}, u32[]{:S(2)}) %copy-start.2) | copy-done | bytes 5529624
  134.3 3.0 %all-to-all-done.6.in_ref = f32[8,72,128]{2,1,0:T(8,128)S(1)} async-done(((f32[8,72,128]{2,1,0:T(8,128)}), f32[8,72,128]{2,1,0:T(8,128)S(1)}, u32[]{:S(2)}, u32[]{:S(2)}) %all-to-all-start.6) | async-done | bytes 294944 | tf_op jit(solution)/shard_map/grad_modes_to_planes/all_to_all | solution.py:801
  137.2 2.2 %grad_plane_synthesis.1 = f32[8,4,2,16,128]{4,3,2,1,0:T(8,128)} custom-call(f32[8,72,128]{2,1,0:T(8,128)S(1)} %all-to-all-done.6.in_ref, f32[8,128]{1,0:T(8,128)S(1)} %get-tuple-element.43.extra_ref, bf16[256,256]{1,0:T(8,128)(2,1)S(1)} %copy-done.14, bf16[128,144]{1,0:T(8,128)(2,1)S(1)} %copy-done.17), custom_call_target="tpu_custom_call" | custom-call | tf_op jit(solution)/shard_map/grad_plane_synthesis/pallas_call | solution.py:317
  139.4 3.1 %all-to-all-start.7 = ((f32[32,32,128]{2,1,0:T(8,128)}), f32[32,32,128]{2,1,0:T(8,128)S(1)}, u32[]{:S(2)}, u32[]{:S(2)}) async-start(f32[32,32,128]{2,1,0:T(8,128)} %bitcast.6), calls=%async_computation.7 | async-start | bytes 1048576 | tf_op jit(solution)/shard_map/grad_planes_to_cells/all_to_all | solution.py:798
  142.5 0.0 copy-start.19
  142.5 12.1 %copy.19 = f32[2,20,20,6,288]{4,0,3,2,1:T(2,128)} copy(f32[2,20,20,6,288]{4,3,2,1,0:T(8,128)} %copy-done.2) | data formatting | bytes 11059200
  154.6 3.4 %all-to-all-done.7 = f32[32,32,128]{2,1,0:T(8,128)S(1)} async-done(((f32[32,32,128]{2,1,0:T(8,128)}), f32[32,32,128]{2,1,0:T(8,128)S(1)}, u32[]{:S(2)}, u32[]{:S(2)}) %all-to-all-start.7) | async-done | bytes 524320 | tf_op jit(solution)/shard_map/grad_planes_to_cells/all_to_all | solution.py:798
  158.0 0.0 copy-done.19
  158.0 1.7 %grad_field.1 = (bf16[20,8,16,256]{3,2,1,0:T(8,128)(2,1)}, f32[20,20]{1,0:T(8,128)}, f32[1,20]{1,0:T(1,128)}) custom-call(f32[8,4,2,16,128]{4,3,2,1,0:T(8,128)S(1)} %bitcast.9, f32[20,8,16,256]{3,2,1,0:T(8,128)S(1)} %copy-done.8, bf16[144,256]{1,0:T(8,128)(2,1)S(1)} %copy-done.19), custom_call_target="tpu_custom_call" | custom-call | tf_op jit(solution)/shard_map/grad_field/pallas_call | solution.py:317
  (13 shorter events, 0.0 us)
Async XLA Ops:
  0.6 1.3 copy-start.3
  1.9 0.8 copy-start.22
  4.1 22.9 %all-to-all-start = ((f32[32,32,128]{2,1,0:T(8,128)}), f32[32,32,128]{2,1,0:T(8,128)S(1)}, u32[]{:S(2)}, u32[]{:S(2)}) async-start(f32[32,32,128]{2,1,0:T(8,128)} %bitcast), calls=%async_computation | async-start | bytes 1048576 | tf_op jit(solution)/shard_map/cells_to_planes/all_to_all | solution.py:798
  11.4 5.3 %copy-start.4 = (bf16[20,8,16,256]{3,2,1,0:T(8,128)(2,1)S(1)}, bf16[20,8,16,256]{3,2,1,0:T(8,128)(2,1)}, u32[]{:S(2)}) copy-start(bf16[20,8,16,256]{3,2,1,0:T(8,128)(2,1)} %field_ref.5) | copy-start | bytes 3932164
  11.4 5.3 %copy-start.23 = (bf16[20,20]{1,0:T(8,128)(2,1)S(1)}, bf16[20,20]{1,0:T(8,128)(2,1)}, u32[]{:S(2)}) copy-start(bf16[20,20]{1,0:T(8,128)(2,1)} %map_ref.3) | copy-start | bytes 2404
  11.4 5.2 %copy-start.24 = (f32[20]{0:T(128)S(1)}, f32[20]{0:T(128)}, u32[]{:S(2)}) copy-start(f32[20]{0:T(128)} %bias_ref.1) | copy-start | bytes 244
  16.7 10.3 %copy-start.12 = (bf16[256,256]{1,0:T(8,128)(2,1)S(1)}, bf16[256,256]{1,0:T(8,128)(2,1)}, u32[]{:S(2)}) copy-start(bf16[256,256]{1,0:T(8,128)(2,1)} %constant.22.clone.y_ref) | copy-start | bytes 393220
  16.7 10.3 %copy-start.18 = (bf16[96,192]{1,0:T(8,128)(2,1)S(1)}, bf16[96,192]{1,0:T(8,128)(2,1)}, u32[]{:S(2)}) copy-start(bf16[96,192]{1,0:T(8,128)(2,1)} %constant.24.clone.x_ref) | copy-start | bytes 110596
  19.5 1.5 copy-start.5
  41.6 2.4 %copy-start = (bf16[2,20,20,6,288]{4,3,2,1,0:T(8,128)(2,1)S(1)}, bf16[2,20,20,6,288]{4,3,2,1,0:T(8,128)(2,1)}, u32[]{:S(2)}) copy-start(bf16[2,20,20,6,288]{4,3,2,1,0:T(8,128)(2,1)} %copy.18.weight_ref) | copy-start | bytes 8294404
  44.0 15.9 %copy-start.14 = (bf16[256,256]{1,0:T(8,128)(2,1)S(1)}, bf16[256,256]{1,0:T(8,128)(2,1)}, u32[]{:S(2)}) copy-start(bf16[256,256]{1,0:T(8,128)(2,1)} %constant.23.clone.y_ref) | copy-start | bytes 393220
  44.0 15.9 %copy-start.17 = (bf16[128,144]{1,0:T(8,128)(2,1)S(1)}, bf16[128,144]{1,0:T(8,128)(2,1)}, u32[]{:S(2)}) copy-start(bf16[128,144]{1,0:T(8,128)(2,1)} %constant.25.clone.x_ref) | copy-start | bytes 110596
  44.0 35.0 %copy-start.11 = (bf16[20,8,16,256]{3,2,1,0:T(8,128)(2,1)S(1)}, bf16[20,8,16,256]{3,2,1,0:T(8,128)(2,1)}, u32[]{:S(2)}) copy-start(bf16[20,8,16,256]{3,2,1,0:T(8,128)(2,1)} %cotangent_ref.1) | copy-start | bytes 3932164
  44.0 35.0 %copy-start.20 = (bf16[144,256]{1,0:T(8,128)(2,1)S(1)}, bf16[144,256]{1,0:T(8,128)(2,1)}, u32[]{:S(2)}) copy-start(bf16[144,256]{1,0:T(8,128)(2,1)} %constant.21.clone.inverse_ref) | copy-start | bytes 221188
  44.0 35.0 %copy-start.21 = (bf16[96,256]{1,0:T(8,128)(2,1)S(1)}, bf16[96,256]{1,0:T(8,128)(2,1)}, u32[]{:S(2)}) copy-start(bf16[96,256]{1,0:T(8,128)(2,1)} %constant.20.clone.forward_ref) | copy-start | bytes 147460
  46.8 37.1 %copy-start.15 = (f32[20,2,6,288]{3,2,1,0:T(8,128)}, f32[20,2,6,288]{3,2,1,0:T(8,128)S(1)}, u32[]{:S(2)}) copy-start(f32[20,2,6,288]{3,2,1,0:T(8,128)S(1)} %get-tuple-element.40.spectrum_ref) | copy-start | bytes 829444
  46.8 32.3 %copy-start.6 = (f32[20,8,16,256]{3,2,1,0:T(8,128)S(1)}, f32[20,8,16,256]{3,2,1,0:T(8,128)}, u32[]{:S(2)}) copy-start(f32[20,8,16,256]{3,2,1,0:T(8,128)} %copy-done.5) | copy-start | bytes 7864324
  83.8 1.1 copy-start.9
  84.9 0.8 copy-start.13
  85.7 18.6 %all-to-all-start.4 = ((f32[32,32,128]{2,1,0:T(8,128)}), f32[32,32,128]{2,1,0:T(8,128)S(1)}, u32[]{:S(2)}, u32[]{:S(2)}) async-start(f32[32,32,128]{2,1,0:T(8,128)} %bitcast.14), calls=%async_computation.4 | async-start | bytes 1048576 | tf_op jit(solution)/shard_map/grad_cells_to_planes/all_to_all | solution.py:798
  88.8 1.3 copy-start.10
  95.9 1.5 copy-start.7
  119.0 2.4 %copy-start.1 = (bf16[2,20,20,6,288]{4,3,2,1,0:T(8,128)(2,1)S(1)}, bf16[2,20,20,6,288]{4,3,2,1,0:T(8,128)(2,1)}, u32[]{:S(2)}) copy-start(bf16[2,20,20,6,288]{4,3,2,1,0:T(8,128)(2,1)} %copy.18.weight_ref) | copy-start | bytes 8294404
  121.4 7.0 %copy-start.16 = (f32[20,2,6,288]{3,2,1,0:T(8,128)S(1)}, f32[20,2,6,288]{3,2,1,0:T(8,128)}, u32[]{:S(2)}) copy-start(f32[20,2,6,288]{3,2,1,0:T(8,128)} %copy-done.15) | copy-start | bytes 829444
  124.8 12.4 %all-to-all-start.6 = ((f32[8,72,128]{2,1,0:T(8,128)}), f32[8,72,128]{2,1,0:T(8,128)S(1)}, u32[]{:S(2)}, u32[]{:S(2)}) async-start(f32[8,72,128]{2,1,0:T(8,128)} %get-tuple-element.39), calls=%async_computation.6 | async-start | bytes 589824 | tf_op jit(solution)/shard_map/grad_modes_to_planes/all_to_all | solution.py:801
  130.5 3.8 %copy-start.2 = (f32[2,20,20,6,288]{4,3,2,1,0:T(8,128)}, f32[2,20,20,6,288]{4,3,2,1,0:T(8,128)S(1)}, u32[]{:S(2)}) copy-start(f32[2,20,20,6,288]{4,3,2,1,0:T(8,128)S(1)} %grad_spectral.1) | copy-start | bytes 16588804
  139.4 18.6 %all-to-all-start.7 = ((f32[32,32,128]{2,1,0:T(8,128)}), f32[32,32,128]{2,1,0:T(8,128)S(1)}, u32[]{:S(2)}, u32[]{:S(2)}) async-start(f32[32,32,128]{2,1,0:T(8,128)} %bitcast.6), calls=%async_computation.7 | async-start | bytes 1048576 | tf_op jit(solution)/shard_map/grad_planes_to_cells/all_to_all | solution.py:798
  142.5 15.5 %copy-start.8 = (f32[20,8,16,256]{3,2,1,0:T(8,128)S(1)}, f32[20,8,16,256]{3,2,1,0:T(8,128)}, u32[]{:S(2)}) copy-start(f32[20,8,16,256]{3,2,1,0:T(8,128)} %copy-done.7) | copy-start | bytes 7864324
  142.5 15.5 %copy-start.19 = (bf16[144,256]{1,0:T(8,128)(2,1)S(1)}, bf16[144,256]{1,0:T(8,128)(2,1)}, u32[]{:S(2)}) copy-start(bf16[144,256]{1,0:T(8,128)(2,1)} %constant.19.clone.inverse_ref) | copy-start | bytes 221188

commit v3 on v2

--- a/solution.py
+++ b/solution.py
@@ -177,7 +177,8 @@
 LANES = 128
 HALF = 64
 SLOT = 32
-VMEM_BYTES = 40 * 1024 * 1024
+CHUNKS = 4
+VMEM_BYTES = 20 * 1024 * 1024
 
 
 def split_table(table):
@@ -258,6 +259,7 @@
             and self.pair_rows == 2 * LANES + 32
             and self.width_y <= HALF
             and size_x == 8
+            and self.channels % CHUNKS == 0
             and self.channels <= SLOT
             and self.channels < size_x * (LANES // SLOT)
             and self.own_z * 2 * self.part_z * size_y == 2 * MZ
@@ -307,21 +309,28 @@
         return tables
 
 
-def call(kernel, out_shape, scratch, *operands, smem=(), **more):
-    specs = [
-        pl.BlockSpec(memory_space=pltpu.SMEM if at in smem else pltpu.VMEM)
-        for at in range(len(operands))
+def call(kernel, out_shape, scratch, *operands, smem=(), hbm=(), hbm_outs=()):
+    operands = [
+        pltpu.with_memory_space_constraint(operand, pltpu.HBM) if at in hbm else operand
+        for at, operand in enumerate(operands)
     ]
+    specs = []
+    for at in range(len(operands)):
+        space = pltpu.SMEM if at in smem else pltpu.HBM if at in hbm else pltpu.VMEM
+        specs.append(pl.BlockSpec(memory_space=space))
     single = not isinstance(out_shape, (tuple, list))
-    outs = pl.BlockSpec(memory_space=pltpu.VMEM)
+    shapes = [out_shape] if single else out_shape
+    outs = [
+        pl.BlockSpec(memory_space=pltpu.HBM if at in hbm_outs else pltpu.VMEM)
+        for at in range(len(shapes))
+    ]
     return pl.pallas_call(
         kernel,
         out_shape=out_shape,
         in_specs=specs,
-        out_specs=outs if single else [outs] * len(out_shape),
+        out_specs=outs[0] if single else outs,
         scratch_shapes=scratch,
         compiler_params=pltpu.CompilerParams(vmem_limit_bytes=VMEM_BYTES),
-        **more,
     )(*operands)
 
 
@@ -362,11 +371,23 @@
                 out_ref[place_x, place_y, which, plan.planes :, :] = zeros
 
 
-def depth_analysis_kernel(plan, field_ref, table_ref, out_ref):
+def depth_analysis_kernel(plan, field_ref, table_ref, out_ref, blocks_ref, held_ref, arrived):
+    copies = [pltpu.make_async_copy(table_ref, held_ref, arrived.at[2])]
+    size = plan.channels // 2
+    for part in range(2):
+        mine = pl.ds(part * size, size)
+        copies.append(
+            pltpu.make_async_copy(field_ref.at[mine], blocks_ref.at[mine], arrived.at[part])
+        )
+    for copy in copies:
+        copy.start()
     clear_spare(plan, out_ref)
-    table = table_ref[...]
+    copies[0].wait()
+    table = held_ref[...]
     for channel in range(plan.channels):
-        block = field_ref[channel].reshape(plan.cells, plan.depth)
+        if channel % size == 0:
+            copies[1 + channel // size].wait()
+        block = blocks_ref[channel].reshape(plan.cells, plan.depth)
         both = product(table, block, NT)
         put_spectrum(plan, out_ref, channel, both[: 2 * MZ] + both[2 * MZ :])
 
@@ -501,7 +522,24 @@
         out_ref[place_x, 4 * pad : 4 * pad + 8, :] = pack_rest(rest_ref)
 
 
-def mix_kernel(plan, in_ref, weight_ref, out_ref, spectrum_ref, mixed_ref, rest_ref):
+def bring_weights(plan, weight_hbm, weight_ref, arrived, by_input):
+    copies = []
+    size = plan.channels // CHUNKS
+    for chunk in range(CHUNKS):
+        mine = pl.ds(chunk * size, size)
+        at = (slice(None), mine) if by_input else (slice(None), slice(None), mine)
+        copies.append(
+            pltpu.make_async_copy(weight_hbm.at[at], weight_ref.at[at], arrived.at[chunk])
+        )
+    for copy in copies:
+        copy.start()
+    return copies
+
+
+def mix_kernel(
+    plan, in_ref, weight_hbm, out_ref, spectrum_ref, mixed_ref, rest_ref, weight_ref, arrived
+):
+    copies = bring_weights(plan, weight_hbm, weight_ref, arrived, False)
     take_modes(plan, in_ref, spectrum_ref, rest_ref)
     shape = (plan.blocks_z, plan.pair_rows)
 
@@ -519,11 +557,26 @@
         mixed_ref[out_channel, 1] = imag_part
         return carry
 
-    lax.fori_loop(0, plan.channels, one, 0)
+    size = plan.channels // CHUNKS
+    for chunk, copy in enumerate(copies):
+        copy.wait()
+        lax.fori_loop(chunk * size, (chunk + 1) * size, one, 0)
     put_modes(plan, mixed_ref, out_ref, rest_ref)
 
 
-def mix_back_kernel(plan, in_ref, weight_ref, out_ref, grad_ref, sums_ref, mixed_ref, rest_ref):
+def mix_back_kernel(
+    plan,
+    in_ref,
+    weight_hbm,
+    out_ref,
+    grad_ref,
+    sums_ref,
+    mixed_ref,
+    rest_ref,
+    weight_ref,
+    arrived,
+):
+    copies = bring_weights(plan, weight_hbm, weight_ref, arrived, True)
     spare = jnp.zeros((1, LANES), jnp.float32)
     for place_x in range(plan.size_x):
         spare = spare + in_ref[place_x, plan.planes : plan.planes + 1, :]
@@ -545,11 +598,15 @@
         mixed_ref[channel, 1] = imag_part
         return carry
 
-    lax.fori_loop(0, plan.channels, one, 0)
+    size = plan.channels // CHUNKS
+    for chunk, copy in enumerate(copies):
+        copy.wait()
+        lax.fori_loop(chunk * size, (chunk + 1) * size, one, 0)
     put_modes(plan, mixed_ref, out_ref, rest_ref)
 
 
-def weight_grad_kernel(plan, spectrum_ref, grad_ref, out_ref):
+def weight_grad_kernel(plan, spectrum_ref, grad_ref, sums_ref, out_ref, passed_ref):
+    passed_ref[...] = sums_ref[...]
     value_re = spectrum_ref[0, 0]
     value_im = spectrum_ref[0, 1]
     for out_channel in range(plan.channels):
@@ -559,21 +616,26 @@
         out_ref[1, 0, out_channel] = value_re * grad_im - value_im * grad_re
 
 
-def weight_grad(plan, spectrum, grad):
+def weight_grad(plan, spectrum, grad, sums):
     modes = (plan.blocks_z, plan.pair_rows)
     return pl.pallas_call(
         functools.partial(weight_grad_kernel, plan),
         grid=(plan.channels,),
-        out_shape=jax.ShapeDtypeStruct((2, plan.channels, plan.channels) + modes, jnp.float32),
+        out_shape=[
+            jax.ShapeDtypeStruct((2, plan.channels, plan.channels) + modes, jnp.float32),
+            jax.ShapeDtypeStruct(sums.shape, jnp.float32),
+        ],
         in_specs=[
             pl.BlockSpec((1, 2) + modes, lambda channel: (channel, 0, 0, 0)),
             pl.BlockSpec((plan.channels, 2) + modes, lambda channel: (0, 0, 0, 0)),
+            pl.BlockSpec(sums.shape, lambda channel: (0, 0)),
         ],
-        out_specs=pl.BlockSpec(
-            (2, 1, plan.channels) + modes, lambda channel: (0, channel, 0, 0, 0)
-        ),
+        out_specs=[
+            pl.BlockSpec((2, 1, plan.channels) + modes, lambda channel: (0, channel, 0, 0, 0)),
+            pl.BlockSpec(sums.shape, lambda channel: (0, 0)),
+        ],
         compiler_params=pltpu.CompilerParams(vmem_limit_bytes=VMEM_BYTES),
-    )(spectrum, grad)
+    )(spectrum, grad, sums)
 
 
 def plane_synthesis_kernel(
@@ -664,7 +726,9 @@
     return product(jnp.concatenate([high, high, low], axis=0), table, TN)
 
 
-def pointwise_kernel(plan, field_ref, map_ref, bias_ref, out_ref):
+def pointwise_kernel(plan, field_ref, map_ref, bias_ref, weight_ref, out_ref, nothing_ref):
+    del weight_ref
+    nothing_ref[...] = jnp.zeros((8, LANES), jnp.float32)
     rows, size = plan.channels * plan.rows_y, plan.rows_y
     wide = widen_map(plan, map_ref[...], False)
 
@@ -686,12 +750,18 @@
     cotangent_ref,
     inverse_ref,
     forward_ref,
+    output_hbm,
+    spectrum_ref,
+    high_hbm,
+    low_hbm,
+    rows_ref,
     output_ref,
-    spectrum_ref,
     high_ref,
     low_ref,
-    rows_ref,
+    sent,
 ):
+    pairs = ((output_ref, output_hbm), (high_ref, high_hbm), (low_ref, low_hbm))
+    copies = []
     clear_spare(plan, spectrum_ref)
     flat = (plan.cells, plan.depth)
     block = (plan.rows_x, plan.rows_y, plan.depth)
@@ -715,6 +785,23 @@
         both = product(forward, high, NT)
         more = product(forward[: 2 * MZ], low, NT)
         put_spectrum(plan, spectrum_ref, channel, both[: 2 * MZ] + both[2 * MZ :] + more)
+        copies += send_block(plan, channel, pairs, sent)
+    for copy in copies:
+        copy.wait()
+
+
+def send_block(plan, channel, pairs, sent):
+    block, inner = divmod(channel, plan.own_c)
+    if inner < plan.own_c - 1:
+        return []
+    mine = pl.ds(block * plan.own_c, plan.own_c)
+    copies = [
+        pltpu.make_async_copy(held.at[mine], target.at[mine], sent.at[at, block])
+        for at, (held, target) in enumerate(pairs)
+    ]
+    for copy in copies:
+        copy.start()
+    return copies
 
 
 def pointwise_grad_kernel(
@@ -758,7 +845,14 @@
 
 
 def last_kernel(
-    plan, in_ref, back_ref, inverse_ref, grad_ref, map_grad_ref, bias_grad_ref, rows_ref
+    plan,
+    in_ref,
+    back_ref,
+    inverse_ref,
+    grad_ref,
+    map_grad_ref,
+    bias_grad_ref,
+    rows_ref,
 ):
     block = (plan.rows_x, plan.rows_y, plan.depth)
     flat = (plan.cells, plan.depth)
@@ -817,6 +911,16 @@
     wide = plan.channels * plan.rows_y
     row_shape = shape((8, LANES))
 
+    blocks_sent = pltpu.SemaphoreType.DMA((3, plan.part_c))
+
+    held_weights = [
+        pltpu.VMEM(spectral_weight.shape, spectral_weight.dtype),
+        pltpu.SemaphoreType.DMA((CHUNKS,)),
+    ]
+
+    def in_hbm(struct):
+        return pltpu.HBM(struct.shape, struct.dtype)
+
     def with_plan(kernel):
         return functools.partial(kernel, plan)
 
@@ -842,23 +946,34 @@
             x_inverse,
         )
 
-    nothing = jnp.zeros((8, LANES), f32)
     with jax.named_scope("depth_analysis"):
-        cells = call(with_plan(depth_analysis_kernel), shape(cell_shape), [], field, z_forward)
+        cells = call(
+            with_plan(depth_analysis_kernel),
+            in_hbm(shape(cell_shape)),
+            [
+                pltpu.VMEM(grid_shape, jnp.bfloat16),
+                pltpu.VMEM(z_forward.shape, jnp.bfloat16),
+                pltpu.SemaphoreType.DMA((3,)),
+            ],
+            field,
+            z_forward,
+            hbm=(0, 1),
+        )
     with jax.named_scope("cells_to_planes"):
         cells = cell_exchange(cells)
     with jax.named_scope("pointwise"):
-        pointwise = call(
+        weights = with_layout_constraint(spectral_weight, Layout((0, 1, 2, 3, 4)))
+        pointwise, nothing = call(
             with_plan(pointwise_kernel),
-            shape(grid_shape),
+            [in_hbm(shape(grid_shape)), row_shape],
             [],
             field,
             pointwise_weight,
             bias,
+            weights,
             smem=(2,),
-        )
-        weights = with_layout_constraint(spectral_weight, Layout((0, 1, 2, 3, 4)))
-        cells, pointwise, weights = lax.optimization_barrier((cells, pointwise, weights))
+            hbm=(3,),
+        )
     with jax.named_scope("plane_analysis"):
         modes = plane_analysis(cells, nothing)
     with jax.named_scope("planes_to_modes"):
@@ -867,9 +982,10 @@
         modes, spectrum = call(
             with_plan(mix_kernel),
             [shape(mode_shape), shape(own_shape)],
-            [own, rest],
+            [own, rest] + held_weights,
             modes,
             weights,
+            hbm=(1,),
         )
     with jax.named_scope("modes_to_planes"):
         modes = mode_exchange(modes)
@@ -881,27 +997,27 @@
         half_grid = shape(grid_shape, jnp.bfloat16)
         output, cells, grad_high, grad_low = call(
             with_plan(activation_kernel),
-            [half_grid, shape(cell_shape), half_grid, half_grid],
-            [lines],
+            [in_hbm(half_grid), in_hbm(shape(cell_shape)), in_hbm(half_grid), in_hbm(half_grid)],
+            [lines] + [pltpu.VMEM(grid_shape, jnp.bfloat16)] * 3 + [blocks_sent],
             cells,
             pointwise,
             cotangent,
             scaled_inverse,
             scaled_forward,
+            hbm_outs=(0, 2, 3),
         )
     with jax.named_scope("grad_cells_to_planes"):
         cells = cell_exchange(cells)
     with jax.named_scope("pointwise_grad"):
         back, sums = call(
             with_plan(pointwise_grad_kernel),
-            [shape(grid_shape), row_shape],
+            [in_hbm(shape(grid_shape)), row_shape],
             [pltpu.VMEM((wide + 16, wide), f32)],
             field,
             grad_high,
             grad_low,
             pointwise_weight,
         )
-        cells, back, sums = lax.optimization_barrier((cells, back, sums))
     with jax.named_scope("grad_plane_analysis"):
         modes = plane_analysis(cells, sums)
     with jax.named_scope("grad_planes_to_modes"):
@@ -910,15 +1026,15 @@
         modes, grad_mix, sums = call(
             with_plan(mix_back_kernel),
             [shape(mode_shape), shape(own_shape), row_shape],
-            [own, rest],
+            [own, rest] + held_weights,
             modes,
             weights,
+            hbm=(1,),
         )
     with jax.named_scope("grad_modes_to_planes"):
         modes = mode_exchange(modes)
     with jax.named_scope("grad_spectral"):
-        grad_spectral = weight_grad(plan, spectrum, grad_mix)
-        modes, grad_spectral = lax.optimization_barrier((modes, grad_spectral))
+        grad_spectral, sums = weight_grad(plan, spectrum, grad_mix, sums)
     with jax.named_scope("grad_plane_synthesis"):
         cells = plane_synthesis(modes, sums)
     with jax.named_scope("grad_planes_to_cells"):

time: 160 us -> 156 us (0.975)
  local copies, waits for them, and re-layouts: 34.3 us -> 23.8 us
  Pallas kernels: 30.8 us -> 37.1 us
    unnamed x52 -> x34, local copies, waits for them, and re-layouts: 34.3 us -> 23.8 us
    pallas_call x11, Pallas kernels: 28.8 us -> 35.1 us  [call(): pl.pallas_call(kernel, out_shape=out_shape, in_specs=specs, out_specs=out...]
  transfers between devices with their start and end apart: 4 -> 4, of which waited for: 4 -> 4; matrix products, arithmetic and copies ran while one was open for 11% -> 11% of each run, Pallas kernels for 7% -> 8%
where the time goes in v3:
time: 156 us; the launch traced here: 155 us
  blocking collectives  57.4 us (37%)
  Pallas kernels  37.1 us (24%)
  local copies, waits for them, and re-layouts  23.8 us (15%)
  waiting for transfers between devices  19.3 us (12%)
  starting transfers between devices  16.9 us (11%)
    all_to_all x3, blocking collectives, mode_exchange(): return lax.all_to_all(values, 'gx', 0, 0, tiled=True)  39.7 us
    pallas_call x11, Pallas kernels, call(): pl.pallas_call(kernel, out_shape=out_shape, in_specs=specs, out_specs=out...  35.1 us
    unnamed x34, local copies, waits for them, and re-layouts  23.8 us
    all_to_all x1, blocking collectives, cell_exchange(): lax.all_to_all(flat, ('gx', 'gy'), 0, 0, tiled=True).reshape(cell_shape)  17.8 us
    all_to_all x3, waiting for transfers between devices, cell_exchange(): lax.all_to_all(flat, ('gx', 'gy'), 0, 0, tiled=True).reshape(cell_shape)  16.2 us
    all_to_all x3, starting transfers between devices, cell_exchange(): lax.all_to_all(flat, ('gx', 'gy'), 0, 0, tiled=True).reshape(cell_shape)  13.5 us
    all_to_all x1, starting transfers between devices, mode_exchange(): return lax.all_to_all(values, 'gx', 0, 0, tiled=True)  3.43 us
    all_to_all x1, waiting for transfers between devices, mode_exchange(): return lax.all_to_all(values, 'gx', 0, 0, tiled=True)  3.14 us
  transfers between devices with their start and end apart: 4, of which 4 were waited for; matrix products, arithmetic and copies ran while one was open for 11% of the time, Pallas kernels for 8%

profile of v3, /device:TPU:0, one launch (start us, length us, event | category | flops | bytes accessed | tf_op | source)
XLA Modules:
  0.0 155.4 jit_solution(10392085645981295066)
XLA Ops:
  0.6 2.6 %depth_analysis.1 = f32[8,4,2,16,128]{4,3,2,1,0:T(8,128)} custom-call(bf16[20,8,16,256]{3,2,1,0:T(8,128)(2,1)} %field_ref.5, bf16[96,256]{1,0:T(8,128)(2,1)} %constant.16.clone.table_ref), custom_call_target="tpu_custom_call" | custom-call | tf_op jit(solution)/shard_map/depth_analysis/pallas_call | solution.py:327
  3.3 7.3 %all-to-all-start = ((f32[32,32,128]{2,1,0:T(8,128)}), f32[32,32,128]{2,1,0:T(8,128)S(1)}, u32[]{:S(2)}, u32[]{:S(2)}) async-start(f32[32,32,128]{2,1,0:T(8,128)} %bitcast.14), calls=%async_computation | async-start | bytes 1048576 | tf_op jit(solution)/shard_map/cells_to_planes/all_to_all | solution.py:892
  10.6 0.0 copy-start
  10.6 0.0 copy-start.14
  10.6 0.0 copy-start.15
  10.6 5.2 %copy.18.weight_ref.weight_hbm = bf16[2,20,20,6,288]{4,3,2,1,0:T(8,128)(2,1)} copy(bf16[2,20,20,6,288]{4,0,3,2,1:T(2,128)(2,1)} %param.15) | data formatting | bytes 5529600 | tf_op args[2]
  15.8 0.0 copy-done
  15.8 0.0 copy-done.14
  15.8 0.0 copy-done.15
  15.8 0.0 copy-start.7
  15.9 0.0 copy-start.10
  15.9 4.3 %pointwise.1 = (f32[20,8,16,256]{3,2,1,0:T(8,128)}, f32[8,128]{1,0:T(8,128)S(1)}) custom-call(bf16[20,8,16,256]{3,2,1,0:T(8,128)(2,1)S(1)} %copy-done, bf16[20,20]{1,0:T(8,128)(2,1)S(1)} %copy-done.14, f32[20]{0:T(128)S(1)} %copy-done.15, bf16[2,20,20,6,288]{4,3,2,1,0:T(8,128)(2,1)} %copy.18.weight_ref.weight_hbm), custom_call_target="tpu_custom_call" | custom-call | tf_op jit(solution)/shard_map/pointwise/pallas_call | solution.py:327
  20.2 5.9 %all-to-all-done = f32[32,32,128]{2,1,0:T(8,128)S(1)} async-done(((f32[32,32,128]{2,1,0:T(8,128)}), f32[32,32,128]{2,1,0:T(8,128)S(1)}, u32[]{:S(2)}, u32[]{:S(2)}) %all-to-all-start) | async-done | bytes 524320 | tf_op jit(solution)/shard_map/cells_to_planes/all_to_all | solution.py:892
  26.1 0.0 copy-done.7
  26.1 0.0 copy-done.10
  26.1 1.4 plane_analysis.1
  27.5 13.3 %all_to_all.40.in_ref = f32[8,72,128]{2,1,0:T(8,128)S(1)} all-to-all(f32[8,72,128]{2,1,0:T(8,128)S(1)} %plane_analysis.1), channel_id=1, replica_groups=mesh['gx'=8,'gy'=4] {'gx'}, dimensions={0} | all-to-all | bytes 589824 | tf_op jit(solution)/shard_map/planes_to_modes/all_to_all | solution.py:895
  40.8 0.0 copy-start.8
  40.8 0.0 copy-start.9
  40.8 0.0 copy-start.6
  40.8 0.0 copy-start.12
  40.8 0.0 copy-start.13
  40.8 4.0 %mix.1 = (f32[8,72,128]{2,1,0:T(8,128)S(1)}, f32[20,2,6,288]{3,2,1,0:T(8,128)S(1)}) custom-call(f32[8,72,128]{2,1,0:T(8,128)S(1)} %all_to_all.40.in_ref, bf16[2,20,20,6,288]{4,3,2,1,0:T(8,128)(2,1)} %copy.18.weight_ref.weight_hbm), custom_call_target="tpu_custom_call" | custom-call | tf_op jit(solution)/shard_map/mix/pallas_call | solution.py:327
  44.9 0.0 copy-start.3
  44.9 13.1 %all_to_all.41.in_ref = f32[8,72,128]{2,1,0:T(8,128)S(1)} all-to-all(f32[8,72,128]{2,1,0:T(8,128)S(1)} %get-tuple-element.24), channel_id=1, replica_groups=mesh['gx'=8,'gy'=4] {'gx'}, dimensions={0} | all-to-all | bytes 589824 | tf_op jit(solution)/shard_map/modes_to_planes/all_to_all | solution.py:895
  58.0 0.0 copy-done.8
  58.0 0.0 copy-done.9
  58.0 1.4 plane_synthesis.1
  59.4 17.8 %all_to_all.42 = f32[32,32,128]{2,1,0:T(8,128)S(1)} all-to-all(f32[32,32,128]{2,1,0:T(8,128)S(1)} %bitcast.13), channel_id=1, replica_groups=mesh['gx'=8,'gy'=4] {'gx','gy'}, dimensions={0} | all-to-all | bytes 1048576 | tf_op jit(solution)/shard_map/planes_to_cells/all_to_all | solution.py:892
  77.2 0.0 copy-done.6
  77.2 0.0 copy-done.12
  77.2 0.0 copy-done.13
  77.2 0.0 copy-done.3
  77.2 5.5 %activation.1 = (bf16[20,8,16,256]{3,2,1,0:T(8,128)(2,1)}, f32[8,4,2,16,128]{4,3,2,1,0:T(8,128)}, bf16[20,8,16,256]{3,2,1,0:T(8,128)(2,1)}, bf16[20,8,16,256]{3,2,1,0:T(8,128)(2,1)}) custom-call(f32[8,4,2,16,128]{4,3,2,1,0:T(8,128)S(1)} %bitcast.10, f32[20,8,16,256]{3,2,1,0:T(8,128)S(1)} %copy-done.3, bf16[20,8,16,256]{3,2,1,0:T(8,128)(2,1)S(1)} %copy-done.6, ...), custom_call_target="tpu_custom_call" | custom-call | tf_op jit(solution)/shard_map/activation/pallas_call | solution.py:327
  82.7 3.1 %all-to-all-start.4 = ((f32[32,32,128]{2,1,0:T(8,128)}), f32[32,32,128]{2,1,0:T(8,128)S(1)}, u32[]{:S(2)}, u32[]{:S(2)}) async-start(f32[32,32,128]{2,1,0:T(8,128)} %bitcast.15), calls=%async_computation.4 | async-start | bytes 1048576 | tf_op jit(solution)/shard_map/grad_cells_to_planes/all_to_all | solution.py:892
  85.8 0.0 copy-start.4
  85.8 1.3 copy-done.4
  87.1 0.0 copy-start.5
  87.1 1.3 copy-done.5
  88.5 6.0 %pointwise_grad.1 = (f32[20,8,16,256]{3,2,1,0:T(8,128)}, f32[8,128]{1,0:T(8,128)S(1)}) custom-call(bf16[20,8,16,256]{3,2,1,0:T(8,128)(2,1)S(1)} %copy-done, bf16[20,8,16,256]{3,2,1,0:T(8,128)(2,1)S(1)} %copy-done.4, bf16[20,8,16,256]{3,2,1,0:T(8,128)(2,1)S(1)} %copy-done.5, bf16[20,20]{1,0:T(8,128)(2,1)S(1)} %copy-done.14), custom_call_target="tpu_custom_call" | custom-call | tf_op jit(solution)/shard_map/pointwise_grad/pallas_call | solution.py:327
  94.5 6.9 %all-to-all-done.4 = f32[32,32,128]{2,1,0:T(8,128)S(1)} async-done(((f32[32,32,128]{2,1,0:T(8,128)}), f32[32,32,128]{2,1,0:T(8,128)S(1)}, u32[]{:S(2)}, u32[]{:S(2)}) %all-to-all-start.4) | async-done | bytes 524320 | tf_op jit(solution)/shard_map/grad_cells_to_planes/all_to_all | solution.py:892
  101.4 1.4 grad_plane_analysis.1
  102.8 13.3 %all_to_all.43.in_ref = f32[8,72,128]{2,1,0:T(8,128)S(1)} all-to-all(f32[8,72,128]{2,1,0:T(8,128)S(1)} %grad_plane_analysis.1), channel_id=1, replica_groups=mesh['gx'=8,'gy'=4] {'gx'}, dimensions={0} | all-to-all | bytes 589824 | tf_op jit(solution)/shard_map/grad_planes_to_modes/all_to_all | solution.py:895
  116.0 4.5 %grad_mix.1 = (f32[8,72,128]{2,1,0:T(8,128)}, f32[20,2,6,288]{3,2,1,0:T(8,128)S(1)}, f32[8,128]{1,0:T(8,128)S(1)}) custom-call(f32[8,72,128]{2,1,0:T(8,128)S(1)} %all_to_all.43.in_ref, bf16[2,20,20,6,288]{4,3,2,1,0:T(8,128)(2,1)} %copy.18.weight_ref.weight_hbm), custom_call_target="tpu_custom_call" | custom-call | tf_op jit(solution)/shard_map/grad_mix/pallas_call | solution.py:327
  120.5 3.4 %all-to-all-start.6 = ((f32[8,72,128]{2,1,0:T(8,128)}), f32[8,72,128]{2,1,0:T(8,128)S(1)}, u32[]{:S(2)}, u32[]{:S(2)}) async-start(f32[8,72,128]{2,1,0:T(8,128)} %get-tuple-element.31), calls=%async_computation.6 | async-start | bytes 589824 | tf_op jit(solution)/shard_map/grad_modes_to_planes/all_to_all | solution.py:895
  124.0 2.0 %grad_spectral.1 = (f32[2,20,20,6,288]{4,3,2,1,0:T(8,128)S(1)}, f32[8,128]{1,0:T(8,128)S(1)}) custom-call(f32[20,2,6,288]{3,2,1,0:T(8,128)S(1)} %get-tuple-element.32.spectrum_ref, f32[20,2,6,288]{3,2,1,0:T(8,128)S(1)} %get-tuple-element.33.grad_ref, f32[8,128]{1,0:T(8,128)S(1)} %get-tuple-element.34.sums_ref), custom_call_target="tpu_custom_call" | custom-call | tf_op jit(solution)/shard_map/grad_spectral/pallas_call | solution.py:621
  126.0 0.0 copy-start.1
  126.0 3.8 %copy-done.1 = f32[2,20,20,6,288]{4,3,2,1,0:T(8,128)} copy-done((f32[2,20,20,6,288]{4,3,2,1,0:T(8,128)}, f32[2,20,20,6,288]{4,3,2,1,0:T(8,128)S(1)}, u32[]{:S(2)}) %copy-start.1) | copy-done | bytes 5529624
  129.8 3.1 %all-to-all-done.6.in_ref = f32[8,72,128]{2,1,0:T(8,128)S(1)} async-done(((f32[8,72,128]{2,1,0:T(8,128)}), f32[8,72,128]{2,1,0:T(8,128)S(1)}, u32[]{:S(2)}, u32[]{:S(2)}) %all-to-all-start.6) | async-done | bytes 294944 | tf_op jit(solution)/shard_map/grad_modes_to_planes/all_to_all | solution.py:895
  132.9 2.2 %grad_plane_synthesis.1 = f32[8,4,2,16,128]{4,3,2,1,0:T(8,128)} custom-call(f32[8,72,128]{2,1,0:T(8,128)S(1)} %all-to-all-done.6.in_ref, f32[8,128]{1,0:T(8,128)S(1)} %get-tuple-element.35.extra_ref, bf16[256,256]{1,0:T(8,128)(2,1)S(1)} %copy-done.8, bf16[128,144]{1,0:T(8,128)(2,1)S(1)} %copy-done.9), custom_call_target="tpu_custom_call" | custom-call | tf_op jit(solution)/shard_map/grad_plane_synthesis/pallas_call | solution.py:327
  135.1 3.1 %all-to-all-start.7 = ((f32[32,32,128]{2,1,0:T(8,128)}), f32[32,32,128]{2,1,0:T(8,128)S(1)}, u32[]{:S(2)}, u32[]{:S(2)}) async-start(f32[32,32,128]{2,1,0:T(8,128)} %bitcast.6), calls=%async_computation.7 | async-start | bytes 1048576 | tf_op jit(solution)/shard_map/grad_planes_to_cells/all_to_all | solution.py:892
  138.2 0.0 copy-start.2
  138.2 0.0 copy-start.11
  138.2 12.1 %copy.19 = f32[2,20,20,6,288]{4,0,3,2,1:T(2,128)} copy(f32[2,20,20,6,288]{4,3,2,1,0:T(8,128)} %copy-done.1) | data formatting | bytes 11059200
  150.3 3.4 %all-to-all-done.7 = f32[32,32,128]{2,1,0:T(8,128)S(1)} async-done(((f32[32,32,128]{2,1,0:T(8,128)}), f32[32,32,128]{2,1,0:T(8,128)S(1)}, u32[]{:S(2)}, u32[]{:S(2)}) %all-to-all-start.7) | async-done | bytes 524320 | tf_op jit(solution)/shard_map/grad_planes_to_cells/all_to_all | solution.py:892
  153.7 0.0 copy-done.2
  153.7 0.0 copy-done.11
  153.7 1.7 %grad_field.1 = (bf16[20,8,16,256]{3,2,1,0:T(8,128)(2,1)}, f32[20,20]{1,0:T(8,128)}, f32[1,20]{1,0:T(1,128)}) custom-call(f32[8,4,2,16,128]{4,3,2,1,0:T(8,128)S(1)} %bitcast.9, f32[20,8,16,256]{3,2,1,0:T(8,128)S(1)} %copy-done.2, bf16[144,256]{1,0:T(8,128)(2,1)S(1)} %copy-done.11), custom_call_target="tpu_custom_call" | custom-call | tf_op jit(solution)/shard_map/grad_field/pallas_call | solution.py:327
Async XLA Ops:
  3.3 22.9 %all-to-all-start = ((f32[32,32,128]{2,1,0:T(8,128)}), f32[32,32,128]{2,1,0:T(8,128)S(1)}, u32[]{:S(2)}, u32[]{:S(2)}) async-start(f32[32,32,128]{2,1,0:T(8,128)} %bitcast.14), calls=%async_computation | async-start | bytes 1048576 | tf_op jit(solution)/shard_map/cells_to_planes/all_to_all | solution.py:892
  10.6 5.3 %copy-start = (bf16[20,8,16,256]{3,2,1,0:T(8,128)(2,1)S(1)}, bf16[20,8,16,256]{3,2,1,0:T(8,128)(2,1)}, u32[]{:S(2)}) copy-start(bf16[20,8,16,256]{3,2,1,0:T(8,128)(2,1)} %field_ref.5) | copy-start | bytes 3932164
  10.6 5.3 %copy-start.14 = (bf16[20,20]{1,0:T(8,128)(2,1)S(1)}, bf16[20,20]{1,0:T(8,128)(2,1)}, u32[]{:S(2)}) copy-start(bf16[20,20]{1,0:T(8,128)(2,1)} %map_ref.3) | copy-start | bytes 2404
  10.6 5.2 %copy-start.15 = (f32[20]{0:T(128)S(1)}, f32[20]{0:T(128)}, u32[]{:S(2)}) copy-start(f32[20]{0:T(128)} %bias_ref.1) | copy-start | bytes 244
  15.8 10.3 %copy-start.7 = (bf16[256,256]{1,0:T(8,128)(2,1)S(1)}, bf16[256,256]{1,0:T(8,128)(2,1)}, u32[]{:S(2)}) copy-start(bf16[256,256]{1,0:T(8,128)(2,1)} %constant.20.clone.y_ref) | copy-start | bytes 393220
  15.9 10.3 %copy-start.10 = (bf16[96,192]{1,0:T(8,128)(2,1)S(1)}, bf16[96,192]{1,0:T(8,128)(2,1)}, u32[]{:S(2)}) copy-start(bf16[96,192]{1,0:T(8,128)(2,1)} %constant.22.clone.x_ref) | copy-start | bytes 110596
  40.8 17.2 %copy-start.8 = (bf16[256,256]{1,0:T(8,128)(2,1)S(1)}, bf16[256,256]{1,0:T(8,128)(2,1)}, u32[]{:S(2)}) copy-start(bf16[256,256]{1,0:T(8,128)(2,1)} %constant.21.clone.y_ref) | copy-start | bytes 393220
  40.8 17.2 %copy-start.9 = (bf16[128,144]{1,0:T(8,128)(2,1)S(1)}, bf16[128,144]{1,0:T(8,128)(2,1)}, u32[]{:S(2)}) copy-start(bf16[128,144]{1,0:T(8,128)(2,1)} %constant.23.clone.x_ref) | copy-start | bytes 110596
  40.8 36.3 %copy-start.6 = (bf16[20,8,16,256]{3,2,1,0:T(8,128)(2,1)S(1)}, bf16[20,8,16,256]{3,2,1,0:T(8,128)(2,1)}, u32[]{:S(2)}) copy-start(bf16[20,8,16,256]{3,2,1,0:T(8,128)(2,1)} %cotangent_ref.1) | copy-start | bytes 3932164
  40.8 36.3 %copy-start.12 = (bf16[144,256]{1,0:T(8,128)(2,1)S(1)}, bf16[144,256]{1,0:T(8,128)(2,1)}, u32[]{:S(2)}) copy-start(bf16[144,256]{1,0:T(8,128)(2,1)} %constant.19.clone.inverse_ref) | copy-start | bytes 221188
  40.8 36.3 %copy-start.13 = (bf16[96,256]{1,0:T(8,128)(2,1)S(1)}, bf16[96,256]{1,0:T(8,128)(2,1)}, u32[]{:S(2)}) copy-start(bf16[96,256]{1,0:T(8,128)(2,1)} %constant.18.clone.forward_ref) | copy-start | bytes 147460
  44.9 32.3 %copy-start.3 = (f32[20,8,16,256]{3,2,1,0:T(8,128)S(1)}, f32[20,8,16,256]{3,2,1,0:T(8,128)}, u32[]{:S(2)}) copy-start(f32[20,8,16,256]{3,2,1,0:T(8,128)} %get-tuple-element.25.pointwise_ref) | copy-start | bytes 7864324
  82.7 18.6 %all-to-all-start.4 = ((f32[32,32,128]{2,1,0:T(8,128)}), f32[32,32,128]{2,1,0:T(8,128)S(1)}, u32[]{:S(2)}, u32[]{:S(2)}) async-start(f32[32,32,128]{2,1,0:T(8,128)} %bitcast.15), calls=%async_computation.4 | async-start | bytes 1048576 | tf_op jit(solution)/shard_map/grad_cells_to_planes/all_to_all | solution.py:892
  85.8 1.3 copy-start.4
  87.1 1.3 copy-start.5
  120.5 12.4 %all-to-all-start.6 = ((f32[8,72,128]{2,1,0:T(8,128)}), f32[8,72,128]{2,1,0:T(8,128)S(1)}, u32[]{:S(2)}, u32[]{:S(2)}) async-start(f32[8,72,128]{2,1,0:T(8,128)} %get-tuple-element.31), calls=%async_computation.6 | async-start | bytes 589824 | tf_op jit(solution)/shard_map/grad_modes_to_planes/all_to_all | solution.py:895
  126.0 3.8 %copy-start.1 = (f32[2,20,20,6,288]{4,3,2,1,0:T(8,128)}, f32[2,20,20,6,288]{4,3,2,1,0:T(8,128)S(1)}, u32[]{:S(2)}) copy-start(f32[2,20,20,6,288]{4,3,2,1,0:T(8,128)S(1)} %get-tuple-element.43) | copy-start | bytes 16588804
  135.1 18.7 %all-to-all-start.7 = ((f32[32,32,128]{2,1,0:T(8,128)}), f32[32,32,128]{2,1,0:T(8,128)S(1)}, u32[]{:S(2)}, u32[]{:S(2)}) async-start(f32[32,32,128]{2,1,0:T(8,128)} %bitcast.6), calls=%async_computation.7 | async-start | bytes 1048576 | tf_op jit(solution)/shard_map/grad_planes_to_cells/all_to_all | solution.py:892
  138.2 15.5 %copy-start.2 = (f32[20,8,16,256]{3,2,1,0:T(8,128)S(1)}, f32[20,8,16,256]{3,2,1,0:T(8,128)}, u32[]{:S(2)}) copy-start(f32[20,8,16,256]{3,2,1,0:T(8,128)} %get-tuple-element.36.back_ref) | copy-start | bytes 7864324
  138.2 15.5 %copy-start.11 = (bf16[144,256]{1,0:T(8,128)(2,1)S(1)}, bf16[144,256]{1,0:T(8,128)(2,1)}, u32[]{:S(2)}) copy-start(bf16[144,256]{1,0:T(8,128)(2,1)} %constant.17.clone.inverse_ref) | copy-start | bytes 221188

commit v4 on v3

--- a/solution.py
+++ b/solution.py
@@ -177,7 +177,7 @@
 LANES = 128
 HALF = 64
 SLOT = 32
-CHUNKS = 4
+CHUNKS = 5
 VMEM_BYTES = 20 * 1024 * 1024
 
 
@@ -260,6 +260,7 @@
             and self.width_y <= HALF
             and size_x == 8
             and self.channels % CHUNKS == 0
+            and self.channels % 4 == 0
             and self.channels <= SLOT
             and self.channels < size_x * (LANES // SLOT)
             and self.own_z * 2 * self.part_z * size_y == 2 * MZ
@@ -371,7 +372,9 @@
                 out_ref[place_x, place_y, which, plan.planes :, :] = zeros
 
 
-def depth_analysis_kernel(plan, field_ref, table_ref, out_ref, blocks_ref, held_ref, arrived):
+def depth_analysis_kernel(
+    plan, field_ref, table_ref, out_hbm, blocks_ref, held_ref, out_ref, arrived, sent
+):
     copies = [pltpu.make_async_copy(table_ref, held_ref, arrived.at[2])]
     size = plan.channels // 2
     for part in range(2):
@@ -382,6 +385,7 @@
     for copy in copies:
         copy.start()
     clear_spare(plan, out_ref)
+    leaving = []
     copies[0].wait()
     table = held_ref[...]
     for channel in range(plan.channels):
@@ -390,6 +394,9 @@
         block = blocks_ref[channel].reshape(plan.cells, plan.depth)
         both = product(table, block, NT)
         put_spectrum(plan, out_ref, channel, both[: 2 * MZ] + both[2 * MZ :])
+        leaving += send_block(plan, channel, ((out_ref, out_hbm, plan.part_z),), sent)
+    for copy in leaving:
+        copy.wait()
 
 
 def swap_blocks(values, block):
@@ -476,16 +483,21 @@
     return packed
 
 
-def unpack_rest(packed, rest_ref):
+def unpack_rest(packed, rest_ref, repeated=False):
+    lanes = lane_ids(8)
     for group in range(4):
-        rest_ref[group * 8 : (group + 1) * 8, :] = roll_lanes(packed, -group * 32)
-
-
-def take_modes(plan, in_ref, modes_ref, rest_ref):
+        turned = roll_lanes(packed, -group * 32)
+        if repeated:
+            turned = jnp.where(lanes < 32, turned, roll_lanes(turned, 32))
+            turned = jnp.where(lanes < 64, turned, roll_lanes(turned, 64))
+        rest_ref[group * 8 : (group + 1) * 8, :] = turned
+
+
+def take_modes(plan, in_ref, modes_ref, rest_ref, beside_ref=None):
     pad, size = plan.plane_rows, plan.own_z
     for place_x in range(plan.size_x):
         block, part = divmod(place_x, plan.part_z)
-        unpack_rest(in_ref[place_x, 4 * pad : 4 * pad + 8, :], rest_ref)
+        unpack_rest(in_ref[place_x, 4 * pad : 4 * pad + 8, :], rest_ref, True)
         for which in range(2):
             for inner in range(plan.own_c):
                 channel = block * plan.own_c + inner
@@ -496,10 +508,14 @@
                     modes_ref[channel, which, kz, at * LANES : (at + 1) * LANES] = in_ref[
                         place_x, begin : begin + size, :
                     ]
-                modes_ref[channel, which, kz, 2 * LANES :] = rest_ref[row : row + size, 0:32]
-
-
-def put_modes(plan, modes_ref, out_ref, rest_ref):
+                modes_ref[channel, which, kz, 2 * LANES :] = rest_ref[row : row + size, :]
+                if beside_ref is not None:
+                    group, slot = divmod(channel, 4)
+                    mine = slice(slot * 32, (slot + 1) * 32)
+                    beside_ref[group, which, kz, mine] = rest_ref[row : row + size, mine]
+
+
+def put_modes(plan, modes_ref, tail, out_ref, rest_ref):
     pad, size = plan.plane_rows, plan.own_z
     zeros = jnp.zeros((pad - plan.planes, LANES), jnp.float32)
     rest_ref[...] = jnp.zeros((2 * pad, LANES), jnp.float32)
@@ -515,109 +531,176 @@
                     out_ref[place_x, begin : begin + size, :] = modes_ref[
                         channel, which, kz, at * LANES : (at + 1) * LANES
                     ]
-                rest_ref[row : row + size, 0:32] = modes_ref[channel, which, kz, 2 * LANES :]
+                rest_ref[row : row + size, 0:32] = tail(channel, which)[kz, 0:32]
             for at in range(2):
                 begin = at * 2 * pad + which * pad + plan.planes
                 out_ref[place_x, begin : begin + pad - plan.planes, :] = zeros
         out_ref[place_x, 4 * pad : 4 * pad + 8, :] = pack_rest(rest_ref)
 
 
-def bring_weights(plan, weight_hbm, weight_ref, arrived, by_input):
-    copies = []
+def bring_weights(plan, weight_hbm, weight_ref, beside_hbm, beside_ref, arrived, by_input):
+    full = pl.ds(0, 2 * LANES)
     size = plan.channels // CHUNKS
+    copies = [pltpu.make_async_copy(beside_hbm, beside_ref, arrived.at[CHUNKS])]
     for chunk in range(CHUNKS):
         mine = pl.ds(chunk * size, size)
-        at = (slice(None), mine) if by_input else (slice(None), slice(None), mine)
+        whole = slice(None)
+        source = (whole, mine) if by_input else (whole, whole, mine)
+        source = source + (whole,) * (4 - len(source)) + (full,)
+        target = source[:4]
         copies.append(
-            pltpu.make_async_copy(weight_hbm.at[at], weight_ref.at[at], arrived.at[chunk])
+            pltpu.make_async_copy(weight_hbm.at[source], weight_ref.at[target], arrived.at[chunk])
         )
     for copy in copies:
         copy.start()
     return copies
 
 
+def add_product(sums, weight_re, weight_im, value_re, value_im, back):
+    weight_re = weight_re.astype(jnp.float32)
+    weight_im = weight_im.astype(jnp.float32)
+    if back:
+        return (
+            sums[0] + (weight_re * value_re + weight_im * value_im),
+            sums[1] + (weight_re * value_im - weight_im * value_re),
+        )
+    return (
+        sums[0] + (weight_re * value_re - weight_im * value_im),
+        sums[1] + (weight_re * value_im + weight_im * value_re),
+    )
+
+
 def mix_kernel(
-    plan, in_ref, weight_hbm, out_ref, spectrum_ref, mixed_ref, rest_ref, weight_ref, arrived
+    plan,
+    in_ref,
+    weight_hbm,
+    beside_hbm,
+    out_ref,
+    spectrum_ref,
+    mixed_ref,
+    rest_ref,
+    tails_ref,
+    weight_ref,
+    beside_ref,
+    arrived,
 ):
-    copies = bring_weights(plan, weight_hbm, weight_ref, arrived, False)
+    copies = bring_weights(plan, weight_hbm, weight_ref, beside_hbm, beside_ref, arrived, False)
     take_modes(plan, in_ref, spectrum_ref, rest_ref)
-    shape = (plan.blocks_z, plan.pair_rows)
-
-    def one(out_channel, carry):
-        real_part = jnp.zeros(shape, jnp.float32)
-        imag_part = jnp.zeros(shape, jnp.float32)
+    full, end = slice(0, 2 * LANES), slice(2 * LANES, 3 * LANES)
+    size = plan.channels // CHUNKS
+    copies[0].wait()
+    for chunk, copy in enumerate(copies[1:]):
+        copy.wait()
+        for out_channel in range(chunk * size, (chunk + 1) * size):
+            zeros = jnp.zeros((plan.blocks_z, 2 * LANES), jnp.float32)
+            sums = (zeros, zeros)
+            for channel in range(plan.channels):
+                sums = add_product(
+                    sums,
+                    weight_ref[0, channel, out_channel],
+                    weight_ref[1, channel, out_channel],
+                    spectrum_ref[channel, 0, :, full],
+                    spectrum_ref[channel, 1, :, full],
+                    False,
+                )
+            mixed_ref[out_channel, 0], mixed_ref[out_channel, 1] = sums
+    for group in range(plan.channels // 4):
+        zeros = jnp.zeros((plan.blocks_z, LANES), jnp.float32)
+        sums = (zeros, zeros)
         for channel in range(plan.channels):
-            weight_re = weight_ref[0, channel, out_channel].astype(jnp.float32)
-            weight_im = weight_ref[1, channel, out_channel].astype(jnp.float32)
-            value_re = spectrum_ref[channel, 0]
-            value_im = spectrum_ref[channel, 1]
-            real_part += weight_re * value_re - weight_im * value_im
-            imag_part += weight_re * value_im + weight_im * value_re
-        mixed_ref[out_channel, 0] = real_part
-        mixed_ref[out_channel, 1] = imag_part
-        return carry
-
-    size = plan.channels // CHUNKS
-    for chunk, copy in enumerate(copies):
-        copy.wait()
-        lax.fori_loop(chunk * size, (chunk + 1) * size, one, 0)
-    put_modes(plan, mixed_ref, out_ref, rest_ref)
+            sums = add_product(
+                sums,
+                beside_ref[0, channel, group],
+                beside_ref[1, channel, group],
+                spectrum_ref[channel, 0, :, end],
+                spectrum_ref[channel, 1, :, end],
+                False,
+            )
+        tails_ref[group, 0], tails_ref[group, 1] = sums
+
+    def tail(channel, which):
+        group, slot = divmod(channel, 4)
+        return roll_lanes(tails_ref[group, which], -slot * 32)
+
+    put_modes(plan, mixed_ref, tail, out_ref, rest_ref)
 
 
 def mix_back_kernel(
     plan,
     in_ref,
     weight_hbm,
+    beside_hbm,
     out_ref,
     grad_ref,
     sums_ref,
     mixed_ref,
     rest_ref,
+    tails_ref,
     weight_ref,
+    beside_ref,
     arrived,
+    grad_beside_ref,
 ):
-    copies = bring_weights(plan, weight_hbm, weight_ref, arrived, True)
+    copies = bring_weights(plan, weight_hbm, weight_ref, beside_hbm, beside_ref, arrived, True)
     spare = jnp.zeros((1, LANES), jnp.float32)
     for place_x in range(plan.size_x):
         spare = spare + in_ref[place_x, plan.planes : plan.planes + 1, :]
     sums_ref[...] = jnp.broadcast_to(spare, (8, LANES))
-    take_modes(plan, in_ref, grad_ref, rest_ref)
-    shape = (plan.blocks_z, plan.pair_rows)
-
-    def one(channel, carry):
-        real_part = jnp.zeros(shape, jnp.float32)
-        imag_part = jnp.zeros(shape, jnp.float32)
-        for out_channel in range(plan.channels):
-            weight_re = weight_ref[0, channel, out_channel].astype(jnp.float32)
-            weight_im = weight_ref[1, channel, out_channel].astype(jnp.float32)
-            value_re = grad_ref[out_channel, 0]
-            value_im = grad_ref[out_channel, 1]
-            real_part += weight_re * value_re + weight_im * value_im
-            imag_part += weight_re * value_im - weight_im * value_re
-        mixed_ref[channel, 0] = real_part
-        mixed_ref[channel, 1] = imag_part
-        return carry
-
+    take_modes(plan, in_ref, grad_ref, rest_ref, grad_beside_ref)
+    full = slice(0, 2 * LANES)
     size = plan.channels // CHUNKS
-    for chunk, copy in enumerate(copies):
+    copies[0].wait()
+    for chunk, copy in enumerate(copies[1:]):
         copy.wait()
-        lax.fori_loop(chunk * size, (chunk + 1) * size, one, 0)
-    put_modes(plan, mixed_ref, out_ref, rest_ref)
+        for channel in range(chunk * size, (chunk + 1) * size):
+            zeros = jnp.zeros((plan.blocks_z, 2 * LANES), jnp.float32)
+            sums = (zeros, zeros)
+            for out_channel in range(plan.channels):
+                sums = add_product(
+                    sums,
+                    weight_ref[0, channel, out_channel],
+                    weight_ref[1, channel, out_channel],
+                    grad_ref[out_channel, 0, :, full],
+                    grad_ref[out_channel, 1, :, full],
+                    True,
+                )
+            mixed_ref[channel, 0], mixed_ref[channel, 1] = sums
+            zeros = jnp.zeros((plan.blocks_z, LANES), jnp.float32)
+            sums = (zeros, zeros)
+            for group in range(plan.channels // 4):
+                sums = add_product(
+                    sums,
+                    beside_ref[0, channel, group],
+                    beside_ref[1, channel, group],
+                    grad_beside_ref[group, 0],
+                    grad_beside_ref[group, 1],
+                    True,
+                )
+            for which in range(2):
+                total = sums[which] + roll_lanes(sums[which], 64)
+                tails_ref[channel, which] = total + roll_lanes(total, 32)
+
+    def tail(channel, which):
+        return tails_ref[channel, which]
+
+    put_modes(plan, mixed_ref, tail, out_ref, rest_ref)
 
 
 def weight_grad_kernel(plan, spectrum_ref, grad_ref, sums_ref, out_ref, passed_ref):
     passed_ref[...] = sums_ref[...]
-    value_re = spectrum_ref[0, 0]
-    value_im = spectrum_ref[0, 1]
+    kept = slice(0, plan.pair_rows)
+    value_re = spectrum_ref[0, 0, :, kept]
+    value_im = spectrum_ref[0, 1, :, kept]
     for out_channel in range(plan.channels):
-        grad_re = grad_ref[out_channel, 0]
-        grad_im = grad_ref[out_channel, 1]
+        grad_re = grad_ref[out_channel, 0, :, kept]
+        grad_im = grad_ref[out_channel, 1, :, kept]
         out_ref[0, 0, out_channel] = value_re * grad_re + value_im * grad_im
         out_ref[1, 0, out_channel] = value_re * grad_im - value_im * grad_re
 
 
 def weight_grad(plan, spectrum, grad, sums):
     modes = (plan.blocks_z, plan.pair_rows)
+    wide = (plan.blocks_z, 3 * LANES)
     return pl.pallas_call(
         functools.partial(weight_grad_kernel, plan),
         grid=(plan.channels,),
@@ -626,8 +709,8 @@
             jax.ShapeDtypeStruct(sums.shape, jnp.float32),
         ],
         in_specs=[
-            pl.BlockSpec((1, 2) + modes, lambda channel: (channel, 0, 0, 0)),
-            pl.BlockSpec((plan.channels, 2) + modes, lambda channel: (0, 0, 0, 0)),
+            pl.BlockSpec((1, 2) + wide, lambda channel: (channel, 0, 0, 0)),
+            pl.BlockSpec((plan.channels, 2) + wide, lambda channel: (0, 0, 0, 0)),
             pl.BlockSpec(sums.shape, lambda channel: (0, 0)),
         ],
         out_specs=[
@@ -726,8 +809,22 @@
     return product(jnp.concatenate([high, high, low], axis=0), table, TN)
 
 
-def pointwise_kernel(plan, field_ref, map_ref, bias_ref, weight_ref, out_ref, nothing_ref):
-    del weight_ref
+def pointwise_kernel(
+    plan, field_ref, map_ref, bias_ref, weight_ref, out_ref, nothing_ref, beside_ref
+):
+    def beside(channel, carry):
+        for which in range(2):
+            for group in range(plan.channels // 4):
+                parts = [
+                    weight_ref[which, channel, group * 4 + slot, :, 2 * LANES :]
+                    for slot in range(4)
+                ]
+                beside_ref[which, channel, group] = jnp.concatenate(
+                    [part.astype(jnp.float32) for part in parts], axis=1
+                ).astype(jnp.bfloat16)
+        return carry
+
+    lax.fori_loop(0, plan.channels, beside, 0)
     nothing_ref[...] = jnp.zeros((8, LANES), jnp.float32)
     rows, size = plan.channels * plan.rows_y, plan.rows_y
     wide = widen_map(plan, map_ref[...], False)
@@ -751,16 +848,22 @@
     inverse_ref,
     forward_ref,
     output_hbm,
-    spectrum_ref,
+    spectrum_hbm,
     high_hbm,
     low_hbm,
     rows_ref,
     output_ref,
+    spectrum_ref,
     high_ref,
     low_ref,
     sent,
 ):
-    pairs = ((output_ref, output_hbm), (high_ref, high_hbm), (low_ref, low_hbm))
+    pairs = (
+        (spectrum_ref, spectrum_hbm, plan.part_z),
+        (output_ref, output_hbm, plan.own_c),
+        (high_ref, high_hbm, plan.own_c),
+        (low_ref, low_hbm, plan.own_c),
+    )
     copies = []
     clear_spare(plan, spectrum_ref)
     flat = (plan.cells, plan.depth)
@@ -772,11 +875,12 @@
         preact = synthesize_depth(plan, in_ref, rows_ref, inverse, channel)
         preact = preact + pointwise_ref[channel].reshape(flat)
         square = preact * preact
-        bend = jnp.tanh(scale * preact * (1.0 + 0.044715 * square))
-        half = 0.5 * (1.0 + bend)
-        output_ref[channel] = (preact * half).astype(jnp.bfloat16).reshape(block)
-        slope = half + (0.5 * scale) * preact * (1.0 - bend * bend) * (
-            1.0 + (3.0 * 0.044715) * square
+        bend = jnp.tanh(preact * (scale + (scale * 0.044715) * square))
+        half = 0.5 + 0.5 * bend
+        active = preact * half
+        output_ref[channel] = active.astype(jnp.bfloat16).reshape(block)
+        slope = half + active * (1.0 - half) * (
+            2.0 * scale + (6.0 * scale * 0.044715) * square
         )
         grad = cotangent_ref[channel].reshape(flat).astype(jnp.float32) * slope
         high, low = split(grad)
@@ -794,11 +898,10 @@
     block, inner = divmod(channel, plan.own_c)
     if inner < plan.own_c - 1:
         return []
-    mine = pl.ds(block * plan.own_c, plan.own_c)
-    copies = [
-        pltpu.make_async_copy(held.at[mine], target.at[mine], sent.at[at, block])
-        for at, (held, target) in enumerate(pairs)
-    ]
+    copies = []
+    for at, (held, target, size) in enumerate(pairs):
+        mine = pl.ds(block * size, size)
+        copies.append(pltpu.make_async_copy(held.at[mine], target.at[mine], sent.at[at, block]))
     for copy in copies:
         copy.start()
     return copies
@@ -881,7 +984,9 @@
     f32 = jnp.float32
     cell_shape = (plan.size_x, plan.size_y, 2, pad, LANES)
     mode_shape = (plan.size_x, 4 * pad + 8, LANES)
-    own_shape = (plan.channels, 2, plan.blocks_z, plan.pair_rows)
+    own_shape = (plan.channels, 2, plan.blocks_z, 3 * LANES)
+    groups = plan.channels // 4
+    beside_shape = (2, plan.channels, groups, plan.blocks_z, LANES)
     grid_shape = field.shape
 
     def shape(dims, kind=f32):
@@ -906,17 +1011,22 @@
     lane_rows = pltpu.VMEM((plan.full_x * pad, LANES), f32)
     lane_modes = pltpu.VMEM((plan.width_x * pad, LANES), f32)
     rest = pltpu.VMEM((2 * pad, LANES), f32)
-    own = pltpu.VMEM(own_shape, f32)
+    own_full = pltpu.VMEM(own_shape[:3] + (2 * LANES,), f32)
+    tails = pltpu.VMEM(own_shape[:3] + (LANES,), f32)
+    group_tails = pltpu.VMEM((groups,) + own_shape[1:3] + (LANES,), f32)
     lines = pltpu.VMEM((2 * MZ, LANES), f32)
     wide = plan.channels * plan.rows_y
     row_shape = shape((8, LANES))
 
-    blocks_sent = pltpu.SemaphoreType.DMA((3, plan.part_c))
+    blocks_sent = pltpu.SemaphoreType.DMA((4, plan.part_c))
 
     held_weights = [
-        pltpu.VMEM(spectral_weight.shape, spectral_weight.dtype),
-        pltpu.SemaphoreType.DMA((CHUNKS,)),
+        pltpu.VMEM(spectral_weight.shape[:4] + (2 * LANES,), spectral_weight.dtype),
+        pltpu.VMEM(beside_shape, jnp.bfloat16),
+        pltpu.SemaphoreType.DMA((CHUNKS + 1,)),
     ]
+
+    held_grid = pltpu.VMEM(grid_shape, jnp.bfloat16)
 
     def in_hbm(struct):
         return pltpu.HBM(struct.shape, struct.dtype)
@@ -953,26 +1063,28 @@
             [
                 pltpu.VMEM(grid_shape, jnp.bfloat16),
                 pltpu.VMEM(z_forward.shape, jnp.bfloat16),
+                pltpu.VMEM(cell_shape, f32),
                 pltpu.SemaphoreType.DMA((3,)),
+                blocks_sent,
             ],
             field,
             z_forward,
             hbm=(0, 1),
+            hbm_outs=(0,),
         )
     with jax.named_scope("cells_to_planes"):
         cells = cell_exchange(cells)
     with jax.named_scope("pointwise"):
         weights = with_layout_constraint(spectral_weight, Layout((0, 1, 2, 3, 4)))
-        pointwise, nothing = call(
+        pointwise, nothing, beside = call(
             with_plan(pointwise_kernel),
-            [in_hbm(shape(grid_shape)), row_shape],
+            [in_hbm(shape(grid_shape)), row_shape, in_hbm(shape(beside_shape, jnp.bfloat16))],
             [],
             field,
             pointwise_weight,
             bias,
             weights,
             smem=(2,),
-            hbm=(3,),
         )
     with jax.named_scope("plane_analysis"):
         modes = plane_analysis(cells, nothing)
@@ -982,10 +1094,11 @@
         modes, spectrum = call(
             with_plan(mix_kernel),
             [shape(mode_shape), shape(own_shape)],
-            [own, rest] + held_weights,
+            [own_full, rest, group_tails] + held_weights,
             modes,
             weights,
-            hbm=(1,),
+            beside,
+            hbm=(1, 2),
         )
     with jax.named_scope("modes_to_planes"):
         modes = mode_exchange(modes)
@@ -998,13 +1111,13 @@
         output, cells, grad_high, grad_low = call(
             with_plan(activation_kernel),
             [in_hbm(half_grid), in_hbm(shape(cell_shape)), in_hbm(half_grid), in_hbm(half_grid)],
-            [lines] + [pltpu.VMEM(grid_shape, jnp.bfloat16)] * 3 + [blocks_sent],
+            [lines, held_grid, pltpu.VMEM(cell_shape, f32), held_grid, held_grid, blocks_sent],
             cells,
             pointwise,
             cotangent,
             scaled_inverse,
             scaled_forward,
-            hbm_outs=(0, 2, 3),
+            hbm_outs=(0, 1, 2, 3),
         )
     with jax.named_scope("grad_cells_to_planes"):
         cells = cell_exchange(cells)
@@ -1026,10 +1139,11 @@
         modes, grad_mix, sums = call(
             with_plan(mix_back_kernel),
             [shape(mode_shape), shape(own_shape), row_shape],
-            [own, rest] + held_weights,
+            [own_full, rest, tails] + held_weights + [group_tails],
             modes,
             weights,
-            hbm=(1,),
+            beside,
+            hbm=(1, 2),
         )
     with jax.named_scope("grad_modes_to_planes"):
         modes = mode_exchange(modes)

time: 156 us -> 154 us (0.987)
  waiting for transfers between devices: 19.3 us -> 17.2 us
    all_to_all x3, waiting for transfers between devices: 16.2 us -> 14.1 us  [cell_exchange(): lax.all_to_all(flat, ('gx', 'gy'), 0, 0, tiled=True).reshape(cell_shape)]
    unnamed x34 -> x36, local copies, waits for them, and re-layouts: 23.8 us -> 23.8 us
  transfers between devices with their start and end apart: 4 -> 4, of which waited for: 4 -> 4; matrix products, arithmetic and copies ran while one was open for 11% -> 10% of each run, Pallas kernels for 8% -> 9%
where the time goes in v4:
time: 154 us; the launch traced here: 153 us
  blocking collectives  57.4 us (37%)
  Pallas kernels  36.4 us (24%)
  local copies, waits for them, and re-layouts  23.8 us (15%)
  waiting for transfers between devices  17.2 us (11%)
  starting transfers between devices  17.1 us (11%)
    all_to_all x3, blocking collectives, mode_exchange(): return lax.all_to_all(values, 'gx', 0, 0, tiled=True)  39.7 us
    pallas_call x11, Pallas kernels, call(): pl.pallas_call(kernel, out_shape=out_shape, in_specs=specs, out_specs=out...  34.4 us
    unnamed x36, local copies, waits for them, and re-layouts  23.8 us
    all_to_all x1, blocking collectives, cell_exchange(): lax.all_to_all(flat, ('gx', 'gy'), 0, 0, tiled=True).reshape(cell_shape)  17.8 us
    all_to_all x3, waiting for transfers between devices, cell_exchange(): lax.all_to_all(flat, ('gx', 'gy'), 0, 0, tiled=True).reshape(cell_shape)  14.1 us
    all_to_all x3, starting transfers between devices, cell_exchange(): lax.all_to_all(flat, ('gx', 'gy'), 0, 0, tiled=True).reshape(cell_shape)  13.7 us
    all_to_all x1, starting transfers between devices, mode_exchange(): return lax.all_to_all(values, 'gx', 0, 0, tiled=True)  3.43 us
    all_to_all x1, waiting for transfers between devices, mode_exchange(): return lax.all_to_all(values, 'gx', 0, 0, tiled=True)  3.12 us
  transfers between devices with their start and end apart: 4, of which 4 were waited for; matrix products, arithmetic and copies ran while one was open for 10% of the time, Pallas kernels for 9%

profile of v4, /device:TPU:0, one launch (start us, length us, event | category | flops | bytes accessed | tf_op | source)
XLA Modules:
  0.0 152.9 jit_solution(4742941841533649973)
XLA Ops:
  0.6 2.6 %depth_analysis.1 = f32[8,4,2,16,128]{4,3,2,1,0:T(8,128)} custom-call(bf16[20,8,16,256]{3,2,1,0:T(8,128)(2,1)} %field_ref.5, bf16[96,256]{1,0:T(8,128)(2,1)} %constant.16.clone.table_ref), custom_call_target="tpu_custom_call" | custom-call | tf_op jit(solution)/shard_map/depth_analysis/pallas_call | solution.py:328
  3.3 7.3 %all-to-all-start = ((f32[32,32,128]{2,1,0:T(8,128)}), f32[32,32,128]{2,1,0:T(8,128)S(1)}, u32[]{:S(2)}, u32[]{:S(2)}) async-start(f32[32,32,128]{2,1,0:T(8,128)} %bitcast.14), calls=%async_computation | async-start | bytes 1048576 | tf_op jit(solution)/shard_map/cells_to_planes/all_to_all | solution.py:997
  10.6 0.0 copy-start.1
  10.6 0.0 copy-start.15
  10.6 0.0 copy-start.16
  10.6 3.0 %copy.18.weight_ref.weight_hbm = bf16[2,20,20,6,288]{4,3,2,1,0:T(8,128)(2,1)S(1)} copy(bf16[2,20,20,6,288]{4,0,3,2,1:T(2,128)(2,1)} %param.15) | data formatting | bytes 5529600 | tf_op args[2]
  13.6 0.0 copy-done.1
  13.6 0.0 copy-done.15
  13.6 0.0 copy-done.16
  13.6 0.0 copy-start.8
  13.6 0.0 copy-start.11
  13.7 6.2 %pointwise.1 = (f32[20,8,16,256]{3,2,1,0:T(8,128)}, f32[8,128]{1,0:T(8,128)S(1)}, bf16[2,20,5,6,128]{4,3,2,1,0:T(8,128)(2,1)}) custom-call(bf16[20,8,16,256]{3,2,1,0:T(8,128)(2,1)S(1)} %copy-done.1, bf16[20,20]{1,0:T(8,128)(2,1)S(1)} %copy-done.15, f32[20]{0:T(128)S(1)} %copy-done.16, bf16[2,20,20,6,288]{4,3,2,1,0:T(8,128)(2,1)S(1)} %copy.18.weight_ref.weight_hbm), custom_call_target="tpu_custom_call" | custom-call | tf_op jit(solution)/shard_map/pointwise/pallas_call | solution.py:328
  19.9 0.0 copy-start
  19.9 2.2 %copy-done = bf16[2,20,20,6,288]{4,3,2,1,0:T(8,128)(2,1)} copy-done((bf16[2,20,20,6,288]{4,3,2,1,0:T(8,128)(2,1)}, bf16[2,20,20,6,288]{4,3,2,1,0:T(8,128)(2,1)S(1)}, u32[]{:S(2)}) %copy-start) | copy-done | bytes 2764824
  22.1 4.0 %all-to-all-done = f32[32,32,128]{2,1,0:T(8,128)S(1)} async-done(((f32[32,32,128]{2,1,0:T(8,128)}), f32[32,32,128]{2,1,0:T(8,128)S(1)}, u32[]{:S(2)}, u32[]{:S(2)}) %all-to-all-start) | async-done | bytes 524320 | tf_op jit(solution)/shard_map/cells_to_planes/all_to_all | solution.py:997
  26.1 0.0 copy-done.8
  26.1 0.0 copy-done.11
  26.1 1.4 plane_analysis.1
  27.6 13.3 %all_to_all.40.in_ref = f32[8,72,128]{2,1,0:T(8,128)S(1)} all-to-all(f32[8,72,128]{2,1,0:T(8,128)S(1)} %plane_analysis.1), channel_id=1, replica_groups=mesh['gx'=8,'gy'=4] {'gx'}, dimensions={0} | all-to-all | bytes 589824 | tf_op jit(solution)/shard_map/planes_to_modes/all_to_all | solution.py:1000
  40.8 0.0 copy-start.9
  40.8 0.0 copy-start.10
  40.8 0.0 copy-start.7
  40.8 0.0 copy-start.13
  40.8 0.0 copy-start.14
  40.9 3.2 %mix.1 = (f32[8,72,128]{2,1,0:T(8,128)S(1)}, f32[20,2,6,384]{3,2,1,0:T(8,128)S(1)}) custom-call(f32[8,72,128]{2,1,0:T(8,128)S(1)} %all_to_all.40.in_ref, bf16[2,20,20,6,288]{4,3,2,1,0:T(8,128)(2,1)} %copy-done, bf16[2,20,5,6,128]{4,3,2,1,0:T(8,128)(2,1)} %get-tuple-element.25.beside_hbm), custom_call_target="tpu_custom_call" | custom-call | tf_op jit(solution)/shard_map/mix/pallas_call | solution.py:328
  44.1 0.0 copy-start.4
  44.1 13.1 %all_to_all.41.in_ref = f32[8,72,128]{2,1,0:T(8,128)S(1)} all-to-all(f32[8,72,128]{2,1,0:T(8,128)S(1)} %get-tuple-element.26), channel_id=1, replica_groups=mesh['gx'=8,'gy'=4] {'gx'}, dimensions={0} | all-to-all | bytes 589824 | tf_op jit(solution)/shard_map/modes_to_planes/all_to_all | solution.py:1000
  57.2 0.0 copy-done.9
  57.2 0.0 copy-done.10
  57.2 1.4 plane_synthesis.1
  58.6 17.8 %all_to_all.42 = f32[32,32,128]{2,1,0:T(8,128)S(1)} all-to-all(f32[32,32,128]{2,1,0:T(8,128)S(1)} %bitcast.13), channel_id=1, replica_groups=mesh['gx'=8,'gy'=4] {'gx','gy'}, dimensions={0} | all-to-all | bytes 1048576 | tf_op jit(solution)/shard_map/planes_to_cells/all_to_all | solution.py:997
  76.3 0.0 copy-done.7
  76.3 0.0 copy-done.13
  76.3 0.0 copy-done.14
  76.4 0.0 copy-done.4
  76.4 4.7 %activation.1 = (bf16[20,8,16,256]{3,2,1,0:T(8,128)(2,1)}, f32[8,4,2,16,128]{4,3,2,1,0:T(8,128)}, bf16[20,8,16,256]{3,2,1,0:T(8,128)(2,1)}, bf16[20,8,16,256]{3,2,1,0:T(8,128)(2,1)}) custom-call(f32[8,4,2,16,128]{4,3,2,1,0:T(8,128)S(1)} %bitcast.10, f32[20,8,16,256]{3,2,1,0:T(8,128)S(1)} %copy-done.4, bf16[20,8,16,256]{3,2,1,0:T(8,128)(2,1)S(1)} %copy-done.7, ...), custom_call_target="tpu_custom_call" | custom-call | tf_op jit(solution)/shard_map/activation/pallas_call | solution.py:328
  81.1 3.3 %all-to-all-start.4 = ((f32[32,32,128]{2,1,0:T(8,128)}), f32[32,32,128]{2,1,0:T(8,128)S(1)}, u32[]{:S(2)}, u32[]{:S(2)}) async-start(f32[32,32,128]{2,1,0:T(8,128)} %bitcast.15), calls=%async_computation.4 | async-start | bytes 1048576 | tf_op jit(solution)/shard_map/grad_cells_to_planes/all_to_all | solution.py:997
  84.4 0.0 copy-start.5
  84.4 1.3 copy-done.5
  85.7 0.0 copy-start.6
  85.7 1.3 copy-done.6
  87.0 6.0 %pointwise_grad.1 = (f32[20,8,16,256]{3,2,1,0:T(8,128)}, f32[8,128]{1,0:T(8,128)S(1)}) custom-call(bf16[20,8,16,256]{3,2,1,0:T(8,128)(2,1)S(1)} %copy-done.1, bf16[20,8,16,256]{3,2,1,0:T(8,128)(2,1)S(1)} %copy-done.5, bf16[20,8,16,256]{3,2,1,0:T(8,128)(2,1)S(1)} %copy-done.6, bf16[20,20]{1,0:T(8,128)(2,1)S(1)} %copy-done.15), custom_call_target="tpu_custom_call" | custom-call | tf_op jit(solution)/shard_map/pointwise_grad/pallas_call | solution.py:328
  93.0 6.7 %all-to-all-done.4 = f32[32,32,128]{2,1,0:T(8,128)S(1)} async-done(((f32[32,32,128]{2,1,0:T(8,128)}), f32[32,32,128]{2,1,0:T(8,128)S(1)}, u32[]{:S(2)}, u32[]{:S(2)}) %all-to-all-start.4) | async-done | bytes 524320 | tf_op jit(solution)/shard_map/grad_cells_to_planes/all_to_all | solution.py:997
  99.7 1.4 grad_plane_analysis.1
  101.1 13.3 %all_to_all.43.in_ref = f32[8,72,128]{2,1,0:T(8,128)S(1)} all-to-all(f32[8,72,128]{2,1,0:T(8,128)S(1)} %grad_plane_analysis.1), channel_id=1, replica_groups=mesh['gx'=8,'gy'=4] {'gx'}, dimensions={0} | all-to-all | bytes 589824 | tf_op jit(solution)/shard_map/grad_planes_to_modes/all_to_all | solution.py:1000
  114.4 3.5 %grad_mix.1 = (f32[8,72,128]{2,1,0:T(8,128)}, f32[20,2,6,384]{3,2,1,0:T(8,128)S(1)}, f32[8,128]{1,0:T(8,128)S(1)}) custom-call(f32[8,72,128]{2,1,0:T(8,128)S(1)} %all_to_all.43.in_ref, bf16[2,20,20,6,288]{4,3,2,1,0:T(8,128)(2,1)} %copy-done, bf16[2,20,5,6,128]{4,3,2,1,0:T(8,128)(2,1)} %get-tuple-element.25.beside_hbm), custom_call_target="tpu_custom_call" | custom-call | tf_op jit(solution)/shard_map/grad_mix/pallas_call | solution.py:328
  118.0 3.4 %all-to-all-start.6 = ((f32[8,72,128]{2,1,0:T(8,128)}), f32[8,72,128]{2,1,0:T(8,128)S(1)}, u32[]{:S(2)}, u32[]{:S(2)}) async-start(f32[8,72,128]{2,1,0:T(8,128)} %get-tuple-element.33), calls=%async_computation.6 | async-start | bytes 589824 | tf_op jit(solution)/shard_map/grad_modes_to_planes/all_to_all | solution.py:1000
  121.4 2.0 %grad_spectral.1 = (f32[2,20,20,6,288]{4,3,2,1,0:T(8,128)S(1)}, f32[8,128]{1,0:T(8,128)S(1)}) custom-call(f32[20,2,6,384]{3,2,1,0:T(8,128)S(1)} %get-tuple-element.34.spectrum_ref, f32[20,2,6,384]{3,2,1,0:T(8,128)S(1)} %get-tuple-element.35.grad_ref, f32[8,128]{1,0:T(8,128)S(1)} %get-tuple-element.36.sums_ref), custom_call_target="tpu_custom_call" | custom-call | tf_op jit(solution)/shard_map/grad_spectral/pallas_call | solution.py:704
  123.4 0.0 copy-start.2
  123.5 3.8 %copy-done.2 = f32[2,20,20,6,288]{4,3,2,1,0:T(8,128)} copy-done((f32[2,20,20,6,288]{4,3,2,1,0:T(8,128)}, f32[2,20,20,6,288]{4,3,2,1,0:T(8,128)S(1)}, u32[]{:S(2)}) %copy-start.2) | copy-done | bytes 5529624
  127.2 3.1 %all-to-all-done.6.in_ref = f32[8,72,128]{2,1,0:T(8,128)S(1)} async-done(((f32[8,72,128]{2,1,0:T(8,128)}), f32[8,72,128]{2,1,0:T(8,128)S(1)}, u32[]{:S(2)}, u32[]{:S(2)}) %all-to-all-start.6) | async-done | bytes 294944 | tf_op jit(solution)/shard_map/grad_modes_to_planes/all_to_all | solution.py:1000
  130.3 2.2 %grad_plane_synthesis.1 = f32[8,4,2,16,128]{4,3,2,1,0:T(8,128)} custom-call(f32[8,72,128]{2,1,0:T(8,128)S(1)} %all-to-all-done.6.in_ref, f32[8,128]{1,0:T(8,128)S(1)} %get-tuple-element.37.extra_ref, bf16[256,256]{1,0:T(8,128)(2,1)S(1)} %copy-done.9, bf16[128,144]{1,0:T(8,128)(2,1)S(1)} %copy-done.10), custom_call_target="tpu_custom_call" | custom-call | tf_op jit(solution)/shard_map/grad_plane_synthesis/pallas_call | solution.py:328
  132.5 3.1 %all-to-all-start.7 = ((f32[32,32,128]{2,1,0:T(8,128)}), f32[32,32,128]{2,1,0:T(8,128)S(1)}, u32[]{:S(2)}, u32[]{:S(2)}) async-start(f32[32,32,128]{2,1,0:T(8,128)} %bitcast.6), calls=%async_computation.7 | async-start | bytes 1048576 | tf_op jit(solution)/shard_map/grad_planes_to_cells/all_to_all | solution.py:997
  135.6 0.0 copy-start.3
  135.7 0.0 copy-start.12
  135.7 12.1 %copy.19 = f32[2,20,20,6,288]{4,0,3,2,1:T(2,128)} copy(f32[2,20,20,6,288]{4,3,2,1,0:T(8,128)} %copy-done.2) | data formatting | bytes 11059200
  147.8 3.4 %all-to-all-done.7 = f32[32,32,128]{2,1,0:T(8,128)S(1)} async-done(((f32[32,32,128]{2,1,0:T(8,128)}), f32[32,32,128]{2,1,0:T(8,128)S(1)}, u32[]{:S(2)}, u32[]{:S(2)}) %all-to-all-start.7) | async-done | bytes 524320 | tf_op jit(solution)/shard_map/grad_planes_to_cells/all_to_all | solution.py:997
  151.2 0.0 copy-done.3
  151.2 0.0 copy-done.12
  151.2 1.7 %grad_field.1 = (bf16[20,8,16,256]{3,2,1,0:T(8,128)(2,1)}, f32[20,20]{1,0:T(8,128)}, f32[1,20]{1,0:T(1,128)}) custom-call(f32[8,4,2,16,128]{4,3,2,1,0:T(8,128)S(1)} %bitcast.9, f32[20,8,16,256]{3,2,1,0:T(8,128)S(1)} %copy-done.3, bf16[144,256]{1,0:T(8,128)(2,1)S(1)} %copy-done.12), custom_call_target="tpu_custom_call" | custom-call | tf_op jit(solution)/shard_map/grad_field/pallas_call | solution.py:328
Async XLA Ops:
  3.3 22.9 %all-to-all-start = ((f32[32,32,128]{2,1,0:T(8,128)}), f32[32,32,128]{2,1,0:T(8,128)S(1)}, u32[]{:S(2)}, u32[]{:S(2)}) async-start(f32[32,32,128]{2,1,0:T(8,128)} %bitcast.14), calls=%async_computation | async-start | bytes 1048576 | tf_op jit(solution)/shard_map/cells_to_planes/all_to_all | solution.py:997
  10.6 3.0 %copy-start.1 = (bf16[20,8,16,256]{3,2,1,0:T(8,128)(2,1)S(1)}, bf16[20,8,16,256]{3,2,1,0:T(8,128)(2,1)}, u32[]{:S(2)}) copy-start(bf16[20,8,16,256]{3,2,1,0:T(8,128)(2,1)} %field_ref.5) | copy-start | bytes 3932164
  10.6 3.0 %copy-start.15 = (bf16[20,20]{1,0:T(8,128)(2,1)S(1)}, bf16[20,20]{1,0:T(8,128)(2,1)}, u32[]{:S(2)}) copy-start(bf16[20,20]{1,0:T(8,128)(2,1)} %map_ref.3) | copy-start | bytes 2404
  10.6 3.0 %copy-start.16 = (f32[20]{0:T(128)S(1)}, f32[20]{0:T(128)}, u32[]{:S(2)}) copy-start(f32[20]{0:T(128)} %bias_ref.1) | copy-start | bytes 244
  13.6 12.5 %copy-start.8 = (bf16[256,256]{1,0:T(8,128)(2,1)S(1)}, bf16[256,256]{1,0:T(8,128)(2,1)}, u32[]{:S(2)}) copy-start(bf16[256,256]{1,0:T(8,128)(2,1)} %constant.20.clone.y_ref) | copy-start | bytes 393220
  13.6 12.5 %copy-start.11 = (bf16[96,192]{1,0:T(8,128)(2,1)S(1)}, bf16[96,192]{1,0:T(8,128)(2,1)}, u32[]{:S(2)}) copy-start(bf16[96,192]{1,0:T(8,128)(2,1)} %constant.22.clone.x_ref) | copy-start | bytes 110596
  19.9 2.2 %copy-start = (bf16[2,20,20,6,288]{4,3,2,1,0:T(8,128)(2,1)}, bf16[2,20,20,6,288]{4,3,2,1,0:T(8,128)(2,1)S(1)}, u32[]{:S(2)}) copy-start(bf16[2,20,20,6,288]{4,3,2,1,0:T(8,128)(2,1)S(1)} %copy.18.weight_ref.weight_hbm) | copy-start | bytes 8294404
  40.8 16.4 %copy-start.9 = (bf16[256,256]{1,0:T(8,128)(2,1)S(1)}, bf16[256,256]{1,0:T(8,128)(2,1)}, u32[]{:S(2)}) copy-start(bf16[256,256]{1,0:T(8,128)(2,1)} %constant.21.clone.y_ref) | copy-start | bytes 393220
  40.8 16.4 %copy-start.10 = (bf16[128,144]{1,0:T(8,128)(2,1)S(1)}, bf16[128,144]{1,0:T(8,128)(2,1)}, u32[]{:S(2)}) copy-start(bf16[128,144]{1,0:T(8,128)(2,1)} %constant.23.clone.x_ref) | copy-start | bytes 110596
  40.8 35.5 %copy-start.7 = (bf16[20,8,16,256]{3,2,1,0:T(8,128)(2,1)S(1)}, bf16[20,8,16,256]{3,2,1,0:T(8,128)(2,1)}, u32[]{:S(2)}) copy-start(bf16[20,8,16,256]{3,2,1,0:T(8,128)(2,1)} %cotangent_ref.1) | copy-start | bytes 3932164
  40.8 35.5 %copy-start.13 = (bf16[144,256]{1,0:T(8,128)(2,1)S(1)}, bf16[144,256]{1,0:T(8,128)(2,1)}, u32[]{:S(2)}) copy-start(bf16[144,256]{1,0:T(8,128)(2,1)} %constant.19.clone.inverse_ref) | copy-start | bytes 221188
  40.8 35.5 %copy-start.14 = (bf16[96,256]{1,0:T(8,128)(2,1)S(1)}, bf16[96,256]{1,0:T(8,128)(2,1)}, u32[]{:S(2)}) copy-start(bf16[96,256]{1,0:T(8,128)(2,1)} %constant.18.clone.forward_ref) | copy-start | bytes 147460
  44.1 32.3 %copy-start.4 = (f32[20,8,16,256]{3,2,1,0:T(8,128)S(1)}, f32[20,8,16,256]{3,2,1,0:T(8,128)}, u32[]{:S(2)}) copy-start(f32[20,8,16,256]{3,2,1,0:T(8,128)} %get-tuple-element.27.pointwise_ref) | copy-start | bytes 7864324
  81.1 18.6 %all-to-all-start.4 = ((f32[32,32,128]{2,1,0:T(8,128)}), f32[32,32,128]{2,1,0:T(8,128)S(1)}, u32[]{:S(2)}, u32[]{:S(2)}) async-start(f32[32,32,128]{2,1,0:T(8,128)} %bitcast.15), calls=%async_computation.4 | async-start | bytes 1048576 | tf_op jit(solution)/shard_map/grad_cells_to_planes/all_to_all | solution.py:997
  84.4 1.3 copy-start.5
  85.7 1.3 copy-start.6
  118.0 12.4 %all-to-all-start.6 = ((f32[8,72,128]{2,1,0:T(8,128)}), f32[8,72,128]{2,1,0:T(8,128)S(1)}, u32[]{:S(2)}, u32[]{:S(2)}) async-start(f32[8,72,128]{2,1,0:T(8,128)} %get-tuple-element.33), calls=%async_computation.6 | async-start | bytes 589824 | tf_op jit(solution)/shard_map/grad_modes_to_planes/all_to_all | solution.py:1000
  123.4 3.8 %copy-start.2 = (f32[2,20,20,6,288]{4,3,2,1,0:T(8,128)}, f32[2,20,20,6,288]{4,3,2,1,0:T(8,128)S(1)}, u32[]{:S(2)}) copy-start(f32[2,20,20,6,288]{4,3,2,1,0:T(8,128)S(1)} %get-tuple-element.45) | copy-start | bytes 16588804
  132.5 18.7 %all-to-all-start.7 = ((f32[32,32,128]{2,1,0:T(8,128)}), f32[32,32,128]{2,1,0:T(8,128)S(1)}, u32[]{:S(2)}, u32[]{:S(2)}) async-start(f32[32,32,128]{2,1,0:T(8,128)} %bitcast.6), calls=%async_computation.7 | async-start | bytes 1048576 | tf_op jit(solution)/shard_map/grad_planes_to_cells/all_to_all | solution.py:997
  135.6 15.5 %copy-start.3 = (f32[20,8,16,256]{3,2,1,0:T(8,128)S(1)}, f32[20,8,16,256]{3,2,1,0:T(8,128)}, u32[]{:S(2)}) copy-start(f32[20,8,16,256]{3,2,1,0:T(8,128)} %get-tuple-element.38.back_ref) | copy-start | bytes 7864324
  135.7 15.5 %copy-start.12 = (bf16[144,256]{1,0:T(8,128)(2,1)S(1)}, bf16[144,256]{1,0:T(8,128)(2,1)}, u32[]{:S(2)}) copy-start(bf16[144,256]{1,0:T(8,128)(2,1)} %constant.17.clone.inverse_ref) | copy-start | bytes 221188

commit v5 on v4

--- a/solution.py
+++ b/solution.py
@@ -258,6 +258,7 @@
             and self.pair_rows % self.width_y == 0
             and self.pair_rows == 2 * LANES + 32
             and self.width_y <= HALF
+            and 3 * max(self.full_x, self.width_x) <= 2 * LANES
             and size_x == 8
             and self.channels % CHUNKS == 0
             and self.channels % 4 == 0
@@ -308,6 +309,19 @@
             high, low = split_table(table)
             tables.append(np.concatenate([high, low, high], axis=1))
         return tables
+
+    def plane_tables(self):
+        tables = []
+        for along_y, along_x in zip(self.y_tables(), self.x_tables()):
+            rows, columns = along_x.shape
+            spare = ((0, -rows % 16), (0, 2 * LANES - columns))
+            tables.append(np.concatenate([along_y, np.pad(along_x, spare)], axis=0))
+        return tables
+
+
+def plane_products(table_ref, rows, columns):
+    across = 2 * LANES
+    return table_ref[:across], table_ref[across : across + rows, :columns]
 
 
 def call(kernel, out_shape, scratch, *operands, smem=(), hbm=(), hbm_outs=()):
@@ -357,11 +371,11 @@
         for part in range(plan.part_z):
             place_x = block * plan.part_z + part
             for which in range(2):
-                rows_ref[at : at + size, :] = in_ref[
+                rows_ref[channel, at : at + size, :] = in_ref[
                     place_x, place_y, which, inner * size : (inner + 1) * size, :
                 ]
                 at += size
-    return rows_ref[...]
+    return rows_ref[channel]
 
 
 def clear_spare(plan, out_ref):
@@ -422,8 +436,9 @@
 
 
 def plane_analysis_kernel(
-    plan, in_ref, extra_ref, y_ref, x_ref, out_ref, rows_ref, modes_ref, rest_ref
+    plan, in_ref, extra_ref, table_ref, out_ref, rows_ref, modes_ref, rest_ref
 ):
+    y_table, x_table = plane_products(table_ref, 2 * plan.width_x, 3 * plan.full_x)
     pad = plan.plane_rows
     left = [
         in_ref[:, place_y, which].reshape(plan.size_x * pad, LANES)
@@ -431,13 +446,13 @@
         for which in range(2)
     ]
     rows_ref[...] = along_y(
-        jnp.concatenate(swap_blocks(left, plan.rows_y), axis=0), y_ref[...]
+        jnp.concatenate(swap_blocks(left, plan.rows_y), axis=0), y_table
     )
     right = jnp.concatenate(
         [rows_ref[pl.ds(plane, plan.full_x, stride=pad), :] for plane in range(plan.planes)], axis=1
     )
     high, low = split(right)
-    both = product(x_ref[...], jnp.concatenate([high, high, low], axis=0))
+    both = product(x_table, jnp.concatenate([high, high, low], axis=0))
     sign = jnp.where(lane_ids(plan.width_x) < HALF, 1.0, -1.0)
     for plane in range(plan.planes):
         mine = slice(plane * LANES, (plane + 1) * LANES)
@@ -469,8 +484,8 @@
             for at in range(2):
                 row = at * 2 * pad + which * pad
                 out_ref[place_x, row : row + pad, :] = tiles[at]
-            rest_ref[which * pad : (which + 1) * pad, :] = tiles[2]
-        out_ref[place_x, 4 * pad : 4 * pad + 8, :] = pack_rest(rest_ref)
+            rest_ref[place_x, which * pad : (which + 1) * pad, :] = tiles[2]
+        out_ref[place_x, 4 * pad : 4 * pad + 8, :] = pack_rest(rest_ref.at[place_x])
         out_ref[place_x, plan.planes : plan.planes + 1, :] = extra_ref[place_x : place_x + 1, :]
 
 
@@ -497,7 +512,7 @@
     pad, size = plan.plane_rows, plan.own_z
     for place_x in range(plan.size_x):
         block, part = divmod(place_x, plan.part_z)
-        unpack_rest(in_ref[place_x, 4 * pad : 4 * pad + 8, :], rest_ref, True)
+        unpack_rest(in_ref[place_x, 4 * pad : 4 * pad + 8, :], rest_ref.at[place_x], True)
         for which in range(2):
             for inner in range(plan.own_c):
                 channel = block * plan.own_c + inner
@@ -508,17 +523,17 @@
                     modes_ref[channel, which, kz, at * LANES : (at + 1) * LANES] = in_ref[
                         place_x, begin : begin + size, :
                     ]
-                modes_ref[channel, which, kz, 2 * LANES :] = rest_ref[row : row + size, :]
+                modes_ref[channel, which, kz, 2 * LANES :] = rest_ref[place_x, row : row + size, :]
                 if beside_ref is not None:
                     group, slot = divmod(channel, 4)
                     mine = slice(slot * 32, (slot + 1) * 32)
-                    beside_ref[group, which, kz, mine] = rest_ref[row : row + size, mine]
+                    beside_ref[group, which, kz, mine] = rest_ref[place_x, row : row + size, mine]
 
 
 def put_modes(plan, modes_ref, tail, out_ref, rest_ref):
     pad, size = plan.plane_rows, plan.own_z
     zeros = jnp.zeros((pad - plan.planes, LANES), jnp.float32)
-    rest_ref[...] = jnp.zeros((2 * pad, LANES), jnp.float32)
+    rest_ref[...] = jnp.zeros(rest_ref.shape, jnp.float32)
     for place_x in range(plan.size_x):
         block, part = divmod(place_x, plan.part_z)
         for which in range(2):
@@ -531,11 +546,11 @@
                     out_ref[place_x, begin : begin + size, :] = modes_ref[
                         channel, which, kz, at * LANES : (at + 1) * LANES
                     ]
-                rest_ref[row : row + size, 0:32] = tail(channel, which)[kz, 0:32]
+                rest_ref[place_x, row : row + size, 0:32] = tail(channel, which)[kz, 0:32]
             for at in range(2):
                 begin = at * 2 * pad + which * pad + plan.planes
                 out_ref[place_x, begin : begin + pad - plan.planes, :] = zeros
-        out_ref[place_x, 4 * pad : 4 * pad + 8, :] = pack_rest(rest_ref)
+        out_ref[place_x, 4 * pad : 4 * pad + 8, :] = pack_rest(rest_ref.at[place_x])
 
 
 def bring_weights(plan, weight_hbm, weight_ref, beside_hbm, beside_ref, arrived, by_input):
@@ -576,16 +591,20 @@
     weight_hbm,
     beside_hbm,
     out_ref,
-    spectrum_ref,
+    spectrum_hbm,
     mixed_ref,
     rest_ref,
     tails_ref,
     weight_ref,
     beside_ref,
     arrived,
+    spectrum_ref,
+    sent,
 ):
     copies = bring_weights(plan, weight_hbm, weight_ref, beside_hbm, beside_ref, arrived, False)
     take_modes(plan, in_ref, spectrum_ref, rest_ref)
+    leaving = pltpu.make_async_copy(spectrum_ref, spectrum_hbm, sent)
+    leaving.start()
     full, end = slice(0, 2 * LANES), slice(2 * LANES, 3 * LANES)
     size = plan.channels // CHUNKS
     copies[0].wait()
@@ -623,6 +642,7 @@
         return roll_lanes(tails_ref[group, which], -slot * 32)
 
     put_modes(plan, mixed_ref, tail, out_ref, rest_ref)
+    leaving.wait()
 
 
 def mix_back_kernel(
@@ -631,7 +651,7 @@
     weight_hbm,
     beside_hbm,
     out_ref,
-    grad_ref,
+    grad_hbm,
     sums_ref,
     mixed_ref,
     rest_ref,
@@ -640,6 +660,8 @@
     beside_ref,
     arrived,
     grad_beside_ref,
+    grad_ref,
+    sent,
 ):
     copies = bring_weights(plan, weight_hbm, weight_ref, beside_hbm, beside_ref, arrived, True)
     spare = jnp.zeros((1, LANES), jnp.float32)
@@ -647,6 +669,8 @@
         spare = spare + in_ref[place_x, plan.planes : plan.planes + 1, :]
     sums_ref[...] = jnp.broadcast_to(spare, (8, LANES))
     take_modes(plan, in_ref, grad_ref, rest_ref, grad_beside_ref)
+    leaving = pltpu.make_async_copy(grad_ref, grad_hbm, sent)
+    leaving.start()
     full = slice(0, 2 * LANES)
     size = plan.channels // CHUNKS
     copies[0].wait()
@@ -684,50 +708,57 @@
         return tails_ref[channel, which]
 
     put_modes(plan, mixed_ref, tail, out_ref, rest_ref)
-
-
-def weight_grad_kernel(plan, spectrum_ref, grad_ref, sums_ref, out_ref, passed_ref):
-    passed_ref[...] = sums_ref[...]
+    leaving.wait()
+
+
+def weight_grad_kernel(plan, spectrum_ref, grad_ref, before_ref, out_ref, after_ref):
+    after_ref[...] = before_ref[...]
     kept = slice(0, plan.pair_rows)
-    value_re = spectrum_ref[0, 0, :, kept]
-    value_im = spectrum_ref[0, 1, :, kept]
-    for out_channel in range(plan.channels):
-        grad_re = grad_ref[out_channel, 0, :, kept]
-        grad_im = grad_ref[out_channel, 1, :, kept]
-        out_ref[0, 0, out_channel] = value_re * grad_re + value_im * grad_im
-        out_ref[1, 0, out_channel] = value_re * grad_im - value_im * grad_re
-
-
-def weight_grad(plan, spectrum, grad, sums):
-    modes = (plan.blocks_z, plan.pair_rows)
+    for channel in range(spectrum_ref.shape[0]):
+        for out_channel in range(plan.channels):
+            for kz in range(plan.blocks_z):
+                row = slice(kz, kz + 1)
+                value_re = spectrum_ref[channel, 0, row, kept]
+                value_im = spectrum_ref[channel, 1, row, kept]
+                grad_re = grad_ref[out_channel, 0, row, kept]
+                grad_im = grad_ref[out_channel, 1, row, kept]
+                out_ref[channel, out_channel, kz, 0:1, :] = value_re * grad_re + value_im * grad_im
+                out_ref[channel, out_channel, kz, 1:2, :] = value_re * grad_im - value_im * grad_re
+
+
+def weight_grad(plan, spectrum, grad, before):
+    own = (plan.blocks_z, 2, plan.pair_rows)
     wide = (plan.blocks_z, 3 * LANES)
-    return pl.pallas_call(
+    step = 4
+    rows, after = pl.pallas_call(
         functools.partial(weight_grad_kernel, plan),
-        grid=(plan.channels,),
+        grid=(plan.channels // step,),
         out_shape=[
-            jax.ShapeDtypeStruct((2, plan.channels, plan.channels) + modes, jnp.float32),
-            jax.ShapeDtypeStruct(sums.shape, jnp.float32),
+            pltpu.HBM((plan.channels, plan.channels) + own, jnp.float32),
+            jax.ShapeDtypeStruct(before.shape, before.dtype),
         ],
         in_specs=[
-            pl.BlockSpec((1, 2) + wide, lambda channel: (channel, 0, 0, 0)),
-            pl.BlockSpec((plan.channels, 2) + wide, lambda channel: (0, 0, 0, 0)),
-            pl.BlockSpec(sums.shape, lambda channel: (0, 0)),
+            pl.BlockSpec((step, 2) + wide, lambda at: (at, 0, 0, 0)),
+            pl.BlockSpec((plan.channels, 2) + wide, lambda at: (0, 0, 0, 0)),
+            pl.BlockSpec(before.shape, lambda at: (0, 0)),
         ],
         out_specs=[
-            pl.BlockSpec((2, 1, plan.channels) + modes, lambda channel: (0, channel, 0, 0, 0)),
-            pl.BlockSpec(sums.shape, lambda channel: (0, 0)),
+            pl.BlockSpec((step, plan.channels) + own, lambda at: (at, 0, 0, 0, 0)),
+            pl.BlockSpec(before.shape, lambda at: (0, 0)),
         ],
         compiler_params=pltpu.CompilerParams(vmem_limit_bytes=VMEM_BYTES),
-    )(spectrum, grad, sums)
+    )(spectrum, grad, before)
+    return jnp.transpose(rows, (3, 0, 1, 2, 4)), after
 
 
 def plane_synthesis_kernel(
-    plan, in_ref, extra_ref, y_ref, x_ref, out_ref, rows_ref, modes_ref, rest_ref
+    plan, in_ref, extra_ref, table_ref, out_ref, rows_ref, modes_ref, rest_ref
 ):
+    y_table, x_table = plane_products(table_ref, 2 * plan.full_x, 3 * plan.width_x)
     pad, width = plan.plane_rows, plan.width_y
     lanes = lane_ids(pad)
     for place_x in range(plan.size_x):
-        unpack_rest(in_ref[place_x, 4 * pad : 4 * pad + 8, :], rest_ref)
+        unpack_rest(in_ref[place_x, 4 * pad : 4 * pad + 8, :], rest_ref.at[place_x])
         tiles = []
         for which in range(2):
             row = which * pad
@@ -735,7 +766,7 @@
                 [
                     in_ref[place_x, row : row + pad, :],
                     in_ref[place_x, 2 * pad + row : 3 * pad + row, :],
-                    rest_ref[row : row + pad, :],
+                    rest_ref[place_x, row : row + pad, :],
                 ]
             )
         for inner in range(plan.own_kx):
@@ -757,7 +788,7 @@
         axis=1,
     )
     high, low = split(right)
-    both = product(x_ref[...], jnp.concatenate([high, high, low], axis=0))
+    both = product(x_table, jnp.concatenate([high, high, low], axis=0))
     sign = jnp.where(lane_ids(plan.full_x) < HALF, -1.0, 1.0)
     for plane in range(plan.planes):
         mine = slice(plane * LANES, (plane + 1) * LANES)
@@ -768,7 +799,7 @@
     rows_ref[pl.ds(plan.planes, plan.full_x, stride=pad), :] = jnp.zeros(
         (plan.full_x, LANES), jnp.float32
     )
-    cells = along_y(rows_ref[...], y_ref[...])
+    cells = along_y(rows_ref[...], y_table)
     size = plan.size_x * pad
     cells = swap_blocks(
         [cells[row * size : (row + 1) * size] for row in range(plan.rows_x)], plan.rows_y
@@ -803,10 +834,10 @@
     )
 
 
-def synthesize_depth(plan, in_ref, rows_ref, table, channel):
+def depth_rows(plan, in_ref, rows_ref, channel):
     rows = take_spectrum(plan, in_ref, rows_ref, channel)
     high, low = split(rows)
-    return product(jnp.concatenate([high, high, low], axis=0), table, TN)
+    return jnp.concatenate([high, high, low], axis=0)
 
 
 def pointwise_kernel(
@@ -872,8 +903,14 @@
     forward = forward_ref[...]
     scale = math.sqrt(2.0 / math.pi)
     for channel in range(plan.channels):
-        preact = synthesize_depth(plan, in_ref, rows_ref, inverse, channel)
-        preact = preact + pointwise_ref[channel].reshape(flat)
+        if channel % plan.own_c == 0:
+            left = [
+                depth_rows(plan, in_ref, rows_ref, channel + inner)
+                for inner in range(plan.own_c)
+            ]
+            conv = product(jnp.concatenate(left, axis=1), inverse, TN)
+        first = channel % plan.own_c * plan.cells
+        preact = conv[first : first + plan.cells] + pointwise_ref[channel].reshape(flat)
         square = preact * preact
         bend = jnp.tanh(preact * (scale + (scale * 0.044715) * square))
         half = 0.5 + 0.5 * bend
@@ -961,7 +998,7 @@
     flat = (plan.cells, plan.depth)
     inverse = inverse_ref[...]
     for channel in range(plan.channels):
-        total = synthesize_depth(plan, in_ref, rows_ref, inverse, channel)
+        total = product(depth_rows(plan, in_ref, rows_ref, channel), inverse, TN)
         total = total + back_ref[channel].reshape(flat)
         grad_ref[channel] = total.astype(jnp.bfloat16).reshape(block)
     shrink = float(plan.full_x * plan.full_y * plan.depth) ** (-0.5)
@@ -1005,16 +1042,15 @@
     z_inverse = jnp.asarray(np.concatenate([z_high, z_low, z_high]))
     scaled_forward = jnp.asarray(np.concatenate([scaled_high, scaled_low]))
     scaled_inverse = jnp.asarray(np.concatenate([scaled_high, scaled_low, scaled_high]))
-    y_forward, y_inverse = (jnp.asarray(table) for table in plan.y_tables())
-    x_forward, x_inverse = (jnp.asarray(table) for table in plan.x_tables())
+    forward_table, inverse_table = (jnp.asarray(table) for table in plan.plane_tables())
 
     lane_rows = pltpu.VMEM((plan.full_x * pad, LANES), f32)
     lane_modes = pltpu.VMEM((plan.width_x * pad, LANES), f32)
-    rest = pltpu.VMEM((2 * pad, LANES), f32)
+    rest = pltpu.VMEM((plan.size_x, 2 * pad, LANES), f32)
     own_full = pltpu.VMEM(own_shape[:3] + (2 * LANES,), f32)
     tails = pltpu.VMEM(own_shape[:3] + (LANES,), f32)
     group_tails = pltpu.VMEM((groups,) + own_shape[1:3] + (LANES,), f32)
-    lines = pltpu.VMEM((2 * MZ, LANES), f32)
+    lines = pltpu.VMEM((plan.channels, 2 * MZ, LANES), f32)
     wide = plan.channels * plan.rows_y
     row_shape = shape((8, LANES))
 
@@ -1041,8 +1077,7 @@
             [lane_rows, lane_modes, rest],
             cells,
             extra,
-            y_forward,
-            x_forward,
+            forward_table,
         )
 
     def plane_synthesis(modes, extra):
@@ -1052,8 +1087,7 @@
             [lane_rows, lane_modes, rest],
             modes,
             extra,
-            y_inverse,
-            x_inverse,
+            inverse_table,
         )
 
     with jax.named_scope("depth_analysis"):
@@ -1093,12 +1127,15 @@
     with jax.named_scope("mix"):
         modes, spectrum = call(
             with_plan(mix_kernel),
-            [shape(mode_shape), shape(own_shape)],
-            [own_full, rest, group_tails] + held_weights,
+            [shape(mode_shape), in_hbm(shape(own_shape))],
+            [own_full, rest, group_tails]
+            + held_weights
+            + [pltpu.VMEM(own_shape, f32), pltpu.SemaphoreType.DMA],
             modes,
             weights,
             beside,
             hbm=(1, 2),
+            hbm_outs=(1,),
         )
     with jax.named_scope("modes_to_planes"):
         modes = mode_exchange(modes)
@@ -1138,12 +1175,15 @@
     with jax.named_scope("grad_mix"):
         modes, grad_mix, sums = call(
             with_plan(mix_back_kernel),
-            [shape(mode_shape), shape(own_shape), row_shape],
-            [own_full, rest, tails] + held_weights + [group_tails],
+            [in_hbm(shape(mode_shape)), in_hbm(shape(own_shape)), row_shape],
+            [own_full, rest, tails]
+            + held_weights
+            + [group_tails, pltpu.VMEM(own_shape, f32), pltpu.SemaphoreType.DMA],
             modes,
             weights,
             beside,
             hbm=(1, 2),
+            hbm_outs=(1,),
         )
     with jax.named_scope("grad_modes_to_planes"):
         modes = mode_exchange(modes)

time: 154 us -> 153 us (level)
  blocking collectives: 57.4 us -> 76.6 us
  local copies, waits for them, and re-layouts: 23.8 us -> 9.95 us
  waiting for transfers between devices: 17.2 us -> 12.6 us
  starting transfers between devices: 17.1 us -> 14 us
  Pallas kernels: 36.4 us -> 38.1 us
    all_to_all x1 -> x2, blocking collectives: 17.8 us -> 36.9 us  [cell_exchange(): lax.all_to_all(flat, ('gx', 'gy'), 0, 0, tiled=True).reshape(cell_shape)]
    unnamed x36 -> x33, local copies, waits for them, and re-layouts: 23.8 us -> 9.95 us
    all_to_all x3 -> x2, waiting for transfers between devices: 14.1 us -> 10.7 us  [cell_exchange(): lax.all_to_all(flat, ('gx', 'gy'), 0, 0, tiled=True).reshape(cell_shape)]
    all_to_all x3 -> x2, starting transfers between devices: 13.7 us -> 10.6 us  [cell_exchange(): lax.all_to_all(flat, ('gx', 'gy'), 0, 0, tiled=True).reshape(cell_shape)]
    pallas_call x1, Pallas kernels: 2.02 us -> 4.96 us  [weight_grad(): pl.pallas_call(functools.partial(weight_grad_kernel, plan), grid=(plan.ch...]
  transfers between devices with their start and end apart: 4 -> 3, of which waited for: 4 -> 3; matrix products, arithmetic and copies ran while one was open for 10% -> 2% of each run, Pallas kernels for 9% -> 11%
where the time goes in v5:
time: 153 us; the launch traced here: 152 us
  blocking collectives  76.6 us (50%)
  Pallas kernels  38.1 us (25%)
  starting transfers between devices  14 us (9%)
  waiting for transfers between devices  12.6 us (8%)
  local copies, waits for them, and re-layouts  9.95 us (7%)
    all_to_all x3, blocking collectives, mode_exchange(): return lax.all_to_all(values, 'gx', 0, 0, tiled=True)  39.7 us
    all_to_all x2, blocking collectives, cell_exchange(): lax.all_to_all(flat, ('gx', 'gy'), 0, 0, tiled=True).reshape(cell_shape)  36.9 us
    pallas_call x11, Pallas kernels, call(): pl.pallas_call(kernel, out_shape=out_shape, in_specs=specs, out_specs=out...  33.1 us
    all_to_all x2, waiting for transfers between devices, cell_exchange(): lax.all_to_all(flat, ('gx', 'gy'), 0, 0, tiled=True).reshape(cell_shape)  10.7 us
    all_to_all x2, starting transfers between devices, cell_exchange(): lax.all_to_all(flat, ('gx', 'gy'), 0, 0, tiled=True).reshape(cell_shape)  10.6 us
    unnamed x33, local copies, waits for them, and re-layouts  9.95 us
    pallas_call x1, Pallas kernels, weight_grad(): pl.pallas_call(functools.partial(weight_grad_kernel, plan), grid=(plan.ch...  4.96 us
    all_to_all x1, starting transfers between devices, mode_exchange(): return lax.all_to_all(values, 'gx', 0, 0, tiled=True)  3.43 us
  transfers between devices with their start and end apart: 3, of which 3 were waited for; matrix products, arithmetic and copies ran while one was open for 2% of the time, Pallas kernels for 11%

profile of v5, /device:TPU:0, one launch (start us, length us, event | category | flops | bytes accessed | tf_op | source)
XLA Modules:
  0.0 152.1 jit_solution(6811846455014232869)
XLA Ops:
  0.6 2.6 %depth_analysis.1 = f32[8,4,2,16,128]{4,3,2,1,0:T(8,128)} custom-call(bf16[20,8,16,256]{3,2,1,0:T(8,128)(2,1)} %field_ref.5, bf16[96,256]{1,0:T(8,128)(2,1)} %constant.12.clone.table_ref), custom_call_target="tpu_custom_call" | custom-call | tf_op jit(solution)/shard_map/depth_analysis/pallas_call | solution.py:342
  3.3 7.3 %all-to-all-start = ((f32[32,32,128]{2,1,0:T(8,128)}), f32[32,32,128]{2,1,0:T(8,128)S(1)}, u32[]{:S(2)}, u32[]{:S(2)}) async-start(f32[32,32,128]{2,1,0:T(8,128)} %bitcast.16), calls=%async_computation | async-start | bytes 1048576 | tf_op jit(solution)/shard_map/cells_to_planes/all_to_all | solution.py:1034
  10.6 0.0 copy-start.1
  10.6 0.0 copy-start.14
  10.6 0.0 copy-start.15
  10.6 3.0 %copy.16.weight_ref.weight_hbm = bf16[2,20,20,6,288]{4,3,2,1,0:T(8,128)(2,1)S(1)} copy(bf16[2,20,20,6,288]{4,0,3,2,1:T(2,128)(2,1)} %param.13) | data formatting | bytes 5529600 | tf_op args[2]
  13.6 0.0 copy-done.1
  13.6 0.0 copy-done.14
  13.6 0.0 copy-done.15
  13.6 0.0 copy-start.8
  13.6 6.2 %pointwise.1 = (f32[20,8,16,256]{3,2,1,0:T(8,128)}, f32[8,128]{1,0:T(8,128)S(1)}, bf16[2,20,5,6,128]{4,3,2,1,0:T(8,128)(2,1)}) custom-call(bf16[20,8,16,256]{3,2,1,0:T(8,128)(2,1)S(1)} %copy-done.1, bf16[20,20]{1,0:T(8,128)(2,1)S(1)} %copy-done.14, f32[20]{0:T(128)S(1)} %copy-done.15, bf16[2,20,20,6,288]{4,3,2,1,0:T(8,128)(2,1)S(1)} %copy.16.weight_ref.weight_hbm), custom_call_target="tpu_custom_call" | custom-call | tf_op jit(solution)/shard_map/pointwise/pallas_call | solution.py:342
  19.8 0.0 copy-start
  19.8 2.2 %copy-done = bf16[2,20,20,6,288]{4,3,2,1,0:T(8,128)(2,1)} copy-done((bf16[2,20,20,6,288]{4,3,2,1,0:T(8,128)(2,1)}, bf16[2,20,20,6,288]{4,3,2,1,0:T(8,128)(2,1)S(1)}, u32[]{:S(2)}) %copy-start) | copy-done | bytes 2764824
  22.1 4.0 %all-to-all-done = f32[32,32,128]{2,1,0:T(8,128)S(1)} async-done(((f32[32,32,128]{2,1,0:T(8,128)}), f32[32,32,128]{2,1,0:T(8,128)S(1)}, u32[]{:S(2)}, u32[]{:S(2)}) %all-to-all-start) | async-done | bytes 524320 | tf_op jit(solution)/shard_map/cells_to_planes/all_to_all | solution.py:1034
  26.1 0.0 copy-done.8
  26.1 1.4 plane_analysis.1
  27.6 13.3 %all_to_all.40.in_ref = f32[8,72,128]{2,1,0:T(8,128)S(1)} all-to-all(f32[8,72,128]{2,1,0:T(8,128)S(1)} %plane_analysis.1), channel_id=1, replica_groups=mesh['gx'=8,'gy'=4] {'gx'}, dimensions={0} | all-to-all | bytes 589824 | tf_op jit(solution)/shard_map/planes_to_modes/all_to_all | solution.py:1037
  40.8 0.0 copy-start.7
  40.8 0.0 copy-start.6
  40.8 0.0 copy-start.12
  40.8 0.0 copy-start.13
  40.8 3.4 %mix.1 = (f32[8,72,128]{2,1,0:T(8,128)S(1)}, f32[20,2,6,384]{3,2,1,0:T(8,128)}) custom-call(f32[8,72,128]{2,1,0:T(8,128)S(1)} %all_to_all.40.in_ref, bf16[2,20,20,6,288]{4,3,2,1,0:T(8,128)(2,1)} %copy-done, bf16[2,20,5,6,128]{4,3,2,1,0:T(8,128)(2,1)} %get-tuple-element.25.beside_hbm), custom_call_target="tpu_custom_call" | custom-call | tf_op jit(solution)/shard_map/mix/pallas_call | solution.py:342
  44.2 0.0 copy-start.3
  44.2 13.1 %all_to_all.41.in_ref = f32[8,72,128]{2,1,0:T(8,128)S(1)} all-to-all(f32[8,72,128]{2,1,0:T(8,128)S(1)} %get-tuple-element.26), channel_id=1, replica_groups=mesh['gx'=8,'gy'=4] {'gx'}, dimensions={0} | all-to-all | bytes 589824 | tf_op jit(solution)/shard_map/modes_to_planes/all_to_all | solution.py:1037
  57.4 0.0 copy-done.7
  57.4 1.4 plane_synthesis.1
  58.7 17.8 %all_to_all.42 = f32[32,32,128]{2,1,0:T(8,128)S(1)} all-to-all(f32[32,32,128]{2,1,0:T(8,128)S(1)} %bitcast.15), channel_id=1, replica_groups=mesh['gx'=8,'gy'=4] {'gx','gy'}, dimensions={0} | all-to-all | bytes 1048576 | tf_op jit(solution)/shard_map/planes_to_cells/all_to_all | solution.py:1034
  76.5 0.0 copy-done.6
  76.5 0.0 copy-done.12
  76.5 0.0 copy-done.13
  76.5 0.0 copy-done.3
  76.5 3.9 %activation.1 = (bf16[20,8,16,256]{3,2,1,0:T(8,128)(2,1)}, f32[8,4,2,16,128]{4,3,2,1,0:T(8,128)}, bf16[20,8,16,256]{3,2,1,0:T(8,128)(2,1)}, bf16[20,8,16,256]{3,2,1,0:T(8,128)(2,1)}) custom-call(f32[8,4,2,16,128]{4,3,2,1,0:T(8,128)S(1)} %bitcast.10, f32[20,8,16,256]{3,2,1,0:T(8,128)S(1)} %copy-done.3, bf16[20,8,16,256]{3,2,1,0:T(8,128)(2,1)S(1)} %copy-done.6, ...), custom_call_target="tpu_custom_call" | custom-call | tf_op jit(solution)/shard_map/activation/pallas_call | solution.py:342
  80.4 3.3 %all-to-all-start.4 = ((f32[32,32,128]{2,1,0:T(8,128)}), f32[32,32,128]{2,1,0:T(8,128)S(1)}, u32[]{:S(2)}, u32[]{:S(2)}) async-start(f32[32,32,128]{2,1,0:T(8,128)} %bitcast.17), calls=%async_computation.4 | async-start | bytes 1048576 | tf_op jit(solution)/shard_map/grad_cells_to_planes/all_to_all | solution.py:1034
  83.7 0.0 copy-start.4
  83.7 1.3 copy-done.4
  85.0 0.0 copy-start.5
  85.0 1.3 copy-done.5
  86.3 6.1 %pointwise_grad.1 = (f32[20,8,16,256]{3,2,1,0:T(8,128)}, f32[8,128]{1,0:T(8,128)S(1)}) custom-call(bf16[20,8,16,256]{3,2,1,0:T(8,128)(2,1)S(1)} %copy-done.1, bf16[20,8,16,256]{3,2,1,0:T(8,128)(2,1)S(1)} %copy-done.4, bf16[20,8,16,256]{3,2,1,0:T(8,128)(2,1)S(1)} %copy-done.5, bf16[20,20]{1,0:T(8,128)(2,1)S(1)} %copy-done.14), custom_call_target="tpu_custom_call" | custom-call | tf_op jit(solution)/shard_map/pointwise_grad/pallas_call | solution.py:342
  92.4 6.7 %all-to-all-done.4 = f32[32,32,128]{2,1,0:T(8,128)S(1)} async-done(((f32[32,32,128]{2,1,0:T(8,128)}), f32[32,32,128]{2,1,0:T(8,128)S(1)}, u32[]{:S(2)}, u32[]{:S(2)}) %all-to-all-start.4) | async-done | bytes 524320 | tf_op jit(solution)/shard_map/grad_cells_to_planes/all_to_all | solution.py:1034
  99.1 1.4 grad_plane_analysis.1
  100.5 13.3 %all_to_all.43.in_ref = f32[8,72,128]{2,1,0:T(8,128)S(1)} all-to-all(f32[8,72,128]{2,1,0:T(8,128)S(1)} %grad_plane_analysis.1), channel_id=1, replica_groups=mesh['gx'=8,'gy'=4] {'gx'}, dimensions={0} | all-to-all | bytes 589824 | tf_op jit(solution)/shard_map/grad_planes_to_modes/all_to_all | solution.py:1037
  113.8 3.8 %grad_mix.1 = (f32[8,72,128]{2,1,0:T(8,128)}, f32[20,2,6,384]{3,2,1,0:T(8,128)}, f32[8,128]{1,0:T(8,128)S(1)}) custom-call(f32[8,72,128]{2,1,0:T(8,128)S(1)} %all_to_all.43.in_ref, bf16[2,20,20,6,288]{4,3,2,1,0:T(8,128)(2,1)} %copy-done, bf16[2,20,5,6,128]{4,3,2,1,0:T(8,128)(2,1)} %get-tuple-element.25.beside_hbm), custom_call_target="tpu_custom_call" | custom-call | tf_op jit(solution)/shard_map/grad_mix/pallas_call | solution.py:342
  117.5 3.4 %all-to-all-start.6 = ((f32[8,72,128]{2,1,0:T(8,128)}), f32[8,72,128]{2,1,0:T(8,128)S(1)}, u32[]{:S(2)}, u32[]{:S(2)}) async-start(f32[8,72,128]{2,1,0:T(8,128)} %get-tuple-element.33), calls=%async_computation.6 | async-start | bytes 589824 | tf_op jit(solution)/shard_map/grad_modes_to_planes/all_to_all | solution.py:1037
  121.0 0.0 copy-start.9
  121.0 1.0 copy-done.9
  122.0 0.0 copy-start.10
  122.0 1.0 copy-done.10
  123.0 0.0 copy-start.2
  123.0 0.0 copy-start.11
  123.0 5.0 %grad_spectral.1 = (f32[20,20,6,2,288]{4,3,2,1,0:T(2,128)}, f32[8,128]{1,0:T(8,128)S(1)}) custom-call(f32[20,2,6,384]{3,2,1,0:T(8,128)S(1)} %copy-done.9, f32[20,2,6,384]{3,2,1,0:T(8,128)S(1)} %copy-done.10, f32[8,128]{1,0:T(8,128)S(1)} %get-tuple-element.36.before_ref), custom_call_target="tpu_custom_call" | custom-call | tf_op jit(solution)/shard_map/grad_spectral/pallas_call | solution.py:733
  128.0 1.9 %all-to-all-done.6.in_ref = f32[8,72,128]{2,1,0:T(8,128)S(1)} async-done(((f32[8,72,128]{2,1,0:T(8,128)}), f32[8,72,128]{2,1,0:T(8,128)S(1)}, u32[]{:S(2)}, u32[]{:S(2)}) %all-to-all-start.6) | async-done | bytes 294944 | tf_op jit(solution)/shard_map/grad_modes_to_planes/all_to_all | solution.py:1037
  129.9 1.4 grad_plane_synthesis.1
  131.3 19.1 %all_to_all.44 = f32[32,32,128]{2,1,0:T(8,128)S(1)} all-to-all(f32[32,32,128]{2,1,0:T(8,128)S(1)} %bitcast.14), channel_id=1, replica_groups=mesh['gx'=8,'gy'=4] {'gx','gy'}, dimensions={0} | all-to-all | bytes 1048576 | tf_op jit(solution)/shard_map/grad_planes_to_cells/all_to_all | solution.py:1034
  150.4 0.0 copy-done.2
  150.4 0.0 copy-done.11
  150.4 1.6 %grad_field.1 = (bf16[20,8,16,256]{3,2,1,0:T(8,128)(2,1)}, f32[20,20]{1,0:T(8,128)}, f32[1,20]{1,0:T(1,128)}) custom-call(f32[8,4,2,16,128]{4,3,2,1,0:T(8,128)S(1)} %bitcast.11, f32[20,8,16,256]{3,2,1,0:T(8,128)S(1)} %copy-done.2, bf16[144,256]{1,0:T(8,128)(2,1)S(1)} %copy-done.11), custom_call_target="tpu_custom_call" | custom-call | tf_op jit(solution)/shard_map/grad_field/pallas_call | solution.py:342
Async XLA Ops:
  3.3 22.9 %all-to-all-start = ((f32[32,32,128]{2,1,0:T(8,128)}), f32[32,32,128]{2,1,0:T(8,128)S(1)}, u32[]{:S(2)}, u32[]{:S(2)}) async-start(f32[32,32,128]{2,1,0:T(8,128)} %bitcast.16), calls=%async_computation | async-start | bytes 1048576 | tf_op jit(solution)/shard_map/cells_to_planes/all_to_all | solution.py:1034
  10.6 3.0 %copy-start.1 = (bf16[20,8,16,256]{3,2,1,0:T(8,128)(2,1)S(1)}, bf16[20,8,16,256]{3,2,1,0:T(8,128)(2,1)}, u32[]{:S(2)}) copy-start(bf16[20,8,16,256]{3,2,1,0:T(8,128)(2,1)} %field_ref.5) | copy-start | bytes 3932164
  10.6 3.0 %copy-start.14 = (bf16[20,20]{1,0:T(8,128)(2,1)S(1)}, bf16[20,20]{1,0:T(8,128)(2,1)}, u32[]{:S(2)}) copy-start(bf16[20,20]{1,0:T(8,128)(2,1)} %map_ref.3) | copy-start | bytes 2404
  10.6 3.0 %copy-start.15 = (f32[20]{0:T(128)S(1)}, f32[20]{0:T(128)}, u32[]{:S(2)}) copy-start(f32[20]{0:T(128)} %bias_ref.1) | copy-start | bytes 244
  13.6 12.5 %copy-start.8 = (bf16[352,256]{1,0:T(8,128)(2,1)S(1)}, bf16[352,256]{1,0:T(8,128)(2,1)}, u32[]{:S(2)}) copy-start(bf16[352,256]{1,0:T(8,128)(2,1)} %constant.16.clone.table_ref) | copy-start | bytes 540676
  19.8 2.2 %copy-start = (bf16[2,20,20,6,288]{4,3,2,1,0:T(8,128)(2,1)}, bf16[2,20,20,6,288]{4,3,2,1,0:T(8,128)(2,1)S(1)}, u32[]{:S(2)}) copy-start(bf16[2,20,20,6,288]{4,3,2,1,0:T(8,128)(2,1)S(1)} %copy.16.weight_ref.weight_hbm) | copy-start | bytes 8294404
  40.8 16.5 %copy-start.7 = (bf16[384,256]{1,0:T(8,128)(2,1)S(1)}, bf16[384,256]{1,0:T(8,128)(2,1)}, u32[]{:S(2)}) copy-start(bf16[384,256]{1,0:T(8,128)(2,1)} %constant.17.clone.table_ref) | copy-start | bytes 589828
  40.8 35.7 %copy-start.6 = (bf16[20,8,16,256]{3,2,1,0:T(8,128)(2,1)S(1)}, bf16[20,8,16,256]{3,2,1,0:T(8,128)(2,1)}, u32[]{:S(2)}) copy-start(bf16[20,8,16,256]{3,2,1,0:T(8,128)(2,1)} %cotangent_ref.1) | copy-start | bytes 3932164
  40.8 35.7 %copy-start.12 = (bf16[144,256]{1,0:T(8,128)(2,1)S(1)}, bf16[144,256]{1,0:T(8,128)(2,1)}, u32[]{:S(2)}) copy-start(bf16[144,256]{1,0:T(8,128)(2,1)} %constant.15.clone.inverse_ref) | copy-start | bytes 221188
  40.8 35.7 %copy-start.13 = (bf16[96,256]{1,0:T(8,128)(2,1)S(1)}, bf16[96,256]{1,0:T(8,128)(2,1)}, u32[]{:S(2)}) copy-start(bf16[96,256]{1,0:T(8,128)(2,1)} %constant.14.clone.forward_ref) | copy-start | bytes 147460
  44.2 32.3 %copy-start.3 = (f32[20,8,16,256]{3,2,1,0:T(8,128)S(1)}, f32[20,8,16,256]{3,2,1,0:T(8,128)}, u32[]{:S(2)}) copy-start(f32[20,8,16,256]{3,2,1,0:T(8,128)} %get-tuple-element.27.pointwise_ref) | copy-start | bytes 7864324
  80.4 18.6 %all-to-all-start.4 = ((f32[32,32,128]{2,1,0:T(8,128)}), f32[32,32,128]{2,1,0:T(8,128)S(1)}, u32[]{:S(2)}, u32[]{:S(2)}) async-start(f32[32,32,128]{2,1,0:T(8,128)} %bitcast.17), calls=%async_computation.4 | async-start | bytes 1048576 | tf_op jit(solution)/shard_map/grad_cells_to_planes/all_to_all | solution.py:1034
  83.7 1.3 copy-start.4
  85.0 1.3 copy-start.5
  117.5 12.4 %all-to-all-start.6 = ((f32[8,72,128]{2,1,0:T(8,128)}), f32[8,72,128]{2,1,0:T(8,128)S(1)}, u32[]{:S(2)}, u32[]{:S(2)}) async-start(f32[8,72,128]{2,1,0:T(8,128)} %get-tuple-element.33), calls=%async_computation.6 | async-start | bytes 589824 | tf_op jit(solution)/shard_map/grad_modes_to_planes/all_to_all | solution.py:1037
  121.0 1.0 copy-start.9
  122.0 1.0 copy-start.10
  123.0 27.4 %copy-start.2 = (f32[20,8,16,256]{3,2,1,0:T(8,128)S(1)}, f32[20,8,16,256]{3,2,1,0:T(8,128)}, u32[]{:S(2)}) copy-start(f32[20,8,16,256]{3,2,1,0:T(8,128)} %get-tuple-element.38.back_ref) | copy-start | bytes 7864324
  123.0 27.4 %copy-start.11 = (bf16[144,256]{1,0:T(8,128)(2,1)S(1)}, bf16[144,256]{1,0:T(8,128)(2,1)}, u32[]{:S(2)}) copy-start(bf16[144,256]{1,0:T(8,128)(2,1)} %constant.13.clone.inverse_ref) | copy-start | bytes 221188

commit v6 on v5

--- a/solution.py
+++ b/solution.py
@@ -747,7 +747,11 @@
             pl.BlockSpec(before.shape, lambda at: (0, 0)),
         ],
         compiler_params=pltpu.CompilerParams(vmem_limit_bytes=VMEM_BYTES),
-    )(spectrum, grad, before)
+    )(
+        pltpu.with_memory_space_constraint(spectrum, pltpu.HBM),
+        pltpu.with_memory_space_constraint(grad, pltpu.HBM),
+        before,
+    )
     return jnp.transpose(rows, (3, 0, 1, 2, 4)), after
 
 

time: 153 us -> 152 us (level)
  local copies, waits for them, and re-layouts: 9.95 us -> 7.9 us
    unnamed x33 -> x29, local copies, waits for them, and re-layouts: 9.95 us -> 7.9 us
  transfers between devices with their start and end apart: 3 -> 3, of which waited for: 3 -> 3; matrix products, arithmetic and copies ran while one was open for 2% -> 2% of each run, Pallas kernels for 11% -> 12%
where the time goes in v6:
time: 152 us; the launch traced here: 151 us
  blocking collectives  75.9 us (50%)
  Pallas kernels  39.4 us (26%)
  starting transfers between devices  14 us (9%)
  waiting for transfers between devices  13.4 us (9%)
  local copies, waits for them, and re-layouts  7.9 us (5%)
    all_to_all x3, blocking collectives, mode_exchange(): return lax.all_to_all(values, 'gx', 0, 0, tiled=True)  39.7 us
    all_to_all x2, blocking collectives, cell_exchange(): lax.all_to_all(flat, ('gx', 'gy'), 0, 0, tiled=True).reshape(cell_shape)  36.2 us
    pallas_call x11, Pallas kernels, call(): pl.pallas_call(kernel, out_shape=out_shape, in_specs=specs, out_specs=out...  33.2 us
    all_to_all x2, waiting for transfers between devices, cell_exchange(): lax.all_to_all(flat, ('gx', 'gy'), 0, 0, tiled=True).reshape(cell_shape)  10.7 us
    all_to_all x2, starting transfers between devices, cell_exchange(): lax.all_to_all(flat, ('gx', 'gy'), 0, 0, tiled=True).reshape(cell_shape)  10.6 us
    unnamed x29, local copies, waits for them, and re-layouts  7.9 us
    pallas_call x1, Pallas kernels, weight_grad(): pl.pallas_call(functools.partial(weight_grad_kernel, plan), grid=(plan.ch...  6.2 us
    all_to_all x1, starting transfers between devices, mode_exchange(): return lax.all_to_all(values, 'gx', 0, 0, tiled=True)  3.43 us
  transfers between devices with their start and end apart: 3, of which 3 were waited for; matrix products, arithmetic and copies ran while one was open for 2% of the time, Pallas kernels for 12%

profile of v6, /device:TPU:0, one launch (start us, length us, event | category | flops | bytes accessed | tf_op | source)
XLA Modules:
  0.0 151.4 jit_solution(8890660195506373425)
XLA Ops:
  0.6 2.6 %depth_analysis.1 = f32[8,4,2,16,128]{4,3,2,1,0:T(8,128)} custom-call(bf16[20,8,16,256]{3,2,1,0:T(8,128)(2,1)} %field_ref.5, bf16[96,256]{1,0:T(8,128)(2,1)} %constant.12.clone.table_ref), custom_call_target="tpu_custom_call" | custom-call | tf_op jit(solution)/shard_map/depth_analysis/pallas_call | solution.py:342
  3.3 7.3 %all-to-all-start = ((f32[32,32,128]{2,1,0:T(8,128)}), f32[32,32,128]{2,1,0:T(8,128)S(1)}, u32[]{:S(2)}, u32[]{:S(2)}) async-start(f32[32,32,128]{2,1,0:T(8,128)} %bitcast.16), calls=%async_computation | async-start | bytes 1048576 | tf_op jit(solution)/shard_map/cells_to_planes/all_to_all | solution.py:1038
  10.6 0.0 copy-start.1
  10.6 0.0 copy-start.12
  10.6 0.0 copy-start.13
  10.6 3.0 %copy.16.weight_ref.weight_hbm = bf16[2,20,20,6,288]{4,3,2,1,0:T(8,128)(2,1)S(1)} copy(bf16[2,20,20,6,288]{4,0,3,2,1:T(2,128)(2,1)} %param.13) | data formatting | bytes 5529600 | tf_op args[2]
  13.6 0.0 copy-done.1
  13.6 0.0 copy-done.12
  13.6 0.0 copy-done.13
  13.6 0.0 copy-start.8
  13.6 6.2 %pointwise.1 = (f32[20,8,16,256]{3,2,1,0:T(8,128)}, f32[8,128]{1,0:T(8,128)S(1)}, bf16[2,20,5,6,128]{4,3,2,1,0:T(8,128)(2,1)}) custom-call(bf16[20,8,16,256]{3,2,1,0:T(8,128)(2,1)S(1)} %copy-done.1, bf16[20,20]{1,0:T(8,128)(2,1)S(1)} %copy-done.12, f32[20]{0:T(128)S(1)} %copy-done.13, bf16[2,20,20,6,288]{4,3,2,1,0:T(8,128)(2,1)S(1)} %copy.16.weight_ref.weight_hbm), custom_call_target="tpu_custom_call" | custom-call | tf_op jit(solution)/shard_map/pointwise/pallas_call | solution.py:342
  19.9 0.0 copy-start
  19.9 2.2 %copy-done = bf16[2,20,20,6,288]{4,3,2,1,0:T(8,128)(2,1)} copy-done((bf16[2,20,20,6,288]{4,3,2,1,0:T(8,128)(2,1)}, bf16[2,20,20,6,288]{4,3,2,1,0:T(8,128)(2,1)S(1)}, u32[]{:S(2)}) %copy-start) | copy-done | bytes 2764824
  22.1 4.0 %all-to-all-done = f32[32,32,128]{2,1,0:T(8,128)S(1)} async-done(((f32[32,32,128]{2,1,0:T(8,128)}), f32[32,32,128]{2,1,0:T(8,128)S(1)}, u32[]{:S(2)}, u32[]{:S(2)}) %all-to-all-start) | async-done | bytes 524320 | tf_op jit(solution)/shard_map/cells_to_planes/all_to_all | solution.py:1038
  26.1 0.0 copy-done.8
  26.1 1.4 plane_analysis.1
  27.6 13.3 %all_to_all.40.in_ref = f32[8,72,128]{2,1,0:T(8,128)S(1)} all-to-all(f32[8,72,128]{2,1,0:T(8,128)S(1)} %plane_analysis.1), channel_id=1, replica_groups=mesh['gx'=8,'gy'=4] {'gx'}, dimensions={0} | all-to-all | bytes 589824 | tf_op jit(solution)/shard_map/planes_to_modes/all_to_all | solution.py:1041
  40.8 0.0 copy-start.7
  40.8 0.0 copy-start.6
  40.8 0.0 copy-start.10
  40.8 0.0 copy-start.11
  40.8 3.4 %mix.1 = (f32[8,72,128]{2,1,0:T(8,128)S(1)}, f32[20,2,6,384]{3,2,1,0:T(8,128)}) custom-call(f32[8,72,128]{2,1,0:T(8,128)S(1)} %all_to_all.40.in_ref, bf16[2,20,20,6,288]{4,3,2,1,0:T(8,128)(2,1)} %copy-done, bf16[2,20,5,6,128]{4,3,2,1,0:T(8,128)(2,1)} %get-tuple-element.25.beside_hbm), custom_call_target="tpu_custom_call" | custom-call | tf_op jit(solution)/shard_map/mix/pallas_call | solution.py:342
  44.2 0.0 copy-start.3
  44.2 13.1 %all_to_all.41.in_ref = f32[8,72,128]{2,1,0:T(8,128)S(1)} all-to-all(f32[8,72,128]{2,1,0:T(8,128)S(1)} %get-tuple-element.26), channel_id=1, replica_groups=mesh['gx'=8,'gy'=4] {'gx'}, dimensions={0} | all-to-all | bytes 589824 | tf_op jit(solution)/shard_map/modes_to_planes/all_to_all | solution.py:1041
  57.4 0.0 copy-done.7
  57.4 1.4 plane_synthesis.1
  58.7 17.8 %all_to_all.42 = f32[32,32,128]{2,1,0:T(8,128)S(1)} all-to-all(f32[32,32,128]{2,1,0:T(8,128)S(1)} %bitcast.15), channel_id=1, replica_groups=mesh['gx'=8,'gy'=4] {'gx','gy'}, dimensions={0} | all-to-all | bytes 1048576 | tf_op jit(solution)/shard_map/planes_to_cells/all_to_all | solution.py:1038
  76.5 0.0 copy-done.6
  76.5 0.0 copy-done.10
  76.5 0.0 copy-done.11
  76.5 0.0 copy-done.3
  76.5 3.9 %activation.1 = (bf16[20,8,16,256]{3,2,1,0:T(8,128)(2,1)}, f32[8,4,2,16,128]{4,3,2,1,0:T(8,128)}, bf16[20,8,16,256]{3,2,1,0:T(8,128)(2,1)}, bf16[20,8,16,256]{3,2,1,0:T(8,128)(2,1)}) custom-call(f32[8,4,2,16,128]{4,3,2,1,0:T(8,128)S(1)} %bitcast.10, f32[20,8,16,256]{3,2,1,0:T(8,128)S(1)} %copy-done.3, bf16[20,8,16,256]{3,2,1,0:T(8,128)(2,1)S(1)} %copy-done.6, ...), custom_call_target="tpu_custom_call" | custom-call | tf_op jit(solution)/shard_map/activation/pallas_call | solution.py:342
  80.4 3.3 %all-to-all-start.4 = ((f32[32,32,128]{2,1,0:T(8,128)}), f32[32,32,128]{2,1,0:T(8,128)S(1)}, u32[]{:S(2)}, u32[]{:S(2)}) async-start(f32[32,32,128]{2,1,0:T(8,128)} %bitcast.17), calls=%async_computation.4 | async-start | bytes 1048576 | tf_op jit(solution)/shard_map/grad_cells_to_planes/all_to_all | solution.py:1038
  83.7 0.0 copy-start.4
  83.7 1.3 copy-done.4
  85.0 0.0 copy-start.5
  85.0 1.3 copy-done.5
  86.3 6.0 %pointwise_grad.1 = (f32[20,8,16,256]{3,2,1,0:T(8,128)}, f32[8,128]{1,0:T(8,128)S(1)}) custom-call(bf16[20,8,16,256]{3,2,1,0:T(8,128)(2,1)S(1)} %copy-done.1, bf16[20,8,16,256]{3,2,1,0:T(8,128)(2,1)S(1)} %copy-done.4, bf16[20,8,16,256]{3,2,1,0:T(8,128)(2,1)S(1)} %copy-done.5, bf16[20,20]{1,0:T(8,128)(2,1)S(1)} %copy-done.12), custom_call_target="tpu_custom_call" | custom-call | tf_op jit(solution)/shard_map/pointwise_grad/pallas_call | solution.py:342
  92.4 6.7 %all-to-all-done.4 = f32[32,32,128]{2,1,0:T(8,128)S(1)} async-done(((f32[32,32,128]{2,1,0:T(8,128)}), f32[32,32,128]{2,1,0:T(8,128)S(1)}, u32[]{:S(2)}, u32[]{:S(2)}) %all-to-all-start.4) | async-done | bytes 524320 | tf_op jit(solution)/shard_map/grad_cells_to_planes/all_to_all | solution.py:1038
  99.1 1.4 grad_plane_analysis.1
  100.5 13.3 %all_to_all.43.in_ref = f32[8,72,128]{2,1,0:T(8,128)S(1)} all-to-all(f32[8,72,128]{2,1,0:T(8,128)S(1)} %grad_plane_analysis.1), channel_id=1, replica_groups=mesh['gx'=8,'gy'=4] {'gx'}, dimensions={0} | all-to-all | bytes 589824 | tf_op jit(solution)/shard_map/grad_planes_to_modes/all_to_all | solution.py:1041
  113.8 3.8 %grad_mix.1 = (f32[8,72,128]{2,1,0:T(8,128)}, f32[20,2,6,384]{3,2,1,0:T(8,128)}, f32[8,128]{1,0:T(8,128)S(1)}) custom-call(f32[8,72,128]{2,1,0:T(8,128)S(1)} %all_to_all.43.in_ref, bf16[2,20,20,6,288]{4,3,2,1,0:T(8,128)(2,1)} %copy-done, bf16[2,20,5,6,128]{4,3,2,1,0:T(8,128)(2,1)} %get-tuple-element.25.beside_hbm), custom_call_target="tpu_custom_call" | custom-call | tf_op jit(solution)/shard_map/grad_mix/pallas_call | solution.py:342
  117.5 3.4 %all-to-all-start.6 = ((f32[8,72,128]{2,1,0:T(8,128)}), f32[8,72,128]{2,1,0:T(8,128)S(1)}, u32[]{:S(2)}, u32[]{:S(2)}) async-start(f32[8,72,128]{2,1,0:T(8,128)} %get-tuple-element.33), calls=%async_computation.6 | async-start | bytes 589824 | tf_op jit(solution)/shard_map/grad_modes_to_planes/all_to_all | solution.py:1041
  121.0 0.0 copy-start.2
  121.0 0.0 copy-start.9
  121.0 6.2 %grad_spectral.1 = (f32[20,20,6,2,288]{4,3,2,1,0:T(2,128)}, f32[8,128]{1,0:T(8,128)S(1)}) custom-call(f32[20,2,6,384]{3,2,1,0:T(8,128)} %get-tuple-element.34.spectrum_ref, f32[20,2,6,384]{3,2,1,0:T(8,128)} %get-tuple-element.35.grad_ref, f32[8,128]{1,0:T(8,128)S(1)} %get-tuple-element.36.before_ref), custom_call_target="tpu_custom_call" | custom-call | tf_op jit(solution)/shard_map/grad_spectral/pallas_call | solution.py:733
  127.2 2.7 %all-to-all-done.6.in_ref = f32[8,72,128]{2,1,0:T(8,128)S(1)} async-done(((f32[8,72,128]{2,1,0:T(8,128)}), f32[8,72,128]{2,1,0:T(8,128)S(1)}, u32[]{:S(2)}, u32[]{:S(2)}) %all-to-all-start.6) | async-done | bytes 294944 | tf_op jit(solution)/shard_map/grad_modes_to_planes/all_to_all | solution.py:1041
  129.9 1.4 grad_plane_synthesis.1
  131.3 18.5 %all_to_all.44 = f32[32,32,128]{2,1,0:T(8,128)S(1)} all-to-all(f32[32,32,128]{2,1,0:T(8,128)S(1)} %bitcast.14), channel_id=1, replica_groups=mesh['gx'=8,'gy'=4] {'gx','gy'}, dimensions={0} | all-to-all | bytes 1048576 | tf_op jit(solution)/shard_map/grad_planes_to_cells/all_to_all | solution.py:1038
  149.7 0.0 copy-done.2
  149.7 0.0 copy-done.9
  149.7 1.6 %grad_field.1 = (bf16[20,8,16,256]{3,2,1,0:T(8,128)(2,1)}, f32[20,20]{1,0:T(8,128)}, f32[1,20]{1,0:T(1,128)}) custom-call(f32[8,4,2,16,128]{4,3,2,1,0:T(8,128)S(1)} %bitcast.11, f32[20,8,16,256]{3,2,1,0:T(8,128)S(1)} %copy-done.2, bf16[144,256]{1,0:T(8,128)(2,1)S(1)} %copy-done.9), custom_call_target="tpu_custom_call" | custom-call | tf_op jit(solution)/shard_map/grad_field/pallas_call | solution.py:342
Async XLA Ops:
  3.3 22.9 %all-to-all-start = ((f32[32,32,128]{2,1,0:T(8,128)}), f32[32,32,128]{2,1,0:T(8,128)S(1)}, u32[]{:S(2)}, u32[]{:S(2)}) async-start(f32[32,32,128]{2,1,0:T(8,128)} %bitcast.16), calls=%async_computation | async-start | bytes 1048576 | tf_op jit(solution)/shard_map/cells_to_planes/all_to_all | solution.py:1038
  10.6 3.0 %copy-start.1 = (bf16[20,8,16,256]{3,2,1,0:T(8,128)(2,1)S(1)}, bf16[20,8,16,256]{3,2,1,0:T(8,128)(2,1)}, u32[]{:S(2)}) copy-start(bf16[20,8,16,256]{3,2,1,0:T(8,128)(2,1)} %field_ref.5) | copy-start | bytes 3932164
  10.6 3.0 %copy-start.12 = (bf16[20,20]{1,0:T(8,128)(2,1)S(1)}, bf16[20,20]{1,0:T(8,128)(2,1)}, u32[]{:S(2)}) copy-start(bf16[20,20]{1,0:T(8,128)(2,1)} %map_ref.3) | copy-start | bytes 2404
  10.6 3.0 %copy-start.13 = (f32[20]{0:T(128)S(1)}, f32[20]{0:T(128)}, u32[]{:S(2)}) copy-start(f32[20]{0:T(128)} %bias_ref.1) | copy-start | bytes 244
  13.6 12.5 %copy-start.8 = (bf16[352,256]{1,0:T(8,128)(2,1)S(1)}, bf16[352,256]{1,0:T(8,128)(2,1)}, u32[]{:S(2)}) copy-start(bf16[352,256]{1,0:T(8,128)(2,1)} %constant.16.clone.table_ref) | copy-start | bytes 540676
  19.9 2.2 %copy-start = (bf16[2,20,20,6,288]{4,3,2,1,0:T(8,128)(2,1)}, bf16[2,20,20,6,288]{4,3,2,1,0:T(8,128)(2,1)S(1)}, u32[]{:S(2)}) copy-start(bf16[2,20,20,6,288]{4,3,2,1,0:T(8,128)(2,1)S(1)} %copy.16.weight_ref.weight_hbm) | copy-start | bytes 8294404
  40.8 16.5 %copy-start.7 = (bf16[384,256]{1,0:T(8,128)(2,1)S(1)}, bf16[384,256]{1,0:T(8,128)(2,1)}, u32[]{:S(2)}) copy-start(bf16[384,256]{1,0:T(8,128)(2,1)} %constant.17.clone.table_ref) | copy-start | bytes 589828
  40.8 35.7 %copy-start.6 = (bf16[20,8,16,256]{3,2,1,0:T(8,128)(2,1)S(1)}, bf16[20,8,16,256]{3,2,1,0:T(8,128)(2,1)}, u32[]{:S(2)}) copy-start(bf16[20,8,16,256]{3,2,1,0:T(8,128)(2,1)} %cotangent_ref.1) | copy-start | bytes 3932164
  40.8 35.7 %copy-start.10 = (bf16[144,256]{1,0:T(8,128)(2,1)S(1)}, bf16[144,256]{1,0:T(8,128)(2,1)}, u32[]{:S(2)}) copy-start(bf16[144,256]{1,0:T(8,128)(2,1)} %constant.15.clone.inverse_ref) | copy-start | bytes 221188
  40.8 35.7 %copy-start.11 = (bf16[96,256]{1,0:T(8,128)(2,1)S(1)}, bf16[96,256]{1,0:T(8,128)(2,1)}, u32[]{:S(2)}) copy-start(bf16[96,256]{1,0:T(8,128)(2,1)} %constant.14.clone.forward_ref) | copy-start | bytes 147460
  44.2 32.3 %copy-start.3 = (f32[20,8,16,256]{3,2,1,0:T(8,128)S(1)}, f32[20,8,16,256]{3,2,1,0:T(8,128)}, u32[]{:S(2)}) copy-start(f32[20,8,16,256]{3,2,1,0:T(8,128)} %get-tuple-element.27.pointwise_ref) | copy-start | bytes 7864324
  80.4 18.6 %all-to-all-start.4 = ((f32[32,32,128]{2,1,0:T(8,128)}), f32[32,32,128]{2,1,0:T(8,128)S(1)}, u32[]{:S(2)}, u32[]{:S(2)}) async-start(f32[32,32,128]{2,1,0:T(8,128)} %bitcast.17), calls=%async_computation.4 | async-start | bytes 1048576 | tf_op jit(solution)/shard_map/grad_cells_to_planes/all_to_all | solution.py:1038
  83.7 1.3 copy-start.4
  85.0 1.3 copy-start.5
  117.5 12.4 %all-to-all-start.6 = ((f32[8,72,128]{2,1,0:T(8,128)}), f32[8,72,128]{2,1,0:T(8,128)S(1)}, u32[]{:S(2)}, u32[]{:S(2)}) async-start(f32[8,72,128]{2,1,0:T(8,128)} %get-tuple-element.33), calls=%async_computation.6 | async-start | bytes 589824 | tf_op jit(solution)/shard_map/grad_modes_to_planes/all_to_all | solution.py:1041
  121.0 28.8 %copy-start.2 = (f32[20,8,16,256]{3,2,1,0:T(8,128)S(1)}, f32[20,8,16,256]{3,2,1,0:T(8,128)}, u32[]{:S(2)}) copy-start(f32[20,8,16,256]{3,2,1,0:T(8,128)} %get-tuple-element.38.back_ref) | copy-start | bytes 7864324
  121.0 28.8 %copy-start.9 = (bf16[144,256]{1,0:T(8,128)(2,1)S(1)}, bf16[144,256]{1,0:T(8,128)(2,1)}, u32[]{:S(2)}) copy-start(bf16[144,256]{1,0:T(8,128)(2,1)} %constant.13.clone.inverse_ref) | copy-start | bytes 221188

commit v7 on v6

--- a/solution.py
+++ b/solution.py
@@ -445,7 +445,7 @@
         for place_y in range(plan.size_y)
         for which in range(2)
     ]
-    rows_ref[...] = along_y(
+    rows_ref[: plan.full_x * pad, :] = along_y(
         jnp.concatenate(swap_blocks(left, plan.rows_y), axis=0), y_table
     )
     right = jnp.concatenate(
@@ -803,7 +803,7 @@
     rows_ref[pl.ds(plan.planes, plan.full_x, stride=pad), :] = jnp.zeros(
         (plan.full_x, LANES), jnp.float32
     )
-    cells = along_y(rows_ref[...], y_table)
+    cells = along_y(rows_ref[: plan.full_x * pad, :], y_table)
     size = plan.size_x * pad
     cells = swap_blocks(
         [cells[row * size : (row + 1) * size] for row in range(plan.rows_x)], plan.rows_y
@@ -1048,8 +1048,8 @@
     scaled_inverse = jnp.asarray(np.concatenate([scaled_high, scaled_low, scaled_high]))
     forward_table, inverse_table = (jnp.asarray(table) for table in plan.plane_tables())
 
-    lane_rows = pltpu.VMEM((plan.full_x * pad, LANES), f32)
-    lane_modes = pltpu.VMEM((plan.width_x * pad, LANES), f32)
+    lane_rows = pltpu.VMEM(((plan.full_x + 1) * pad, LANES), f32)
+    lane_modes = pltpu.VMEM(((plan.width_x + 1) * pad, LANES), f32)
     rest = pltpu.VMEM((plan.size_x, 2 * pad, LANES), f32)
     own_full = pltpu.VMEM(own_shape[:3] + (2 * LANES,), f32)
     tails = pltpu.VMEM(own_shape[:3] + (LANES,), f32)

time: 152 us -> 152 us (level)
  no operation moved by 1% of the time
where the time goes in v7:
time: 152 us; the launch traced here: 151 us
  blocking collectives  75.9 us (50%)
  Pallas kernels  39.4 us (26%)
  starting transfers between devices  14 us (9%)
  waiting for transfers between devices  13.4 us (9%)
  local copies, waits for them, and re-layouts  7.9 us (5%)
    all_to_all x3, blocking collectives, mode_exchange(): return lax.all_to_all(values, 'gx', 0, 0, tiled=True)  39.7 us
    all_to_all x2, blocking collectives, cell_exchange(): lax.all_to_all(flat, ('gx', 'gy'), 0, 0, tiled=True).reshape(cell_shape)  36.2 us
    pallas_call x11, Pallas kernels, call(): pl.pallas_call(kernel, out_shape=out_shape, in_specs=specs, out_specs=out...  33.2 us
    all_to_all x2, waiting for transfers between devices, cell_exchange(): lax.all_to_all(flat, ('gx', 'gy'), 0, 0, tiled=True).reshape(cell_shape)  10.7 us
    all_to_all x2, starting transfers between devices, cell_exchange(): lax.all_to_all(flat, ('gx', 'gy'), 0, 0, tiled=True).reshape(cell_shape)  10.6 us
    unnamed x29, local copies, waits for them, and re-layouts  7.9 us
    pallas_call x1, Pallas kernels, weight_grad(): pl.pallas_call(functools.partial(weight_grad_kernel, plan), grid=(plan.ch...  6.2 us
    all_to_all x1, starting transfers between devices, mode_exchange(): return lax.all_to_all(values, 'gx', 0, 0, tiled=True)  3.43 us
  transfers between devices with their start and end apart: 3, of which 3 were waited for; matrix products, arithmetic and copies ran while one was open for 2% of the time, Pallas kernels for 12%

profile of v7, /device:TPU:0, one launch (start us, length us, event | category | flops | bytes accessed | tf_op | source)
XLA Modules:
  0.0 151.4 jit_solution(15694004719534570919)
XLA Ops:
  0.6 2.6 %depth_analysis.1 = f32[8,4,2,16,128]{4,3,2,1,0:T(8,128)} custom-call(bf16[20,8,16,256]{3,2,1,0:T(8,128)(2,1)} %field_ref.5, bf16[96,256]{1,0:T(8,128)(2,1)} %constant.12.clone.table_ref), custom_call_target="tpu_custom_call" | custom-call | tf_op jit(solution)/shard_map/depth_analysis/pallas_call | solution.py:342
  3.3 7.3 %all-to-all-start = ((f32[32,32,128]{2,1,0:T(8,128)}), f32[32,32,128]{2,1,0:T(8,128)S(1)}, u32[]{:S(2)}, u32[]{:S(2)}) async-start(f32[32,32,128]{2,1,0:T(8,128)} %bitcast.16), calls=%async_computation | async-start | bytes 1048576 | tf_op jit(solution)/shard_map/cells_to_planes/all_to_all | solution.py:1038
  10.6 0.0 copy-start.1
  10.6 0.0 copy-start.12
  10.6 0.0 copy-start.13
  10.6 3.0 %copy.16.weight_ref.weight_hbm = bf16[2,20,20,6,288]{4,3,2,1,0:T(8,128)(2,1)S(1)} copy(bf16[2,20,20,6,288]{4,0,3,2,1:T(2,128)(2,1)} %param.13) | data formatting | bytes 5529600 | tf_op args[2]
  13.6 0.0 copy-done.1
  13.6 0.0 copy-done.12
  13.6 0.0 copy-done.13
  13.6 0.0 copy-start.8
  13.6 6.2 %pointwise.1 = (f32[20,8,16,256]{3,2,1,0:T(8,128)}, f32[8,128]{1,0:T(8,128)S(1)}, bf16[2,20,5,6,128]{4,3,2,1,0:T(8,128)(2,1)}) custom-call(bf16[20,8,16,256]{3,2,1,0:T(8,128)(2,1)S(1)} %copy-done.1, bf16[20,20]{1,0:T(8,128)(2,1)S(1)} %copy-done.12, f32[20]{0:T(128)S(1)} %copy-done.13, bf16[2,20,20,6,288]{4,3,2,1,0:T(8,128)(2,1)S(1)} %copy.16.weight_ref.weight_hbm), custom_call_target="tpu_custom_call" | custom-call | tf_op jit(solution)/shard_map/pointwise/pallas_call | solution.py:342
  19.9 0.0 copy-start
  19.9 2.2 %copy-done = bf16[2,20,20,6,288]{4,3,2,1,0:T(8,128)(2,1)} copy-done((bf16[2,20,20,6,288]{4,3,2,1,0:T(8,128)(2,1)}, bf16[2,20,20,6,288]{4,3,2,1,0:T(8,128)(2,1)S(1)}, u32[]{:S(2)}) %copy-start) | copy-done | bytes 2764824
  22.1 4.0 %all-to-all-done = f32[32,32,128]{2,1,0:T(8,128)S(1)} async-done(((f32[32,32,128]{2,1,0:T(8,128)}), f32[32,32,128]{2,1,0:T(8,128)S(1)}, u32[]{:S(2)}, u32[]{:S(2)}) %all-to-all-start) | async-done | bytes 524320 | tf_op jit(solution)/shard_map/cells_to_planes/all_to_all | solution.py:1038
  26.1 0.0 copy-done.8
  26.1 1.4 plane_analysis.1
  27.6 13.3 %all_to_all.40.in_ref = f32[8,72,128]{2,1,0:T(8,128)S(1)} all-to-all(f32[8,72,128]{2,1,0:T(8,128)S(1)} %plane_analysis.1), channel_id=1, replica_groups=mesh['gx'=8,'gy'=4] {'gx'}, dimensions={0} | all-to-all | bytes 589824 | tf_op jit(solution)/shard_map/planes_to_modes/all_to_all | solution.py:1041
  40.8 0.0 copy-start.7
  40.8 0.0 copy-start.6
  40.8 0.0 copy-start.10
  40.8 0.0 copy-start.11
  40.8 3.4 %mix.1 = (f32[8,72,128]{2,1,0:T(8,128)S(1)}, f32[20,2,6,384]{3,2,1,0:T(8,128)}) custom-call(f32[8,72,128]{2,1,0:T(8,128)S(1)} %all_to_all.40.in_ref, bf16[2,20,20,6,288]{4,3,2,1,0:T(8,128)(2,1)} %copy-done, bf16[2,20,5,6,128]{4,3,2,1,0:T(8,128)(2,1)} %get-tuple-element.25.beside_hbm), custom_call_target="tpu_custom_call" | custom-call | tf_op jit(solution)/shard_map/mix/pallas_call | solution.py:342
  44.2 0.0 copy-start.3
  44.2 13.1 %all_to_all.41.in_ref = f32[8,72,128]{2,1,0:T(8,128)S(1)} all-to-all(f32[8,72,128]{2,1,0:T(8,128)S(1)} %get-tuple-element.26), channel_id=1, replica_groups=mesh['gx'=8,'gy'=4] {'gx'}, dimensions={0} | all-to-all | bytes 589824 | tf_op jit(solution)/shard_map/modes_to_planes/all_to_all | solution.py:1041
  57.4 0.0 copy-done.7
  57.4 1.4 plane_synthesis.1
  58.7 17.8 %all_to_all.42 = f32[32,32,128]{2,1,0:T(8,128)S(1)} all-to-all(f32[32,32,128]{2,1,0:T(8,128)S(1)} %bitcast.15), channel_id=1, replica_groups=mesh['gx'=8,'gy'=4] {'gx','gy'}, dimensions={0} | all-to-all | bytes 1048576 | tf_op jit(solution)/shard_map/planes_to_cells/all_to_all | solution.py:1038
  76.5 0.0 copy-done.6
  76.5 0.0 copy-done.10
  76.5 0.0 copy-done.11
  76.5 0.0 copy-done.3
  76.5 3.9 %activation.1 = (bf16[20,8,16,256]{3,2,1,0:T(8,128)(2,1)}, f32[8,4,2,16,128]{4,3,2,1,0:T(8,128)}, bf16[20,8,16,256]{3,2,1,0:T(8,128)(2,1)}, bf16[20,8,16,256]{3,2,1,0:T(8,128)(2,1)}) custom-call(f32[8,4,2,16,128]{4,3,2,1,0:T(8,128)S(1)} %bitcast.10, f32[20,8,16,256]{3,2,1,0:T(8,128)S(1)} %copy-done.3, bf16[20,8,16,256]{3,2,1,0:T(8,128)(2,1)S(1)} %copy-done.6, ...), custom_call_target="tpu_custom_call" | custom-call | tf_op jit(solution)/shard_map/activation/pallas_call | solution.py:342
  80.4 3.3 %all-to-all-start.4 = ((f32[32,32,128]{2,1,0:T(8,128)}), f32[32,32,128]{2,1,0:T(8,128)S(1)}, u32[]{:S(2)}, u32[]{:S(2)}) async-start(f32[32,32,128]{2,1,0:T(8,128)} %bitcast.17), calls=%async_computation.4 | async-start | bytes 1048576 | tf_op jit(solution)/shard_map/grad_cells_to_planes/all_to_all | solution.py:1038
  83.7 0.0 copy-start.4
  83.7 1.3 copy-done.4
  85.0 0.0 copy-start.5
  85.0 1.3 copy-done.5
  86.3 6.0 %pointwise_grad.1 = (f32[20,8,16,256]{3,2,1,0:T(8,128)}, f32[8,128]{1,0:T(8,128)S(1)}) custom-call(bf16[20,8,16,256]{3,2,1,0:T(8,128)(2,1)S(1)} %copy-done.1, bf16[20,8,16,256]{3,2,1,0:T(8,128)(2,1)S(1)} %copy-done.4, bf16[20,8,16,256]{3,2,1,0:T(8,128)(2,1)S(1)} %copy-done.5, bf16[20,20]{1,0:T(8,128)(2,1)S(1)} %copy-done.12), custom_call_target="tpu_custom_call" | custom-call | tf_op jit(solution)/shard_map/pointwise_grad/pallas_call | solution.py:342
  92.4 6.7 %all-to-all-done.4 = f32[32,32,128]{2,1,0:T(8,128)S(1)} async-done(((f32[32,32,128]{2,1,0:T(8,128)}), f32[32,32,128]{2,1,0:T(8,128)S(1)}, u32[]{:S(2)}, u32[]{:S(2)}) %all-to-all-start.4) | async-done | bytes 524320 | tf_op jit(solution)/shard_map/grad_cells_to_planes/all_to_all | solution.py:1038
  99.1 1.4 grad_plane_analysis.1
  100.5 13.3 %all_to_all.43.in_ref = f32[8,72,128]{2,1,0:T(8,128)S(1)} all-to-all(f32[8,72,128]{2,1,0:T(8,128)S(1)} %grad_plane_analysis.1), channel_id=1, replica_groups=mesh['gx'=8,'gy'=4] {'gx'}, dimensions={0} | all-to-all | bytes 589824 | tf_op jit(solution)/shard_map/grad_planes_to_modes/all_to_all | solution.py:1041
  113.8 3.8 %grad_mix.1 = (f32[8,72,128]{2,1,0:T(8,128)}, f32[20,2,6,384]{3,2,1,0:T(8,128)}, f32[8,128]{1,0:T(8,128)S(1)}) custom-call(f32[8,72,128]{2,1,0:T(8,128)S(1)} %all_to_all.43.in_ref, bf16[2,20,20,6,288]{4,3,2,1,0:T(8,128)(2,1)} %copy-done, bf16[2,20,5,6,128]{4,3,2,1,0:T(8,128)(2,1)} %get-tuple-element.25.beside_hbm), custom_call_target="tpu_custom_call" | custom-call | tf_op jit(solution)/shard_map/grad_mix/pallas_call | solution.py:342
  117.5 3.4 %all-to-all-start.6 = ((f32[8,72,128]{2,1,0:T(8,128)}), f32[8,72,128]{2,1,0:T(8,128)S(1)}, u32[]{:S(2)}, u32[]{:S(2)}) async-start(f32[8,72,128]{2,1,0:T(8,128)} %get-tuple-element.33), calls=%async_computation.6 | async-start | bytes 589824 | tf_op jit(solution)/shard_map/grad_modes_to_planes/all_to_all | solution.py:1041
  121.0 0.0 copy-start.2
  121.0 0.0 copy-start.9
  121.0 6.2 %grad_spectral.1 = (f32[20,20,6,2,288]{4,3,2,1,0:T(2,128)}, f32[8,128]{1,0:T(8,128)S(1)}) custom-call(f32[20,2,6,384]{3,2,1,0:T(8,128)} %get-tuple-element.34.spectrum_ref, f32[20,2,6,384]{3,2,1,0:T(8,128)} %get-tuple-element.35.grad_ref, f32[8,128]{1,0:T(8,128)S(1)} %get-tuple-element.36.before_ref), custom_call_target="tpu_custom_call" | custom-call | tf_op jit(solution)/shard_map/grad_spectral/pallas_call | solution.py:733
  127.2 2.7 %all-to-all-done.6.in_ref = f32[8,72,128]{2,1,0:T(8,128)S(1)} async-done(((f32[8,72,128]{2,1,0:T(8,128)}), f32[8,72,128]{2,1,0:T(8,128)S(1)}, u32[]{:S(2)}, u32[]{:S(2)}) %all-to-all-start.6) | async-done | bytes 294944 | tf_op jit(solution)/shard_map/grad_modes_to_planes/all_to_all | solution.py:1041
  129.9 1.4 grad_plane_synthesis.1
  131.3 18.5 %all_to_all.44 = f32[32,32,128]{2,1,0:T(8,128)S(1)} all-to-all(f32[32,32,128]{2,1,0:T(8,128)S(1)} %bitcast.14), channel_id=1, replica_groups=mesh['gx'=8,'gy'=4] {'gx','gy'}, dimensions={0} | all-to-all | bytes 1048576 | tf_op jit(solution)/shard_map/grad_planes_to_cells/all_to_all | solution.py:1038
  149.7 0.0 copy-done.2
  149.7 0.0 copy-done.9
  149.7 1.6 %grad_field.1 = (bf16[20,8,16,256]{3,2,1,0:T(8,128)(2,1)}, f32[20,20]{1,0:T(8,128)}, f32[1,20]{1,0:T(1,128)}) custom-call(f32[8,4,2,16,128]{4,3,2,1,0:T(8,128)S(1)} %bitcast.11, f32[20,8,16,256]{3,2,1,0:T(8,128)S(1)} %copy-done.2, bf16[144,256]{1,0:T(8,128)(2,1)S(1)} %copy-done.9), custom_call_target="tpu_custom_call" | custom-call | tf_op jit(solution)/shard_map/grad_field/pallas_call | solution.py:342
Async XLA Ops:
  3.3 22.9 %all-to-all-start = ((f32[32,32,128]{2,1,0:T(8,128)}), f32[32,32,128]{2,1,0:T(8,128)S(1)}, u32[]{:S(2)}, u32[]{:S(2)}) async-start(f32[32,32,128]{2,1,0:T(8,128)} %bitcast.16), calls=%async_computation | async-start | bytes 1048576 | tf_op jit(solution)/shard_map/cells_to_planes/all_to_all | solution.py:1038
  10.6 3.0 %copy-start.1 = (bf16[20,8,16,256]{3,2,1,0:T(8,128)(2,1)S(1)}, bf16[20,8,16,256]{3,2,1,0:T(8,128)(2,1)}, u32[]{:S(2)}) copy-start(bf16[20,8,16,256]{3,2,1,0:T(8,128)(2,1)} %field_ref.5) | copy-start | bytes 3932164
  10.6 3.0 %copy-start.12 = (bf16[20,20]{1,0:T(8,128)(2,1)S(1)}, bf16[20,20]{1,0:T(8,128)(2,1)}, u32[]{:S(2)}) copy-start(bf16[20,20]{1,0:T(8,128)(2,1)} %map_ref.3) | copy-start | bytes 2404
  10.6 3.0 %copy-start.13 = (f32[20]{0:T(128)S(1)}, f32[20]{0:T(128)}, u32[]{:S(2)}) copy-start(f32[20]{0:T(128)} %bias_ref.1) | copy-start | bytes 244
  13.6 12.5 %copy-start.8 = (bf16[352,256]{1,0:T(8,128)(2,1)S(1)}, bf16[352,256]{1,0:T(8,128)(2,1)}, u32[]{:S(2)}) copy-start(bf16[352,256]{1,0:T(8,128)(2,1)} %constant.16.clone.table_ref) | copy-start | bytes 540676
  19.9 2.2 %copy-start = (bf16[2,20,20,6,288]{4,3,2,1,0:T(8,128)(2,1)}, bf16[2,20,20,6,288]{4,3,2,1,0:T(8,128)(2,1)S(1)}, u32[]{:S(2)}) copy-start(bf16[2,20,20,6,288]{4,3,2,1,0:T(8,128)(2,1)S(1)} %copy.16.weight_ref.weight_hbm) | copy-start | bytes 8294404
  40.8 16.5 %copy-start.7 = (bf16[384,256]{1,0:T(8,128)(2,1)S(1)}, bf16[384,256]{1,0:T(8,128)(2,1)}, u32[]{:S(2)}) copy-start(bf16[384,256]{1,0:T(8,128)(2,1)} %constant.17.clone.table_ref) | copy-start | bytes 589828
  40.8 35.7 %copy-start.6 = (bf16[20,8,16,256]{3,2,1,0:T(8,128)(2,1)S(1)}, bf16[20,8,16,256]{3,2,1,0:T(8,128)(2,1)}, u32[]{:S(2)}) copy-start(bf16[20,8,16,256]{3,2,1,0:T(8,128)(2,1)} %cotangent_ref.1) | copy-start | bytes 3932164
  40.8 35.7 %copy-start.10 = (bf16[144,256]{1,0:T(8,128)(2,1)S(1)}, bf16[144,256]{1,0:T(8,128)(2,1)}, u32[]{:S(2)}) copy-start(bf16[144,256]{1,0:T(8,128)(2,1)} %constant.15.clone.inverse_ref) | copy-start | bytes 221188
  40.8 35.7 %copy-start.11 = (bf16[96,256]{1,0:T(8,128)(2,1)S(1)}, bf16[96,256]{1,0:T(8,128)(2,1)}, u32[]{:S(2)}) copy-start(bf16[96,256]{1,0:T(8,128)(2,1)} %constant.14.clone.forward_ref) | copy-start | bytes 147460
  44.2 32.3 %copy-start.3 = (f32[20,8,16,256]{3,2,1,0:T(8,128)S(1)}, f32[20,8,16,256]{3,2,1,0:T(8,128)}, u32[]{:S(2)}) copy-start(f32[20,8,16,256]{3,2,1,0:T(8,128)} %get-tuple-element.27.pointwise_ref) | copy-start | bytes 7864324
  80.4 18.6 %all-to-all-start.4 = ((f32[32,32,128]{2,1,0:T(8,128)}), f32[32,32,128]{2,1,0:T(8,128)S(1)}, u32[]{:S(2)}, u32[]{:S(2)}) async-start(f32[32,32,128]{2,1,0:T(8,128)} %bitcast.17), calls=%async_computation.4 | async-start | bytes 1048576 | tf_op jit(solution)/shard_map/grad_cells_to_planes/all_to_all | solution.py:1038
  83.7 1.3 copy-start.4
  85.0 1.3 copy-start.5
  117.5 12.4 %all-to-all-start.6 = ((f32[8,72,128]{2,1,0:T(8,128)}), f32[8,72,128]{2,1,0:T(8,128)S(1)}, u32[]{:S(2)}, u32[]{:S(2)}) async-start(f32[8,72,128]{2,1,0:T(8,128)} %get-tuple-element.33), calls=%async_computation.6 | async-start | bytes 589824 | tf_op jit(solution)/shard_map/grad_modes_to_planes/all_to_all | solution.py:1041
  121.0 28.8 %copy-start.2 = (f32[20,8,16,256]{3,2,1,0:T(8,128)S(1)}, f32[20,8,16,256]{3,2,1,0:T(8,128)}, u32[]{:S(2)}) copy-start(f32[20,8,16,256]{3,2,1,0:T(8,128)} %get-tuple-element.38.back_ref) | copy-start | bytes 7864324
  121.0 28.8 %copy-start.9 = (bf16[144,256]{1,0:T(8,128)(2,1)S(1)}, bf16[144,256]{1,0:T(8,128)(2,1)}, u32[]{:S(2)}) copy-start(bf16[144,256]{1,0:T(8,128)(2,1)} %constant.13.clone.inverse_ref) | copy-start | bytes 221188
